TPU v7x, 32 devices: a whole 2x2x4 slice. The times are simulated.
32 devices in a mesh: dp: 4 (over y, x), ctx: 8 (over z, core).
Axes of the slice: x: 2, y: 2, z: 4, core: 2. Of those that a mesh axis runs over, the one named last changes fastest.
Arguments:
- hidden_in: bfloat16 [4, 1024, 2048], P('dp', 'ctx'), may hold values from -6 to 6
- out_grad: bfloat16 [4, 1024, 2048], P('dp', 'ctx'), may hold values from -6 to 6
- seg_ids: int32 [4, 1024], P('dp', 'ctx'), may hold values from 0 to 15, never falling along the last dimension, each value on 1 to 512 neighbouring positions
- valid_mask: int32 [4, 1024], P('dp', 'ctx'), may hold values 0 or 1
- w_query: float32 [2048, 2048], P(('dp', 'ctx')), may hold values from -0.1875 to 0.1875
- w_key: float32 [2048, 2048], P(('dp', 'ctx')), may hold values from -0.1875 to 0.1875
- w_value: float32 [2048, 2048], P(('dp', 'ctx')), may hold values from -0.125 to 0.125
- w_output: float32 [2048, 2048], P(('dp', 'ctx')), may hold values from -0.375 to 0.375
- w_gate: float32 [2048, 8192], P(('dp', 'ctx')), may hold values from -0.125 to 0.125
- w_up: float32 [2048, 8192], P(('dp', 'ctx')), may hold values from -0.125 to 0.125
- w_down: float32 [8192, 2048], P(('dp', 'ctx')), may hold values from -0.0625 to 0.0625
- gain_attn: float32 [2048], P(('dp', 'ctx')), may hold values from 0.5 to 1.5
- gain_mlp: float32 [2048], P(('dp', 'ctx')), may hold values from 0.5 to 1.5
Outputs:
- result: bfloat16 [4, 1024, 2048], P('dp', 'ctx')
- grad_input: bfloat16 [4, 1024, 2048], P('dp', 'ctx')
- grad_query: float32 [2048, 2048], P(('dp', 'ctx'))
- grad_key: float32 [2048, 2048], P(('dp', 'ctx'))
- grad_value: float32 [2048, 2048], P(('dp', 'ctx'))
- grad_output: float32 [2048, 2048], P(('dp', 'ctx'))
- grad_gate: float32 [2048, 8192], P(('dp', 'ctx'))
- grad_up: float32 [2048, 8192], P(('dp', 'ctx'))
- grad_down: float32 [8192, 2048], P(('dp', 'ctx'))
- grad_gain_attn: float32 [2048], P(('dp', 'ctx'))
- grad_gain_mlp: float32 [2048], P(('dp', 'ctx'))
- mass_mean: float32 [], replicated
Inputs may be any that keep to these rules, and one draw needn't show every extreme that they name: `seg_ids`: within a slot ids never fall; each document has 1 to 512 tokens and one has exactly 512.
All inputs are finite; a program needn't handle non-finite values. No bound on the sum of `valid_mask` on one device may be relied on, other than what follows from the above.
Results may differ from a plain program's by a relative error of at most 0.015.
The roundings to bfloat16 on the way count: a program that leaves them out, or rounds other values in their place, can miss the bound.
Values may be sent and summed in bfloat16 or wider, within the bound.
A program may use at most 704 MiB of HBM per device.

v0:
```python
import math

import jax
import jax.numpy as jnp
from jax import lax
from jax.sharding import PartitionSpec as P

HEADS = 16
HEAD_DIM = 128


norm_eps = 1e-05
rope_base = 10000.0
score_shift = math.log(4096.0)
contract_rows = (((0,), (0,)), ((), ()))
contract_cols = (((1,), (1,)), ((), ()))


def rotate(values, cosines, sines):
    half_dim = values.shape[-1] // 2
    first = values[..., :half_dim]
    second = values[..., half_dim:]
    cos_b = cosines[:, None, :]
    sin_b = sines[:, None, :]
    return jnp.concatenate(
        [first * cos_b - second * sin_b, second * cos_b + first * sin_b], axis=-1
    )


def rotate_back(grads, cosines, sines):
    half_dim = grads.shape[-1] // 2
    first = grads[..., :half_dim]
    second = grads[..., half_dim:]
    cos_b = cosines[:, None, :]
    sin_b = sines[:, None, :]
    return jnp.concatenate(
        [first * cos_b + second * sin_b, second * cos_b - first * sin_b], axis=-1
    )


def rope_tables(positions):
    half_dim = HEAD_DIM // 2
    inverse = jnp.exp(
        jnp.arange(half_dim, dtype=jnp.float32) * (-2.0 * math.log(rope_base) / HEAD_DIM)
    )
    angles = positions[:, None] * inverse[None, :]
    return (jnp.cos(angles), jnp.sin(angles))


def block_mask(query_index, query_seg, key_seg, key_valid, key_start, block_len):
    key_index = key_start + jnp.arange(block_len, dtype=jnp.int32)
    seg_block = lax.dynamic_slice_in_dim(key_seg, key_start, block_len)
    valid_block = lax.dynamic_slice_in_dim(key_valid, key_start, block_len)
    allowed = (
        (query_seg[:, None] == seg_block[None, :])
        & (key_index[None, :] <= query_index[:, None])
        & (valid_block[None, :] == 1)
    )
    return allowed.astype(jnp.float32)


def inverse_rms(values):
    return lax.rsqrt(jnp.mean(values * values, axis=-1, keepdims=True) + norm_eps)


def shards(
    hidden_in,
    out_grad,
    seg_ids,
    valid_mask,
    w_query,
    w_key,
    w_value,
    w_output,
    w_gate,
    w_up,
    w_down,
    gain_attn,
    gain_mlp,
):
    inputs_f = hidden_in[0].astype(jnp.float32)
    row_count, width = inputs_f.shape
    score_scale = 1.0 / math.sqrt(HEAD_DIM)
    shape3 = (row_count, HEADS, HEAD_DIM)
    ctx_rank = lax.axis_index("ctx")
    local_seg = seg_ids[0]
    local_valid = valid_mask[0]
    valid_f = local_valid.astype(jnp.float32)
    all_codes = lax.all_gather(local_seg * 2 + local_valid, "ctx", axis=0, tiled=True)
    key_seg = all_codes // 2
    key_valid = all_codes % 2
    seq_len = all_codes.shape[0]
    query_index = ctx_rank * row_count + jnp.arange(row_count, dtype=jnp.int32)
    starts = jnp.sum((key_seg[None, :] < local_seg[:, None]).astype(jnp.int32), axis=1)
    cosines, sines = rope_tables((query_index - starts).astype(jnp.float32))
    attn_pack = (
        w_query.astype(jnp.bfloat16),
        w_key.astype(jnp.bfloat16),
        w_value.astype(jnp.bfloat16),
        w_output.astype(jnp.bfloat16),
        gain_attn.astype(jnp.bfloat16),
    )
    query_w, key_w, value_w, output_w, gain_one = (
        lax.all_gather(attn_pack[0], ("dp", "ctx"), axis=0, tiled=True),
        lax.all_gather(attn_pack[1], ("dp", "ctx"), axis=0, tiled=True),
        lax.all_gather(attn_pack[2], ("dp", "ctx"), axis=0, tiled=True),
        lax.all_gather(attn_pack[3], ("dp", "ctx"), axis=0, tiled=True),
        lax.all_gather(attn_pack[4], ("dp", "ctx"), axis=0, tiled=True),
    )
    inv_first = inverse_rms(inputs_f)
    normed_first = inputs_f * inv_first
    attn_in = (normed_first * gain_one.astype(jnp.float32)).astype(jnp.bfloat16)
    queries = rotate(
        jnp.dot(attn_in, query_w, preferred_element_type=jnp.float32).reshape(shape3),
        cosines,
        sines,
    ).astype(jnp.bfloat16)
    keys_local = (
        rotate(
            jnp.dot(attn_in, key_w, preferred_element_type=jnp.float32).reshape(shape3),
            cosines,
            sines,
        )
        .astype(jnp.bfloat16)
        .reshape(row_count, width)
    )
    values_local = jnp.dot(attn_in, value_w, preferred_element_type=jnp.float32).astype(
        jnp.bfloat16
    )
    keys_all, values_all = (
        lax.all_gather(keys_local, "ctx", axis=0, tiled=True),
        lax.all_gather(values_local, "ctx", axis=0, tiled=True),
    )
    block_len = math.gcd(seq_len, 1024)
    block_count = seq_len // block_len
    keys3 = keys_all.reshape(seq_len, HEADS, HEAD_DIM)
    values3 = values_all.reshape(seq_len, HEADS, HEAD_DIM)

    def forward_step(block, carry):
        accum, mass = carry
        key_start = block * block_len
        key_block = lax.dynamic_slice_in_dim(keys3, key_start, block_len, 0)
        value_block = lax.dynamic_slice_in_dim(values3, key_start, block_len, 0)
        allowed = block_mask(query_index, local_seg, key_seg, key_valid, key_start, block_len)
        scores = (
            jnp.einsum("qhd,khd->hqk", queries, key_block, preferred_element_type=jnp.float32)
            * score_scale
            - score_shift
        )
        probs = jax.nn.sigmoid(scores) * allowed[None]
        accum = accum + jnp.einsum(
            "hqk,khd->qhd",
            probs.astype(jnp.bfloat16),
            value_block,
            preferred_element_type=jnp.float32,
        )
        return (accum, mass + jnp.sum(probs, axis=(0, 2)))

    attended, mass = lax.fori_loop(
        0,
        block_count,
        forward_step,
        (jnp.zeros(shape3, jnp.float32), jnp.zeros((row_count,), jnp.float32)),
    )
    attn_out = attended.reshape(row_count, width).astype(jnp.bfloat16)
    middle = inputs_f + jnp.dot(attn_out, output_w, preferred_element_type=jnp.float32)
    inv_second = inverse_rms(middle)
    normed_second = middle * inv_second
    hidden_width = w_gate.shape[1]
    mlp_pack = (
        w_gate.astype(jnp.bfloat16),
        w_up.astype(jnp.bfloat16),
        gain_mlp.astype(jnp.bfloat16),
    )
    gate_piece = lax.all_gather(mlp_pack[0], ("dp", "ctx"), axis=0, tiled=True)
    up_piece = lax.all_gather(mlp_pack[1], ("dp", "ctx"), axis=0, tiled=True)
    gain_piece = lax.all_gather(mlp_pack[2], ("dp", "ctx"), axis=0, tiled=True)
    columns = (normed_second * gain_piece.astype(jnp.float32)).astype(jnp.bfloat16)
    gate_acc = jnp.dot(columns, gate_piece, preferred_element_type=jnp.float32)
    up_acc = jnp.dot(columns, up_piece, preferred_element_type=jnp.float32)
    sig_gate = jax.nn.sigmoid(gate_acc)
    silu_gate = gate_acc * sig_gate
    hidden = (silu_gate * up_acc).astype(jnp.bfloat16)
    down_pack = w_down.astype(jnp.bfloat16)
    branch_two = jnp.dot(
        hidden,
        lax.all_gather(down_pack, ("dp", "ctx"), axis=0, tiled=True),
        preferred_element_type=jnp.float32,
    )
    result = (middle + branch_two).astype(jnp.bfloat16)
    grad_out = out_grad[0]
    grad_f = grad_out.astype(jnp.float32)
    grad_hidden = lax.dot_general(
        grad_out,
        lax.all_gather(down_pack, ("dp", "ctx"), axis=0, tiled=True),
        contract_cols,
        preferred_element_type=jnp.float32,
    )
    grad_gate_b = (grad_hidden * up_acc * sig_gate * (1.0 + gate_acc * (1.0 - sig_gate))).astype(
        jnp.bfloat16
    )
    grad_up_b = (grad_hidden * silu_gate).astype(jnp.bfloat16)
    gate_piece, up_piece, gain_piece = lax.all_gather(
        (mlp_pack[0], mlp_pack[1], mlp_pack[2]), ("dp", "ctx"), axis=0, tiled=True
    )
    grad_cols = lax.dot_general(
        grad_gate_b, gate_piece, contract_cols, preferred_element_type=jnp.float32
    )
    grad_cols = grad_cols + lax.dot_general(
        grad_up_b, up_piece, contract_cols, preferred_element_type=jnp.float32
    )
    back_pair = jnp.stack([grad_cols, grad_cols * gain_piece.astype(jnp.float32)])
    grad_normed = back_pair[0]
    scaled_second = back_pair[1]
    gain_two_term = jnp.sum(grad_normed * normed_second, axis=0)
    grad_middle = grad_f + inv_second * (
        scaled_second
        - normed_second * jnp.mean(scaled_second * normed_second, axis=-1, keepdims=True)
    )
    grad_branch = grad_middle.astype(jnp.bfloat16)
    query_b, key_b, value_b, output_b, gain_back = (
        lax.all_gather(attn_pack[0], ("dp", "ctx"), axis=0, tiled=True),
        lax.all_gather(attn_pack[1], ("dp", "ctx"), axis=0, tiled=True),
        lax.all_gather(attn_pack[2], ("dp", "ctx"), axis=0, tiled=True),
        lax.all_gather(attn_pack[3], ("dp", "ctx"), axis=0, tiled=True),
        lax.all_gather(attn_pack[4], ("dp", "ctx"), axis=0, tiled=True),
    )
    keys_back, values_back = (
        lax.all_gather(keys_local, "ctx", axis=0, tiled=True),
        lax.all_gather(values_local, "ctx", axis=0, tiled=True),
    )
    keys_b3 = keys_back.reshape(seq_len, HEADS, HEAD_DIM)
    values_b3 = values_back.reshape(seq_len, HEADS, HEAD_DIM)
    grad_attended = (
        lax.dot_general(grad_branch, output_b, contract_cols, preferred_element_type=jnp.float32)
        .astype(jnp.bfloat16)
        .reshape(shape3)
    )

    def score_grads(key_block, value_block, allowed):
        scores = (
            jnp.einsum("qhd,khd->hqk", queries, key_block, preferred_element_type=jnp.float32)
            * score_scale
            - score_shift
        )
        sig_scores = jax.nn.sigmoid(scores)
        prob_low = (sig_scores * allowed).astype(jnp.bfloat16)
        grad_probs = jnp.einsum(
            "qhd,khd->hqk", grad_attended, value_block, preferred_element_type=jnp.float32
        )
        grad_scores = (grad_probs * sig_scores * (1.0 - sig_scores) * allowed).astype(jnp.bfloat16)
        return (grad_scores, prob_low)

    def backward_step(block, carry):
        grad_rot, score_buf, prob_buf = carry
        key_start = block * block_len
        key_block = lax.dynamic_slice_in_dim(keys_b3, key_start, block_len, 0)
        value_block = lax.dynamic_slice_in_dim(values_b3, key_start, block_len, 0)
        allowed = block_mask(query_index, local_seg, key_seg, key_valid, key_start, block_len)[None]
        grad_scores, prob_low = score_grads(key_block, value_block, allowed)
        grad_rot = (
            grad_rot
            + jnp.einsum("hqk,khd->qhd", grad_scores, key_block, preferred_element_type=jnp.float32)
            * score_scale
        )
        score_buf = lax.dynamic_update_slice_in_dim(score_buf, grad_scores, key_start, 2)
        prob_buf = lax.dynamic_update_slice_in_dim(prob_buf, prob_low, key_start, 2)
        return (grad_rot, score_buf, prob_buf)

    buffer_shape = (HEADS, row_count, seq_len)
    back_start = (
        jnp.zeros(shape3, jnp.float32),
        jnp.zeros(buffer_shape, jnp.bfloat16),
        jnp.zeros(buffer_shape, jnp.bfloat16),
    )
    grad_rot, score_buf, prob_buf = lax.fori_loop(0, block_count, backward_step, back_start)
    count = row_count * lax.axis_size("ctx")
    grad_keys = (
        jnp.einsum("hqk,qhd->khd", score_buf, queries, preferred_element_type=jnp.float32)
        * score_scale
    )
    grad_values = jnp.einsum(
        "hqk,qhd->khd", prob_buf, grad_attended, preferred_element_type=jnp.float32
    )
    key_value_sum = lax.psum_scatter(
        jnp.concatenate(
            [grad_keys.reshape(count, width), grad_values.reshape(count, width)], axis=1
        ),
        "ctx",
        scatter_dimension=0,
        tiled=True,
    )
    grad_keys_f = key_value_sum[:, :width]
    grad_values_f = key_value_sum[:, width:]
    grad_keys_b = (
        rotate_back(grad_keys_f.reshape(shape3), cosines, sines)
        .astype(jnp.bfloat16)
        .reshape(row_count, width)
    )
    grad_values_b = grad_values_f.astype(jnp.bfloat16)
    grad_queries_b = (
        rotate_back(grad_rot, cosines, sines).astype(jnp.bfloat16).reshape(row_count, width)
    )
    grad_attn_in = lax.dot_general(
        grad_queries_b, query_b, contract_cols, preferred_element_type=jnp.float32
    )
    grad_attn_in = grad_attn_in + lax.dot_general(
        grad_keys_b, key_b, contract_cols, preferred_element_type=jnp.float32
    )
    grad_attn_in = grad_attn_in + lax.dot_general(
        grad_values_b, value_b, contract_cols, preferred_element_type=jnp.float32
    )
    scaled_first = grad_attn_in * gain_back.astype(jnp.float32)
    gain_one_term = jnp.sum(grad_attn_in * normed_first, axis=0)
    grad_input = grad_middle + inv_first * (
        scaled_first - normed_first * jnp.mean(scaled_first * normed_first, axis=-1, keepdims=True)
    )
    attention_sum = lax.psum_scatter(
        jnp.concatenate(
            [
                lax.dot_general(
                    attn_in, grad_queries_b, contract_rows, preferred_element_type=jnp.float32
                ),
                lax.dot_general(
                    attn_in, grad_keys_b, contract_rows, preferred_element_type=jnp.float32
                ),
                lax.dot_general(
                    attn_in, grad_values_b, contract_rows, preferred_element_type=jnp.float32
                ),
                lax.dot_general(
                    attn_out, grad_branch, contract_rows, preferred_element_type=jnp.float32
                ),
            ],
            axis=1,
        ),
        ("dp", "ctx"),
        scatter_dimension=0,
        tiled=True,
    )
    gate_up_sum = lax.psum_scatter(
        jnp.concatenate(
            [
                lax.dot_general(
                    columns, grad_gate_b, contract_rows, preferred_element_type=jnp.float32
                ),
                lax.dot_general(
                    columns, grad_up_b, contract_rows, preferred_element_type=jnp.float32
                ),
            ],
            axis=1,
        ),
        ("dp", "ctx"),
        scatter_dimension=0,
        tiled=True,
    )
    down_sum = lax.psum_scatter(
        lax.dot_general(hidden, grad_out, contract_rows, preferred_element_type=jnp.float32),
        ("dp", "ctx"),
        scatter_dimension=0,
        tiled=True,
    )
    totals = lax.psum(
        (gain_one_term, gain_two_term, jnp.sum(valid_f * mass) / HEADS), ("dp", "ctx")
    )
    owner = lax.axis_index(("dp", "ctx"))
    gain_rows = gain_attn.shape[0]
    grad_gain_attn = lax.dynamic_slice_in_dim(totals[0], owner * gain_rows, gain_rows)
    grad_gain_mlp = lax.dynamic_slice_in_dim(totals[1], owner * gain_rows, gain_rows)
    mass_mean = totals[2] / (lax.axis_size("dp") * seq_len)
    return (
        result[None],
        grad_input.astype(jnp.bfloat16)[None],
        attention_sum[:, :width],
        attention_sum[:, width : 2 * width],
        attention_sum[:, 2 * width : 3 * width],
        attention_sum[:, 3 * width :],
        gate_up_sum[:, :hidden_width],
        gate_up_sum[:, hidden_width:],
        down_sum,
        grad_gain_attn,
        grad_gain_mlp,
        mass_mean,
    )


def solution(mesh):
    return jax.shard_map(
        shards,
        mesh=mesh,
        in_specs=(
            P("dp", "ctx", None),
            P("dp", "ctx", None),
            P("dp", "ctx"),
            P("dp", "ctx"),
            P(("dp", "ctx"), None),
            P(("dp", "ctx"), None),
            P(("dp", "ctx"), None),
            P(("dp", "ctx"), None),
            P(("dp", "ctx"), None),
            P(("dp", "ctx"), None),
            P(("dp", "ctx"), None),
            P(("dp", "ctx")),
            P(("dp", "ctx")),
        ),
        out_specs=(
            P("dp", "ctx", None),
            P("dp", "ctx", None),
            P(("dp", "ctx"), None),
            P(("dp", "ctx"), None),
            P(("dp", "ctx"), None),
            P(("dp", "ctx"), None),
            P(("dp", "ctx"), None),
            P(("dp", "ctx"), None),
            P(("dp", "ctx"), None),
            P(("dp", "ctx")),
            P(("dp", "ctx")),
            P(),
        ),
        check_vma=False,
    )
```

profile of v0, /device:TPU:9, one launch (start us, length us, event | category | flops | bytes accessed | tf_op | source)
XLA Modules:
  0.0 4574.9 jit_solution(2171194354622785981)
XLA Ops:
  14.5 41.0 all-reduce.4
  67.8 22.8 all-gather.17.cloned.1.call-done
  102.9 67.3 %all-gather.15.cloned.1.call-done = bf16[2048,2048]{1,0:T(8,128)(2,1)} async-done(((bf16[64,2048]{1,0:T(8,128)(2,1)}), bf16[2048,2048]{1,0:T(8,128)(2,1)}) %all-gather.15.cloned.1.call-update) | async-done | bytes 8388624 | tf_op jit(solution)/shard_map/all_gather | solution.py:104
  192.4 57.4 %all-gather.11.cloned.1.call-done = bf16[2048,2048]{1,0:T(8,128)(2,1)} async-done(((bf16[64,2048]{1,0:T(8,128)(2,1)}), bf16[2048,2048]{1,0:T(8,128)(2,1)}) %all-gather.11.cloned.1.call-update) | async-done | bytes 8388624 | tf_op jit(solution)/shard_map/all_gather | solution.py:106
  264.8 32.1 all-gather.19.cloned.1.call-done
  306.1 38.0 all-gather.13.cloned.1.call-done
  350.6 74.6 %all-gather.21.cloned.1.call-done = bf16[2048,2048]{1,0:T(8,128)(2,1)} async-done(((bf16[64,2048]{1,0:T(8,128)(2,1)}), bf16[2048,2048]{1,0:T(8,128)(2,1)}) %all-gather.21.cloned.1.call-update) | async-done | bytes 8388624 | tf_op jit(solution)/shard_map/all_gather | solution.py:107
  430.2 190.2 %all-gather.25.cloned.1.call-done = bf16[2048,8192]{1,0:T(8,128)(2,1)} async-done(((bf16[64,8192]{1,0:T(8,128)(2,1)}), bf16[2048,8192]{1,0:T(8,128)(2,1)}) %all-gather.25.cloned.1.call-update) | async-done | bytes 33554448 | tf_op jit(solution)/shard_map/all_gather | solution.py:176
  637.3 179.5 %all-gather.23.cloned.1.call-done = bf16[2048,8192]{1,0:T(8,128)(2,1)} async-done(((bf16[64,8192]{1,0:T(8,128)(2,1)}), bf16[2048,8192]{1,0:T(8,128)(2,1)}) %all-gather.23.cloned.1.call-update) | async-done | bytes 33554448 | tf_op jit(solution)/shard_map/all_gather | solution.py:175
  816.9 17.3 fusion.68
  834.2 179.3 %all-gather.27.cloned.1.call-done = bf16[8192,2048]{1,0:T(8,128)(2,1)} async-done(((bf16[256,2048]{1,0:T(8,128)(2,1)}), bf16[8192,2048]{1,0:T(8,128)(2,1)}) %all-gather.27.cloned.1.call-update) | async-done | bytes 33554448 | tf_op jit(solution)/shard_map/all_gather | solution.py:187
  1013.4 20.9 multiply_convert_fusion.2
  1034.3 17.4 fusion.70
  1051.8 18.1 multiply_reduce_fusion.1
  1099.0 26.1 fusion.73
  1125.0 23.8 fusion.72
  1148.8 88.2 %pad_maximum_fusion = f32[2048,16384]{1,0:T(8,128)} fusion(f32[2048,8192]{1,0:T(8,128)} %fusion.73, f32[2048,8192]{1,0:T(8,128)} %fusion.72), kind=kLoop, calls=%fused_computation | loop fusion | flops 33554432 | bytes 268435456 | tf_op jit(solution)/shard_map/concatenate | solution.py:341
  1286.7 40.5 pad_maximum_fusion.1
  1327.2 63.2 %copy.63 = f32[2048,8192]{1,0:T(8,128)} copy(f32[2048,8192]{0,1:T(8,128)} %pad_maximum_fusion.1) | data formatting | bytes 134217728
  1392.1 24.2 fusion.33
  1450.7 44.1 all-reduce.3
  1497.8 1651.9 %all-reduce.7.cloned.1.call-done = f32[2048,16384]{1,0:T(8,128)} async-done(((f32[2048,16384]{1,0:T(8,128)}), f32[2048,16384]{1,0:T(8,128)}) %all-reduce.7.cloned.1.call-update) | async-done | bytes 134217744
  3154.7 703.5 %reduce-scatter.10.cloned.1.call-done = f32[64,8192]{1,0:T(8,128)} async-done(((f32[2048,8192]{1,0:T(8,128)}), f32[64,8192]{1,0:T(8,128)}) %reduce-scatter.10.cloned.1.call-update) | async-done | bytes 2097168
  3861.1 706.0 %reduce-scatter.8.cloned.1.call-done = f32[256,2048]{1,0:T(8,128)} async-done(((f32[8192,2048]{1,0:T(8,128)}), f32[256,2048]{1,0:T(8,128)}) %reduce-scatter.8.cloned.1.call-update) | async-done | bytes 2097168 | tf_op jit(solution)/shard_map/reduce_scatter | solution.py:356
  (181 shorter events, 230.6 us)
Async XLA Ops:
  7.2 83.4 %all-gather.17.cloned.1.call-start = ((), (), s32[]{:S(2)}) async-start(), calls=%async_computation.6 | async-start | bytes 8650752 | tf_op jit(solution)/shard_map/all_gather | solution.py:105
  9.0 161.2 %all-gather.15.cloned.1.call-start = ((), (), s32[]{:S(2)}) async-start(), calls=%async_computation.5 | async-start | bytes 8650752 | tf_op jit(solution)/shard_map/all_gather | solution.py:104
  10.9 238.9 %all-gather.11.cloned.1.call-start = ((), (), s32[]{:S(2)}) async-start(), calls=%async_computation.3 | async-start | bytes 8650752 | tf_op jit(solution)/shard_map/all_gather | solution.py:106
  12.7 284.2 %all-gather.19.cloned.1.call-start = ((), (), s32[]{:S(2)}) async-start(), calls=%async_computation.7 | async-start | bytes 4718592 | tf_op jit(solution)/shard_map/all_gather | solution.py:131
  55.5 194.3 %copy-start.27 = (f32[2048]{0:T(1024)}, f32[2048]{0:T(1024)S(1)}, u32[]{:S(2)}) copy-start(f32[2048]{0:T(1024)S(1)} %convert_element_type.168) | copy-start | bytes 24580
  67.6 182.2 %copy-start.34 = (f32[128]{0:T(128)}, f32[128]{0:T(128)S(1)}, u32[]{:S(2)}) copy-start(f32[128]{0:T(128)S(1)} %add_rsqrt_fusion.1) | copy-start | bytes 1540
  67.8 123.3 %copy-start.30 = (f32[128,64]{0,1:T(8,128)}, f32[128,64]{0,1:T(8,128)S(1)}, u32[]{:S(2)}) copy-start(f32[128,64]{0,1:T(8,128)S(1)} %get-tuple-element.150) | copy-start | bytes 98308
  67.8 123.3 %copy-start.32 = (f32[128,64]{0,1:T(8,128)}, f32[128,64]{0,1:T(8,128)S(1)}, u32[]{:S(2)}) copy-start(f32[128,64]{0,1:T(8,128)S(1)} %get-tuple-element.151) | copy-start | bytes 98308
  191.5 105.5 %copy-start.25 = (bf16[128,16,64]{0,2,1:T(8,128)(2,1)}, bf16[128,16,64]{0,2,1:T(8,128)(2,1)S(1)}, u32[]{:S(2)}) copy-start(bf16[128,16,64]{0,2,1:T(8,128)(2,1)S(1)} %get-tuple-element.143) | copy-start | bytes 786436
  192.4 64.8 %copy-start.24 = (f32[64,8192]{1,0:T(8,128)S(1)}, f32[64,8192]{1,0:T(8,128)}, u32[]{:S(2)}) copy-start(f32[64,8192]{1,0:T(8,128)} %param.22) | copy-start | bytes 6291460
  192.4 151.7 %all-gather.13.cloned.1.call-start = ((), (), s32[]{:S(2)}) async-start(), calls=%async_computation.4 | async-start | bytes 4718592 | tf_op jit(solution)/shard_map/all_gather | solution.py:132
  255.3 169.9 %all-gather.21.cloned.1.call-start = ((), (), s32[]{:S(2)}) async-start(), calls=%async_computation.8 | async-start | bytes 8650752 | tf_op jit(solution)/shard_map/all_gather | solution.py:107
  257.1 363.2 %all-gather.25.cloned.1.call-start = ((), (), s32[]{:S(2)}) async-start(), calls=%async_computation.10 | async-start | bytes 34603008 | tf_op jit(solution)/shard_map/all_gather | solution.py:176
  258.3 558.6 %all-gather.23.cloned.1.call-start = ((), (), s32[]{:S(2)}) async-start(), calls=%async_computation.9 | async-start | bytes 34603008 | tf_op jit(solution)/shard_map/all_gather | solution.py:175
  261.3 752.2 %all-gather.27.cloned.1.call-start = ((), (), s32[]{:S(2)}) async-start(), calls=%async_computation.11 | async-start | bytes 34603008 | tf_op jit(solution)/shard_map/all_gather | solution.py:187
  264.1 1001.3 %reduce-scatter.6.cloned.1.call-start = ((), (), s32[]{:S(2)}) async-start(), calls=%async_computation.12 | async-start | bytes 18874368 | tf_op jit(solution)/shard_map/reduce_scatter | solution.py:285
  350.6 79.3 %copy-start.14 = (bf16[16,128,128]{2,1,0:T(8,128)(2,1)}, bf16[16,128,128]{2,1,0:T(8,128)(2,1)S(1)}, u32[]{:S(2)}) copy-start(bf16[16,128,128]{2,1,0:T(8,128)(2,1)S(1)} %fusion.19) | copy-start | bytes 1572868
  430.0 639.8 %copy-start.5 = (f32[128,2048]{1,0:T(8,128)}, f32[128,2048]{1,0:T(8,128)S(1)}, u32[]{:S(2)}) copy-start(f32[128,2048]{1,0:T(8,128)S(1)} %get-tuple-element.153) | copy-start | bytes 3145732
  637.3 376.1 %copy-start.22 = (bf16[1,128,2048]{2,1,0:T(8,128)(2,1)S(1)}, bf16[1,128,2048]{2,1,0:T(8,128)(2,1)}, u32[]{:S(2)}) copy-start(bf16[1,128,2048]{2,1,0:T(8,128)(2,1)} %param.14) | copy-start | bytes 1572868
  1098.9 2050.9 %all-reduce.7.cloned.1.call-start = ((), (), s32[]{:S(2)}) async-start(), calls=%async_computation.15 | async-start | bytes 268435456
  1098.9 26.1 copy-start.12
  1237.0 2621.2 %reduce-scatter.10.cloned.1.call-start = ((), (), s32[]{:S(2)}) async-start(), calls=%async_computation.14 | async-start | bytes 69206016
  1390.4 3176.7 %reduce-scatter.8.cloned.1.call-start = ((), (), s32[]{:S(2)}) async-start(), calls=%async_computation.13 | async-start | bytes 69206016 | tf_op jit(solution)/shard_map/reduce_scatter | solution.py:356
  1447.6 49.0 %copy-start.10 = (f32[128,2048]{1,0:T(8,128)S(1)}, f32[128,2048]{1,0:T(8,128)}, u32[]{:S(2)}) copy-start(f32[128,2048]{1,0:T(8,128)} %copy-done.8) | copy-start | bytes 3145732
  (32 other events, 314.5 us)
Sparse Core Ops, SparseCore 0:
  11.6 78.9 all-gather.16
  94.2 75.9 all-gather.14
  173.8 75.9 all-gather.10
  251.8 45.0 all-gather.18
  298.9 45.1 all-gather.12
  347.5 77.6 all-gather.20
  428.8 191.4 all-gather.24
  623.9 192.9 all-gather.22
  820.4 192.9 all-gather.26
  1099.0 166.3 reduce-scatter.5
  1271.8 1877.8 all-reduce.6
  3152.0 706.1 reduce-scatter.9
  3861.1 705.8 reduce-scatter.7
where the time goes:
time: 4590 us; the launch traced here: 4570 us
  waiting for transfers between devices  3920 us (85%)
  matrix products  282 us (6%)
  other arithmetic  159 us (3%)
  local copies, waits for them, and re-layouts  104 us (2%)
  blocking collectives  94.4 us (2%)
    unnamed x15, waiting for transfers between devices  2360 us
    reduce_scatter x1, waiting for transfers between devices, shards(): lax.psum_scatter(lax.dot_general(hidden, grad_out, contract_rows, preferr...  706 us
    all_gather x1, waiting for transfers between devices, shards(): up_piece = lax.all_gather(mlp_pack[1], ('dp', 'ctx'), axis=0, tiled=True)  190 us
    all_gather x1, waiting for transfers between devices, shards(): gate_piece = lax.all_gather(mlp_pack[0], ('dp', 'ctx'), axis=0, tiled=True)  180 us
    all_gather x1, waiting for transfers between devices, shards(): lax.all_gather(down_pack, ('dp', 'ctx'), axis=0, tiled=True)  179 us
  transfers between devices with their start and end apart: 13, of which 13 were waited for; matrix products, arithmetic and copies ran while one was open for 10% of the time, Pallas kernels for 0%

commit v1 on v0

v1 whole, which is shorter than its diff:
```python
import math

import jax
import jax.numpy as jnp
from jax import lax
from jax.sharding import PartitionSpec as P

HEAD_DIM = 128
norm_eps = 1e-05
rope_base = 10000.0
score_shift = math.log(4096.0)
score_scale = 1.0 / math.sqrt(HEAD_DIM)
contract_rows = (((0,), (0,)), ((), ()))
contract_cols = (((1,), (1,)), ((), ()))
f32 = jnp.float32
bf16 = jnp.bfloat16


def dot(a, b, dims=(((1,), (0,)), ((), ()))):
    return lax.dot_general(a, b, dims, preferred_element_type=f32)


def rope_tables(positions):
    half_dim = HEAD_DIM // 2
    inverse = jnp.exp(
        jnp.arange(half_dim, dtype=f32) * (-2.0 * math.log(rope_base) / HEAD_DIM)
    )
    angles = positions[:, None] * inverse[None, :]
    return jnp.cos(angles), jnp.sin(angles)


def rotate(values, cosines, sines, sign):
    half = HEAD_DIM // 2
    parts = []
    for h in range(values.shape[1] // HEAD_DIM):
        a = values[:, h * HEAD_DIM : h * HEAD_DIM + half]
        b = values[:, h * HEAD_DIM + half : (h + 1) * HEAD_DIM]
        parts += [a * cosines - sign * b * sines, b * cosines + sign * a * sines]
    return jnp.concatenate(parts, axis=1)


def inverse_rms(values):
    return lax.rsqrt(jnp.mean(values * values, axis=-1, keepdims=True) + norm_eps)


def gather(v, axes, axis=0):
    return lax.all_gather(v, axes, axis=axis, tiled=True)


def scatter_sum(v, axes):
    return lax.psum_scatter(v, axes, scatter_dimension=0, tiled=True)


def swap(v, axes):
    return lax.all_to_all(v, axes, split_axis=0, concat_axis=0, tiled=True)


def shards(
    hidden_in,
    out_grad,
    seg_ids,
    valid_mask,
    w_query,
    w_key,
    w_value,
    w_output,
    w_gate,
    w_up,
    w_down,
    gain_attn,
    gain_mlp,
):
    dpn = lax.axis_size("dp")
    cn = lax.axis_size("ctx")
    x_local = hidden_in[0]
    rows, width = x_local.shape
    seq = rows * cn
    dr = w_query.shape[0]
    hw = width // cn
    heads = hw // HEAD_DIM
    ff_rows = w_down.shape[0]
    ff = ff_rows * dpn

    codes = gather(seg_ids[0] * 2 + valid_mask[0], "ctx")
    seg = codes // 2
    valid = codes % 2
    index = jnp.arange(seq, dtype=jnp.int32)
    starts = jnp.sum((seg[None, :] < seg[:, None]).astype(jnp.int32), axis=1)
    cosines, sines = rope_tables((index - starts).astype(f32))
    allowed = (
        (seg[:, None] == seg[None, :])
        & (index[None, :] <= index[:, None])
        & (valid[None, :] == 1)
    )

    gains = gather(jnp.stack([gain_attn, gain_mlp], axis=1).astype(bf16), ("dp", "ctx")).astype(f32)
    gain_one = gains[:, 0]
    gain_two = gains[:, 1]

    qkv = jnp.concatenate(
        [w.astype(bf16).reshape(dr, cn, hw) for w in (w_query, w_key, w_value)], axis=2
    ).transpose(1, 0, 2)
    out_cols = w_output.astype(bf16)
    qkv = gather(swap(qkv, "ctx").reshape(cn * dr, 3 * hw), "dp")
    owner = lax.axis_index("dp") * cn + lax.axis_index("ctx")
    wo_full = gather(out_cols, ("dp", "ctx"))
    wo = lax.dynamic_slice_in_dim(wo_full, lax.axis_index("ctx") * hw, hw, 0)
    gate_up = jnp.concatenate(
        [w.astype(bf16).reshape(dr, dpn, cn, ff_rows) for w in (w_gate, w_up)], axis=1
    ).transpose(2, 0, 1, 3).reshape(cn, dr, 2 * ff)
    gate_up = gather(swap(gate_up, "ctx").reshape(cn * dr, 2 * ff), "dp")
    down = gather(w_down.astype(bf16), "dp")

    xs = gather(x_local, "ctx").astype(f32)
    dy_local = out_grad[0]
    dys = gather(dy_local, "ctx")
    inv_all = inverse_rms(xs)
    xh_all = xs * inv_all
    an = (xh_all * gain_one).astype(bf16)
    proj = dot(an, qkv)
    q = rotate(proj[:, :hw], cosines, sines, 1.0).astype(bf16)
    k = rotate(proj[:, hw : 2 * hw], cosines, sines, 1.0).astype(bf16)
    v = proj[:, 2 * hw :].astype(bf16)

    def per_head(t, h):
        return t[:, h * HEAD_DIM : (h + 1) * HEAD_DIM]

    outs = []
    mass = jnp.zeros((seq,), f32)
    for h in range(heads):
        s = dot(per_head(q, h), per_head(k, h), contract_cols) * score_scale - score_shift
        p = jnp.where(allowed, jax.nn.sigmoid(s), 0.0)
        mass = mass + jnp.sum(p, axis=1)
        outs.append(dot(p.astype(bf16), per_head(v, h)))
    o = jnp.concatenate(outs, axis=1).astype(bf16)
    x_f = x_local.astype(f32)
    h1 = x_f + scatter_sum(dot(o, wo).astype(bf16), "ctx").astype(f32)
    r2 = inverse_rms(h1)
    xh2 = h1 * r2
    bn = gather((xh2 * gain_two).astype(bf16), "ctx")
    gu = dot(bn, gate_up)
    gate = gu[:, :ff]
    up = gu[:, ff:]
    sig = jax.nn.sigmoid(gate)
    silu = gate * sig
    hid = (silu * up).astype(bf16)
    result = h1 + scatter_sum(dot(hid, down).astype(bf16), "ctx").astype(f32)
    dhid = dot(dys, down, contract_cols)
    dgate = (dhid * up * sig * (1.0 + gate * (1.0 - sig))).astype(bf16)
    dup = (dhid * silu).astype(bf16)
    dgu = jnp.concatenate([dgate, dup], axis=1)
    dbn = scatter_sum(dot(dgu, gate_up, contract_cols).astype(bf16), "ctx").astype(f32)
    g_gu = scatter_sum(dot(bn, dgu, contract_rows).astype(bf16), "dp")
    g_down = scatter_sum(dot(hid, dys, contract_rows).astype(bf16), "dp")
    term_two = jnp.sum(dbn * xh2, axis=0)
    u2 = dbn * gain_two
    dh1 = dy_local.astype(f32) + r2 * (u2 - xh2 * jnp.mean(u2 * xh2, axis=-1, keepdims=True))
    dob = gather(dh1.astype(bf16), "ctx")
    do = dot(dob, wo, contract_cols).astype(bf16)
    dqs, dks, dvs = [], [], []
    for h in range(heads):
        qh, kh, vh, doh = (per_head(t, h) for t in (q, k, v, do))
        s = dot(qh, kh, contract_cols) * score_scale - score_shift
        sg = jnp.where(allowed, jax.nn.sigmoid(s), 0.0)
        pb = sg.astype(bf16)
        ds = (dot(doh, vh, contract_cols) * sg * (1.0 - sg)).astype(bf16)
        dqs.append(dot(ds, kh) * score_scale)
        dks.append(dot(ds, qh, contract_rows) * score_scale)
        dvs.append(dot(pb, doh, contract_rows))
    dq = rotate(jnp.concatenate(dqs, axis=1), cosines, sines, -1.0).astype(bf16)
    dk = rotate(jnp.concatenate(dks, axis=1), cosines, sines, -1.0).astype(bf16)
    dv = jnp.concatenate(dvs, axis=1).astype(bf16)
    dqkv = jnp.concatenate([dq, dk, dv], axis=1)
    dan_part = dot(dqkv, qkv, contract_cols)
    term_one = jnp.sum(dan_part * xh_all, axis=0)
    dan = scatter_sum(dan_part.astype(bf16), "ctx").astype(f32)
    inv_one = inverse_rms(x_f)
    xh1 = x_f * inv_one
    u1 = dan * gain_one
    grad_input = dh1 + inv_one * (u1 - xh1 * jnp.mean(u1 * xh1, axis=-1, keepdims=True))

    g_qkv = dot(an, dqkv, contract_rows).astype(bf16)
    g_out = dot(o, dob, contract_rows).astype(bf16)
    g_out_full = jnp.zeros((width, width), bf16)
    g_out_full = lax.dynamic_update_slice_in_dim(g_out_full, g_out, lax.axis_index("ctx") * hw, 0)
    g_out_own = scatter_sum(g_out_full, ("dp", "ctx")).astype(f32)
    g_qkv = swap(scatter_sum(g_qkv, "dp").reshape(cn, dr, 3 * hw), "ctx").astype(f32)
    g_q, g_k, g_v = (
        g_qkv[:, :, i * hw : (i + 1) * hw].transpose(1, 0, 2).reshape(dr, width) for i in range(3)
    )
    g_gu = swap(g_gu.reshape(cn, dr, 2 * ff), "ctx").astype(f32)
    g_gate, g_up = (
        g_gu[:, :, i * ff : (i + 1) * ff]
        .reshape(cn, dr, dpn, ff_rows)
        .transpose(1, 2, 0, 3)
        .reshape(dr, dpn * cn * ff_rows)
        for i in range(2)
    )
    totals = lax.psum(
        (term_one, term_two, jnp.sum(valid.astype(f32) * mass) / (heads * cn)), ("dp", "ctx")
    )
    grad_gain_attn = lax.dynamic_slice_in_dim(totals[0], owner * dr, dr)
    grad_gain_mlp = lax.dynamic_slice_in_dim(totals[1], owner * dr, dr)
    mass_mean = totals[2] / (dpn * seq)
    return (
        result.astype(bf16)[None],
        grad_input.astype(bf16)[None],
        g_q,
        g_k,
        g_v,
        g_out_own,
        g_gate,
        g_up,
        g_down.astype(f32),
        grad_gain_attn,
        grad_gain_mlp,
        mass_mean,
    )


def solution(mesh):
    tok = P("dp", "ctx", None)
    ids = P("dp", "ctx")
    mat = P(("dp", "ctx"), None)
    vec = P(("dp", "ctx"))
    return jax.shard_map(
        shards,
        mesh=mesh,
        in_specs=(tok, tok, ids, ids) + (mat,) * 7 + (vec, vec),
        out_specs=(tok, tok) + (mat,) * 7 + (vec, vec, P()),
        check_vma=False,
    )
```

time: 4590 us -> 1130 us (0.25)
  waiting for transfers between devices: 3920 us -> 625 us
  blocking collectives: 94.4 us -> 266 us
  matrix products: 282 us -> 116 us
  other arithmetic: 159 us -> 39.3 us
  local copies, waits for them, and re-layouts: 104 us -> 34.9 us
    unnamed x15 -> x16, waiting for transfers between devices: 2360 us -> 1.61 us
    all_gather x9 -> x8, waiting for transfers between devices: 841 us -> 323 us  [gather(): return lax.all_gather(v, axes, axis=axis, tiled=True)]
    reduce_scatter x2 -> x8, waiting for transfers between devices: 721 us -> 300 us  [scatter_sum(): return lax.psum_scatter(v, axes, scatter_dimension=0, tiled=True)]
    all_to_all x0 -> x3, blocking collectives: none -> 171 us  [swap(): return lax.all_to_all(v, axes, split_axis=0, concat_axis=0, tiled=True)]
    dot_general x27 -> x24, matrix products: 282 us -> 116 us  [dot(): return lax.dot_general(a, b, dims, preferred_element_type=f32)]
    concatenate x4 -> x0, other arithmetic: 136 us -> none  [the longest x1 88.2 us: shards(): jnp.concatenate([lax.dot_general(columns, grad_gate_b, contract_rows, pre...]
    unnamed x91 -> x108, local copies, waits for them, and re-layouts: 68.9 us -> 14.1 us
  transfers between devices with their start and end apart: 13 -> 17, of which waited for: 13 -> 13; matrix products, arithmetic and copies ran while one was open for 10% -> 13% of each run, Pallas kernels for 0% -> 0%
where the time goes in v1:
time: 1130 us; the launch traced here: 1110 us
  waiting for transfers between devices  625 us (55%)
  blocking collectives  266 us (24%)
  matrix products  116 us (10%)
  other arithmetic  39.3 us (3%)
  local copies, waits for them, and re-layouts  34.9 us (3%)
  between operations  17.7 us (2%)
    all_gather x8, waiting for transfers between devices, gather(): return lax.all_gather(v, axes, axis=axis, tiled=True)  323 us
    reduce_scatter x8, waiting for transfers between devices, scatter_sum(): return lax.psum_scatter(v, axes, scatter_dimension=0, tiled=True)  300 us
    all_to_all x3, blocking collectives, swap(): return lax.all_to_all(v, axes, split_axis=0, concat_axis=0, tiled=True)  171 us
    dot_general x24, matrix products, dot(): return lax.dot_general(a, b, dims, preferred_element_type=f32)  116 us
    all_gather x2, blocking collectives, gather(): return lax.all_gather(v, axes, axis=axis, tiled=True)  53.5 us
    psum x1, blocking collectives, shards(): lax.psum((term_one, term_two, jnp.sum(valid.astype(f32) * mass) / (heads...  41.5 us
  transfers between devices with their start and end apart: 17, of which 13 were waited for; matrix products, arithmetic and copies ran while one was open for 13% of the time, Pallas kernels for 0%

profile of v1, /device:TPU:9, one launch (start us, length us, event | category | flops | bytes accessed | tf_op | source)
XLA Modules:
  0.0 1108.1 jit_solution(13455781456987480580)
XLA Ops:
  11.7 41.3 %all_to_all.20 = bf16[8,64,768]{2,1,0:T(8,128)(2,1)} all-to-all(bf16[8,64,768]{2,1,0:T(8,128)(2,1)S(1)} %copy.73), channel_id=1, replica_groups=mesh['dp'=4,'ctx'=8] {'ctx'}, dimensions={0} | all-to-all | bytes 1572864 | tf_op jit(solution)/shard_map/all_to_all | solution.py:55
  53.9 40.1 %all-gather.3 = bf16[32,64,2]{1,2,0:T(2,128)(2,1)S(1)} all-gather(bf16[1,64,2]{1,2,0:T(2,128)(2,1)S(1)} %maximum_bitcast_fusion.2), channel_id=1, replica_groups=mesh['dp'=4,'ctx'=8] {'dp','ctx'}, dimensions={0}, use_global_device_ids=true | all-gather | bytes 8448 | tf_op jit(solution)/shard_map/all_gather | solution.py:47
  94.1 13.4 %all-gather = s32[1,1024]{1,0:T(1,128)S(1)} all-gather(s32[1,128]{1,0:T(1,128)S(1)} %multiply_add_fusion), channel_id=2, replica_groups=mesh['dp'=4,'ctx'=8] {'ctx'}, dimensions={1}, use_global_device_ids=true | all-gather | bytes 4608 | tf_op jit(solution)/shard_map/all_gather | solution.py:47
  132.6 66.2 %all-gather.15.cloned.1.call-done = bf16[2048,2048]{1,0:T(8,128)(2,1)} async-done(((bf16[64,2048]{1,0:T(8,128)(2,1)}), bf16[2048,2048]{1,0:T(8,128)(2,1)}) %all-gather.15.cloned.1.call-update) | async-done | bytes 8388624 | tf_op jit(solution)/shard_map/all_gather | solution.py:47
  209.4 78.4 %all_to_all.21 = bf16[8,64,2048]{2,1,0:T(8,128)(2,1)} all-to-all(bf16[8,64,2048]{2,1,0:T(8,128)(2,1)} %reshape.134), channel_id=1, replica_groups=mesh['dp'=4,'ctx'=8] {'ctx'}, dimensions={0} | all-to-all | bytes 4194304 | tf_op jit(solution)/shard_map/all_to_all | solution.py:55
  301.3 82.8 %all-gather.19.cloned.1.call-done = bf16[2048,2048]{1,0:T(8,128)(2,1)} async-done(((bf16[512,2048]{1,0:T(8,128)(2,1)}), bf16[2048,2048]{1,0:T(8,128)(2,1)}) %all-gather.19.cloned.1.call-update) | async-done | bytes 8388624 | tf_op jit(solution)/shard_map/all_gather | solution.py:47
  384.0 48.1 %all-gather.17.cloned.1.call-done = bf16[1024,2048]{1,0:T(8,128)(2,1)} async-done(((bf16[128,2048]{1,0:T(8,128)(2,1)}), bf16[1024,2048]{1,0:T(8,128)(2,1)}) %all-gather.17.cloned.1.call-update) | async-done | bytes 4194320 | tf_op jit(solution)/shard_map/all_gather | solution.py:47
  432.1 14.6 %fusion.144 = f32[1024,2048]{0,1:T(8,128)} fusion(bf16[1024,2048]{1,0:T(8,128)(2,1)} %all-gather.17.cloned.1.call-done, bf16[2048,2048]{1,0:T(8,128)(2,1)} %all-gather.19.cloned.1.call-done), kind=kOutput, calls=%fused_computation.209 | convolution fusion | flops 8589934592 | bytes 20971520 | tf_op jit(solution)/shard_map/dot_general | solution.py:20
  446.7 40.4 %all-gather.21.cloned.1.call-done = bf16[1024,2048]{1,0:T(8,128)(2,1)} async-done(((bf16[256,2048]{1,0:T(8,128)(2,1)}), bf16[1024,2048]{1,0:T(8,128)(2,1)}) %all-gather.21.cloned.1.call-update) | async-done | bytes 4194320 | tf_op jit(solution)/shard_map/all_gather | solution.py:47
  487.1 47.7 %all-gather.27.cloned.1.call-done = bf16[1,1024,2048]{2,1,0:T(8,128)(2,1)} async-done(((bf16[1,128,2048]{2,1,0:T(8,128)(2,1)}), bf16[1,1024,2048]{2,1,0:T(8,128)(2,1)}) %all-gather.27.cloned.1.call-update) | async-done | bytes 4194320 | tf_op jit(solution)/shard_map/all_gather | solution.py:47
  534.8 13.3 %multiply_convert_fusion.3 = (bf16[1024,1024]{0,1:T(8,128)(2,1)S(1)}, bf16[1024,1024]{0,1:T(8,128)(2,1)S(1)}, bf16[1024,1024]{0,1:T(8,128)(2,1)}) fusion(f32[1024,2048]{0,1:T(8,128)} %fusion.144, bf16[1024,2048]{1,0:T(8,128)(2,1)} %all-gather.21.cloned.1.call-done, bf16[1,1024,2048]{2,1,0:T(8,128)(2,1)} %all-gather.27.cloned.1.call-done), kind=kOutput, calls=%fused_computation.16 | convolution fusion | flops 4310695936 | bytes 23068672 | tf_op jit(solution)/shard_map/dot_general | solution.py:20
  550.0 10.9 convolution_convert_fusion.1
  561.0 48.4 %reduce-scatter.13.cloned.1.call-done = bf16[128,2048]{1,0:T(8,128)(2,1)} async-done(((bf16[1024,2048]{1,0:T(8,128)(2,1)}), bf16[128,2048]{1,0:T(8,128)(2,1)}) %reduce-scatter.13.cloned.1.call-update) | async-done | bytes 524304 | tf_op jit(solution)/shard_map/reduce_scatter | solution.py:51
  614.0 13.9 %convolution_convert_fusion = bf16[2048,2048]{1,0:T(8,128)(2,1)} fusion(bf16[1024,2048]{1,0:T(8,128)(2,1)} %all-gather.17.cloned.1.call-done, bf16[1024,1024]{0,1:T(8,128)(2,1)} %copy-done.49, bf16[1024,1024]{0,1:T(8,128)(2,1)} %copy-done.48), kind=kOutput, calls=%fused_computation.7 | convolution fusion | flops 8602517504 | bytes 16777216 | tf_op jit(solution)/shard_map/dot_general | solution.py:20
  628.1 31.6 %all-gather.23.cloned.1.call-done = bf16[1024,2048]{1,0:T(8,128)(2,1)} async-done(((bf16[128,2048]{1,0:T(8,128)(2,1)}), bf16[1024,2048]{1,0:T(8,128)(2,1)}) %all-gather.23.cloned.1.call-update) | async-done | bytes 4194320 | tf_op jit(solution)/shard_map/all_gather | solution.py:47
  687.9 9.7 fusion.12
  699.1 8.8 fusion.3
  708.0 9.6 convolution_convert_fusion.3
  724.4 24.7 %reduce-scatter.21.cloned.1.call-done = bf16[512,2048]{1,0:T(8,128)(2,1)} async-done(((bf16[2048,2048]{1,0:T(8,128)(2,1)}), bf16[512,2048]{1,0:T(8,128)(2,1)}) %reduce-scatter.21.cloned.1.call-update) | async-done | bytes 2097168 | tf_op jit(solution)/shard_map/reduce_scatter | solution.py:51
  749.1 51.6 %all_to_all.22 = bf16[8,64,2048]{2,1,0:T(8,128)(2,1)S(1)} all-to-all(bf16[8,64,2048]{2,1,0:T(8,128)(2,1)} %bitcast.123), channel_id=1, replica_groups=mesh['dp'=4,'ctx'=8] {'ctx'}, dimensions={0} | all-to-all | bytes 4194304 | tf_op jit(solution)/shard_map/all_to_all | solution.py:55
  809.5 42.7 %reduce-scatter.23.cloned.1.call-done = bf16[256,2048]{1,0:T(8,128)(2,1)} async-done(((bf16[1024,2048]{1,0:T(8,128)(2,1)}), bf16[256,2048]{1,0:T(8,128)(2,1)}) %reduce-scatter.23.cloned.1.call-update) | async-done | bytes 1048592 | tf_op jit(solution)/shard_map/reduce_scatter | solution.py:51
  855.0 41.5 %all-reduce = (f32[2048]{0:T(1024)S(1)}, f32[2048]{0:T(1024)S(1)}, f32[]{:T(128)}) all-reduce(f32[2048]{0:T(1024)S(1)} %get-tuple-element.20, f32[2048]{0:T(1024)S(1)} %copy-done.29, f32[]{:T(128)S(6)} %div.57), channel_id=1, replica_groups=mesh['dp'=4,'ctx'=8] {'dp','ctx'}, use_global_device_ids=true, to_apply=%region_15.16 | all-reduce | flops 4097 | bytes 32776 | tf_op jit(solution)/shard_map/psum | solution.py:199
  918.1 36.1 %reduce-scatter.11.cloned.1.call-done = bf16[128,2048]{1,0:T(8,128)(2,1)} async-done(((bf16[1024,2048]{1,0:T(8,128)(2,1)}), bf16[128,2048]{1,0:T(8,128)(2,1)}) %reduce-scatter.11.cloned.1.call-update) | async-done | bytes 524304 | tf_op jit(solution)/shard_map/reduce_scatter | solution.py:51
  957.2 141.0 %reduce-scatter.19.cloned.1.call-done = bf16[64,2048]{1,0:T(8,128)(2,1)} async-done(((bf16[2048,2048]{1,0:T(8,128)(2,1)}), bf16[64,2048]{1,0:T(8,128)(2,1)}) %reduce-scatter.19.cloned.1.call-update) | async-done | bytes 262160 | tf_op jit(solution)/shard_map/reduce_scatter | solution.py:51
  (224 shorter events, 133.7 us)
Async XLA Ops:
  7.2 101.0 %all-gather.25.cloned.1.call-start = ((), (), s32[]{:S(2)}) async-start(), calls=%async_computation.26 | async-start | bytes 4718592 | tf_op jit(solution)/shard_map/all_gather | solution.py:47
  7.9 109.5 %all-gather.13.cloned.1.call-start = ((), (), s32[]{:S(2)}) async-start(), calls=%async_computation.12 | async-start | bytes 3932160 | tf_op jit(solution)/shard_map/all_gather | solution.py:47
  10.3 83.9 %copy-start.46 = (s32[1,128]{1,0:T(1,128)S(1)}, s32[1,128]{1,0:T(1,128)}, u32[]{:S(2)}) copy-start(s32[1,128]{1,0:T(1,128)} %param.16) | copy-start | bytes 1540
  10.3 83.8 %copy-start.47 = (s32[1,128]{1,0:T(1,128)S(1)}, s32[1,128]{1,0:T(1,128)}, u32[]{:S(2)}) copy-start(s32[1,128]{1,0:T(1,128)} %param.15) | copy-start | bytes 1540
  53.0 145.8 %all-gather.15.cloned.1.call-start = ((), (), s32[]{:S(2)}) async-start(), calls=%async_computation.13 | async-start | bytes 8650752 | tf_op jit(solution)/shard_map/all_gather | solution.py:47
  53.8 241.5 %reduce-scatter.9.cloned.1.call-start = ((), (), s32[]{:S(2)}) async-start(), calls=%async_computation.14 | async-start | bytes 4718592 | tf_op jit(solution)/shard_map/reduce_scatter | solution.py:51
  203.3 180.7 %all-gather.19.cloned.1.call-start = ((), (), s32[]{:S(2)}) async-start(), calls=%async_computation.16 | async-start | bytes 10485760 | tf_op jit(solution)/shard_map/all_gather | solution.py:47
  209.4 85.9 %copy-start.4 = (bf16[1,128,2048]{2,1,0:T(8,128)(2,1)S(1)}, bf16[1,128,2048]{2,1,0:T(8,128)(2,1)}, u32[]{:S(2)}) copy-start(bf16[1,128,2048]{2,1,0:T(8,128)(2,1)} %param.13) | copy-start | bytes 1572868
  209.4 89.9 %copy-start.12 = (f32[256,2048]{1,0:T(8,128)S(1)}, f32[256,2048]{1,0:T(8,128)}, u32[]{:S(2)}) copy-start(f32[256,2048]{1,0:T(8,128)} %param.23) | copy-start | bytes 6291460
  287.9 144.2 %all-gather.17.cloned.1.call-start = ((), (), s32[]{:S(2)}) async-start(), calls=%async_computation.15 | async-start | bytes 4718592 | tf_op jit(solution)/shard_map/all_gather | solution.py:47
  299.3 187.8 %all-gather.21.cloned.1.call-start = ((), (), s32[]{:S(2)}) async-start(), calls=%async_computation.17 | async-start | bytes 5242880 | tf_op jit(solution)/shard_map/all_gather | solution.py:47
  300.5 234.3 %all-gather.27.cloned.1.call-start = ((), (), s32[]{:S(2)}) async-start(), calls=%async_computation.27 | async-start | bytes 4718592 | tf_op jit(solution)/shard_map/all_gather | solution.py:47
  301.2 308.2 %reduce-scatter.13.cloned.1.call-start = ((), (), s32[]{:S(2)}) async-start(), calls=%async_computation.19 | async-start | bytes 4718592 | tf_op jit(solution)/shard_map/reduce_scatter | solution.py:51
  560.9 98.8 %all-gather.23.cloned.1.call-start = ((), (), s32[]{:S(2)}) async-start(), calls=%async_computation.20 | async-start | bytes 4718592 | tf_op jit(solution)/shard_map/all_gather | solution.py:47
  613.9 135.2 %reduce-scatter.21.cloned.1.call-start = ((), (), s32[]{:S(2)}) async-start(), calls=%async_computation.24 | async-start | bytes 10485760 | tf_op jit(solution)/shard_map/reduce_scatter | solution.py:51
  627.9 172.7 %reduce-scatter.17.cloned.1.call-start = ((), (), s32[]{:S(2)}) async-start(), calls=%async_computation.22 | async-start | bytes 3932160 | tf_op jit(solution)/shard_map/reduce_scatter | solution.py:51
  687.6 164.5 %reduce-scatter.23.cloned.1.call-start = ((), (), s32[]{:S(2)}) async-start(), calls=%async_computation.25 | async-start | bytes 5242880 | tf_op jit(solution)/shard_map/reduce_scatter | solution.py:51
  697.6 219.1 %reduce-scatter.15.cloned.1.call-start = ((), (), s32[]{:S(2)}) async-start(), calls=%async_computation.21 | async-start | bytes 4718592 | tf_op jit(solution)/shard_map/reduce_scatter | solution.py:51
  708.0 246.2 %reduce-scatter.11.cloned.1.call-start = ((), (), s32[]{:S(2)}) async-start(), calls=%async_computation.18 | async-start | bytes 4718592 | tf_op jit(solution)/shard_map/reduce_scatter | solution.py:51
  717.6 380.6 %reduce-scatter.19.cloned.1.call-start = ((), (), s32[]{:S(2)}) async-start(), calls=%async_computation.23 | async-start | bytes 8650752 | tf_op jit(solution)/shard_map/reduce_scatter | solution.py:51
  724.4 83.8 %copy-start.28 = (s32[1,1024]{1,0:T(1,128)S(1)}, s32[1,1024]{1,0:T(1,128)}, u32[]{:S(2)}) copy-start(s32[1,1024]{1,0:T(1,128)} %copy-done.27) | copy-start | bytes 12292
  749.1 105.9 %copy-start.41 = (f32[128]{0:T(128)S(1)}, f32[128]{0:T(128)}, u32[]{:S(2)}) copy-start(f32[128]{0:T(128)} %get-tuple-element.14) | copy-start | bytes 1540
  749.1 105.9 %copy-start.29 = (f32[2048]{0:T(1024)S(1)}, f32[2048]{0:T(1024)}, u32[]{:S(2)}) copy-start(f32[2048]{0:T(1024)} %get-tuple-element.12) | copy-start | bytes 24580
  800.6 112.1 %all-to-all-start.2 = ((bf16[8,64,768]{2,1,0:T(8,128)(2,1)}), bf16[8,64,768]{2,1,0:T(8,128)(2,1)}, u32[]{:S(2)}, u32[]{:S(2)}) async-start(bf16[8,64,768]{2,1,0:T(8,128)(2,1)} %bitcast.132), calls=%async_computation.7 | async-start | bytes 1572864 | tf_op jit(solution)/shard_map/all_to_all | solution.py:55
  (43 other events, 807.4 us)
Sparse Core Ops, SparseCore 0:
  9.6 59.6 all-gather.24
  71.2 46.1 all-gather.12
  121.0 77.7 all-gather.14
  203.4 91.8 reduce-scatter.8
  297.0 86.9 all-gather.18
  386.1 46.0 all-gather.16
  434.5 52.5 all-gather.20
  488.7 46.0 all-gather.26
  561.1 48.3 reduce-scatter.12
  614.0 45.6 all-gather.22
  662.8 86.1 reduce-scatter.20
  752.2 43.9 reduce-scatter.16
  799.4 52.6 reduce-scatter.22
  854.3 49.5 reduce-scatter.14
  906.0 48.1 reduce-scatter.10
  956.3 141.8 reduce-scatter.18

commit v2 on v1

v2 whole, which is shorter than its diff:
```python
import functools
import math

import jax
import jax.numpy as jnp
from jax import lax
from jax.experimental import pallas as pl
from jax.experimental.pallas import tpu as pltpu
from jax.sharding import PartitionSpec as P

HEAD_DIM = 128
norm_eps = 1e-05
rope_base = 10000.0
score_shift = math.log(4096.0)
score_scale = 1.0 / math.sqrt(HEAD_DIM)
contract_rows = (((0,), (0,)), ((), ()))
contract_cols = (((1,), (1,)), ((), ()))
plain = (((1,), (0,)), ((), ()))
f32 = jnp.float32
bf16 = jnp.bfloat16
MESH = pl.DeviceIdType.MESH
ANY = pl.BlockSpec(memory_space=pl.ANY)
VMEM = pl.BlockSpec(memory_space=pltpu.VMEM)


def dot(a, b, dims=plain):
    return lax.dot_general(a, b, dims, preferred_element_type=f32)


def remote(src, dst, send, recv, target):
    return pltpu.make_async_remote_copy(
        src_ref=src,
        dst_ref=dst,
        send_sem=send,
        recv_sem=recv,
        device_id=target,
        device_id_type=MESH,
    )


def greet(target):
    pl.semaphore_signal(
        pltpu.get_barrier_semaphore(), inc=1, device_id=target, device_id_type=MESH
    )


def place(cn):
    c = lax.axis_index("ctx")
    j, k = c // 2, c % 2
    return c, j, k, cn // 2, 2 * j + 1 - k


def greet_line(cn):
    c, j, _, n, sib = place(cn)
    greet({"ctx": sib})

    @pl.when(j < n - 1)
    def _():
        greet({"ctx": c + 2})

    @pl.when(j > 0)
    def _():
        greet({"ctx": c - 2})

    inner = jnp.where(j > 0, 1, 0) + jnp.where(j < n - 1, 1, 0)
    pl.semaphore_wait(pltpu.get_barrier_semaphore(), 1 + inner)


def greet_ctx(cn):
    c = lax.axis_index("ctx")
    for s in range(1, cn):
        greet({"ctx": lax.rem(c + s, cn)})


class LineGather:
    def __init__(self, cn, own, full, sem):
        self.cn, self.own, self.full, self.sem = cn, own, full, sem

    def copy(self, src, origin, kind, target):
        _, _, k, _, _ = place(self.cn)
        sem = self.sem
        return remote(
            src,
            self.full.at[2 * origin + k],
            sem.at[kind, origin],
            sem.at[3 if kind < 2 else 4, origin],
            {"ctx": target},
        )

    def start(self):
        c, j, _, n, sib = place(self.cn)

        @pl.when(j < n - 1)
        def _():
            self.copy(self.own, j, 0, c + 2).start()

        @pl.when(j > 0)
        def _():
            self.copy(self.own, j, 1, c - 2).start()

        self.copy(self.own, j, 2, sib).start()

    def forward(self):
        c, j, k, n, sib = place(self.cn)
        for s in range(1, n):

            @pl.when(j - s >= 0)
            def _():
                o = j - s
                block = self.full.at[2 * o + k]
                self.copy(block, o, 0, sib).wait_recv()

                @pl.when(j < n - 1)
                def _():
                    self.copy(block, o, 0, c + 2).start()

                self.copy(block, o, 2, sib).start()

            @pl.when(j + s <= n - 1)
            def _():
                o = j + s
                block = self.full.at[2 * o + k]
                self.copy(block, o, 1, sib).wait_recv()

                @pl.when(j > 0)
                def _():
                    self.copy(block, o, 1, c - 2).start()

                self.copy(block, o, 2, sib).start()

    def finish(self):
        c, j, k, n, sib = place(self.cn)
        for o in range(n):
            block = self.full.at[2 * o + 1 - k]
            remote(
                block, block, self.sem.at[2, o], self.sem.at[4, o], {"ctx": sib}
            ).wait_recv()
        for o in range(n):
            block = self.full.at[2 * o + k]

            @pl.when((j < n - 1) & (o <= j))
            def _():
                self.copy(block, o, 0, sib).wait_send()

            @pl.when((j > 0) & (o >= j))
            def _():
                self.copy(block, o, 1, sib).wait_send()

            self.copy(block, o, 2, sib).wait_send()


class Swap:
    def __init__(self, cn, src, dst, sem, local):
        self.cn, self.src, self.dst, self.sem, self.local = cn, src, dst, sem, local

    def copy(self, s):
        c = lax.axis_index("ctx")
        peer = lax.rem(c + s, self.cn)
        return remote(
            self.src.at[peer],
            self.dst.at[c],
            self.sem.at[0, s],
            self.sem.at[1, s],
            {"ctx": peer},
        )

    def start(self):
        c = lax.axis_index("ctx")
        for s in range(1, self.cn):
            self.copy(s).start()
        pltpu.make_async_copy(self.src.at[c], self.dst.at[c], self.local).start()

    def finish(self):
        c = lax.axis_index("ctx")
        pltpu.make_async_copy(self.src.at[c], self.dst.at[c], self.local).wait()
        for s in range(1, self.cn):
            source = lax.rem(c - s + self.cn, self.cn)
            block = self.dst.at[source]
            remote(
                block, block, self.sem.at[0, s], self.sem.at[1, s], {"ctx": source}
            ).wait_recv()
            self.copy(s).wait_send()


class LineSum:
    def __init__(self, cn, compute, part, cross, cross_in, flow, arrived, sem):
        self.cn, self.compute, self.part = cn, compute, part
        self.cross, self.cross_in, self.flow = cross, cross_in, flow
        self.arrived, self.sem = arrived, sem

    def across(self, t):
        _, _, _, _, sib = place(self.cn)
        return remote(
            self.cross.at[t],
            self.cross_in.at[t],
            self.sem.at[0, t],
            self.sem.at[2, t],
            {"ctx": sib},
        )

    def along(self, t, slot, target):
        return remote(
            self.flow.at[t],
            self.arrived.at[slot],
            self.sem.at[1, t],
            self.sem.at[3, slot],
            {"ctx": target},
        )

    def produce(self, t, slot):
        _, _, k, _, _ = place(self.cn)
        part = self.part.at[slot]
        self.compute(t, part)
        self.cross[t] = part[1 - k].astype(bf16)
        self.across(t).start()

    def collect(self, t, slot):
        _, j, k, n, sib = place(self.cn)
        part = self.part.at[slot, k]
        self.across(t).wait_recv()
        part[...] += self.cross_in[t].astype(f32)

        @pl.when((j > 0) & (t >= j))
        def _():
            self.along(t, t, sib).wait_recv()
            part[...] += self.arrived[t].astype(f32)

        @pl.when((j < n - 1) & (t <= j))
        def _():
            slot_in = jnp.where(t == j, n, t)
            self.along(t, slot_in, sib).wait_recv()
            part[...] += self.arrived[slot_in].astype(f32)

    def send(self, t, slot, up):
        c, j, k, n, _ = place(self.cn)
        self.flow[t] = self.part[slot, k].astype(bf16)
        there = t if up else jnp.where(t == j - 1, n, t)
        self.along(t, there, c + 2 if up else c - 2).start()

    def drain(self):
        _, j, _, n, sib = place(self.cn)

        @pl.loop(0, n)
        def _(t):
            self.across(t).wait_send()

            @pl.when(t != j)
            def _():
                self.along(t, t, sib).wait_send()


def line_sums(cn, sums):
    _, j, _, n, _ = place(cn)

    @pl.loop(0, n - 1)
    def _(i):
        for total in sums:

            @pl.when(n - 1 - i > j)
            def _():
                total.produce(n - 1 - i, 0)

            @pl.when(i < j)
            def _():
                total.produce(i, 1)

        for total in sums:

            @pl.when(n - 1 - i > j)
            def _():
                total.collect(n - 1 - i, 0)
                total.send(n - 1 - i, 0, True)

            @pl.when(i < j)
            def _():
                total.collect(i, 1)
                total.send(i, 1, False)

    for total in sums:
        total.produce(j, 0)
    for total in sums:
        total.collect(j, 0)


def sum_scratch(cn, rows, width):
    n = cn // 2
    return [
        pltpu.VMEM((2, 2, rows, width), f32),
        pltpu.VMEM((n, rows, width), bf16),
        pltpu.VMEM((n, rows, width), bf16),
        pltpu.VMEM((n, rows, width), bf16),
        pltpu.VMEM((n + 1, rows, width), bf16),
        pltpu.SemaphoreType.DMA((4, n + 1)),
    ]


def product(a_ref, b_ref, dims, rows, width):
    tile = min(512, width)

    def compute(t, out):
        a = a_ref[pl.ds(pl.multiple_of(t * 2 * rows, 2 * rows), 2 * rows), :]

        @pl.loop(0, width // tile)
        def _(i):
            at = pl.ds(pl.multiple_of(i * tile, tile), tile)
            b = b_ref[:, at] if dims == plain else b_ref[at, :]
            out[:, :, at] = dot(a, b, dims).reshape(2, rows, tile)

    return compute


def rms(v):
    return lax.rsqrt(jnp.mean(v * v, axis=-1, keepdims=True) + norm_eps)


def front_kernel(cn, x, pack, x_all, pack_all, gsem, ssem, local):
    greet_ctx(cn)
    pl.semaphore_wait(pltpu.get_barrier_semaphore(), cn - 1)
    c = lax.axis_index("ctx")
    swap = Swap(cn, pack, pack_all, ssem, local.at[0])
    gather = LineGather(cn, x, x_all, gsem)
    swap.start()
    gather.start()
    keep = pltpu.make_async_copy(x, x_all.at[c], local.at[1])
    keep.start()
    gather.forward()
    keep.wait()
    swap.finish()
    gather.finish()


def spread_kernel(cn, dpn, pack, wo, pack_all, wo_all, ssem, osem, local):
    c, d = lax.axis_index("ctx"), lax.axis_index("dp")
    greet_ctx(cn)
    for r in range(dpn):
        g = c * dpn + r
        src_d, src_c = g // cn, lax.rem(g, cn)

        @pl.when((src_d != d) | (src_c != c))
        def _():
            greet({"dp": src_d, "ctx": src_c})

    mine = d * cn + c
    home, slot = mine // dpn, lax.rem(mine, dpn)
    outs = jnp.where(home == c, dpn - 1, dpn)
    pl.semaphore_wait(pltpu.get_barrier_semaphore(), cn - 1 + outs)
    swap = Swap(cn, pack, pack_all, ssem, local.at[0])
    swap.start()

    def copy(to):
        return remote(
            wo,
            wo_all.at[slot],
            osem.at[0, to],
            osem.at[1, slot],
            {"dp": to, "ctx": home},
        )

    def own():
        return pltpu.make_async_copy(wo, wo_all.at[slot], local.at[1])

    for to in range(dpn):
        self_target = (home == c) & (d == to)

        @pl.when(jnp.logical_not(self_target))
        def _():
            copy(to).start()

        @pl.when(self_target)
        def _():
            own().start()

    swap.finish()
    for r in range(dpn):
        g = c * dpn + r
        local_piece = g == mine

        @pl.when(jnp.logical_not(local_piece))
        def _():
            block = wo_all.at[r]
            remote(
                block, block, osem.at[0, r], osem.at[1, r], {"dp": d, "ctx": c}
            ).wait_recv()

        @pl.when(local_piece)
        def _():
            own().wait()

    for to in range(dpn):

        @pl.when(jnp.logical_not((home == c) & (d == to)))
        def _():
            copy(to).wait_send()


def middle_kernel(cn, o, wo, x, gain, h1, bn_all, own, gsem, lsem, *scratch):
    greet_line(cn)
    c, _, k, _, _ = place(cn)
    rows, width = x.shape
    total = LineSum(cn, product(o, wo, plain, rows, width), *scratch)
    line_sums(cn, [total])
    mid = x[...].astype(f32) + total.part[0, k]
    h1[...] = mid
    own[...] = (mid * rms(mid) * gain[...]).astype(bf16)
    gather = LineGather(cn, own, bn_all, gsem)
    gather.start()
    keep = pltpu.make_async_copy(own, bn_all.at[c], lsem)
    keep.start()
    gather.forward()
    keep.wait()
    gather.finish()
    total.drain()


def back_kernel(
    cn, dgu, w, h1, dy, gain, dh1, dob_all, term, own, gsem, lsem, *scratch
):
    greet_line(cn)
    c, _, k, _, _ = place(cn)
    rows, width = dy.shape
    total = LineSum(cn, product(dgu, w, contract_cols, rows, width), *scratch)
    line_sums(cn, [total])
    dbn = total.part[0, k]
    mid = h1[...]
    r2 = rms(mid)
    xh2 = mid * r2
    term[...] = jnp.sum(dbn * xh2, axis=0, keepdims=True)
    u2 = dbn * gain[...]
    grad = dy[...].astype(f32) + r2 * (u2 - xh2 * jnp.mean(u2 * xh2, axis=-1, keepdims=True))
    dh1[...] = grad
    own[...] = grad.astype(bf16)
    gather = LineGather(cn, own, dob_all, gsem)
    gather.start()
    keep = pltpu.make_async_copy(own, dob_all.at[c], lsem)
    keep.start()
    gather.forward()
    keep.wait()
    gather.finish()
    total.drain()


def last_kernel(
    cn, dqkv, w, dh1, x, gain, hid, down, h1, grad_in, result, term, *scratch
):
    greet_line(cn)
    _, _, k, _, _ = place(cn)
    rows, width = x.shape
    half = len(scratch) // 2
    dan_sum = LineSum(cn, product(dqkv, w, contract_cols, rows, width), *scratch[:half])
    res_sum = LineSum(cn, product(hid, down, plain, rows, width), *scratch[half:])
    line_sums(cn, [dan_sum, res_sum])
    result[...] = (h1[...] + res_sum.part[0, k]).astype(bf16)
    dan = dan_sum.part[0, k]
    xf = x[...].astype(f32)
    r1 = rms(xf)
    xh1 = xf * r1
    term[...] = jnp.sum(dan * xh1, axis=0, keepdims=True)
    u1 = dan * gain[...]
    grad = dh1[...] + r1 * (u1 - xh1 * jnp.mean(u1 * xh1, axis=-1, keepdims=True))
    grad_in[...] = grad.astype(bf16)
    dan_sum.drain()
    res_sum.drain()


def return_kernel(
    cn, dpn, qkv, gu, go, tot, qkv_all, gu_all, go_all, tot_out,
    tot_in, tot_sum, tot_last, qsem, usem, osem, tsem, dsem, local,
):
    c, d = lax.axis_index("ctx"), lax.axis_index("dp")
    mine = d * cn + c
    home, slot = mine // dpn, lax.rem(mine, dpn)
    greet_ctx(cn)
    for s in range(1, dpn):
        greet({"dp": lax.rem(d + s, dpn)})
    for s in range(dpn):

        @pl.when((home != c) | (d != s))
        def _():
            greet({"dp": s, "ctx": home})

    self_sends = jnp.where(home == c, dpn - 1, dpn)
    pl.semaphore_wait(pltpu.get_barrier_semaphore(), cn - 1 + dpn - 1 + self_sends)
    totals = Swap(cn, tot, tot_in, tsem, local.at[0])
    totals.start()
    first = Swap(cn, qkv, qkv_all, qsem, local.at[1])
    first.start()

    def copy(r):
        g = c * dpn + r
        return remote(
            go.at[r],
            go_all.at[d],
            osem.at[0, r],
            osem.at[1, d],
            {"dp": g // cn, "ctx": lax.rem(g, cn)},
        )

    def own(r):
        return pltpu.make_async_copy(go.at[r], go_all.at[d], local.at[2])

    for r in range(dpn):
        here = c * dpn + r == mine

        @pl.when(jnp.logical_not(here))
        def _():
            copy(r).start()

        @pl.when(here)
        def _():
            own(r).start()

    second = Swap(cn, gu, gu_all, usem, local.at[3])
    second.start()
    totals.finish()
    tot_sum[...] = jnp.sum(tot_in[...], axis=0)

    def share(s):
        peer = lax.rem(d + s, dpn)
        return remote(
            tot_sum.at[peer], tot_last.at[d], dsem.at[0, s], dsem.at[1, s], {"dp": peer}
        )

    for s in range(1, dpn):
        share(s).start()
    tot_last[d] = tot_sum[d]
    for s in range(1, dpn):
        source = lax.rem(d - s + dpn, dpn)
        block = tot_last.at[source]
        remote(
            block, block, dsem.at[0, s], dsem.at[1, s], {"dp": source}
        ).wait_recv()
    for s in range(1, dpn):
        share(s).wait_send()
    tot_out[...] = jnp.sum(tot_last[...], axis=0)
    for s in range(dpn):
        block = go_all.at[s]
        here = (home == c) & (d == s)

        @pl.when(jnp.logical_not(here))
        def _():
            remote(
                block, block, osem.at[0, s], osem.at[1, s], {"dp": s, "ctx": home}
            ).wait_recv()

        @pl.when(here)
        def _():
            own(slot).wait()

    for r in range(dpn):

        @pl.when(c * dpn + r != mine)
        def _():
            copy(r).wait_send()

    first.finish()
    second.finish()


def call(kernel, outs, ins, specs_in, specs_out, scratch, number, flops=0, moved=0):
    return pl.pallas_call(
        kernel,
        out_shape=outs,
        in_specs=specs_in,
        out_specs=specs_out,
        scratch_shapes=scratch,
        compiler_params=pltpu.CompilerParams(
            collective_id=number, has_side_effects=True, vmem_limit_bytes=60 * 2**20
        ),
        cost_estimate=pl.CostEstimate(flops=flops, bytes_accessed=moved, transcendentals=0),
    )(*ins)


def shape(dims, dtype=bf16):
    return jax.ShapeDtypeStruct(dims, dtype)


def rope_tables(positions):
    half_dim = HEAD_DIM // 2
    inverse = jnp.exp(
        jnp.arange(half_dim, dtype=f32) * (-2.0 * math.log(rope_base) / HEAD_DIM)
    )
    angles = positions[:, None] * inverse[None, :]
    return jnp.cos(angles), jnp.sin(angles)


def rotate(values, cosines, sines, sign):
    half = HEAD_DIM // 2
    parts = []
    for h in range(values.shape[1] // HEAD_DIM):
        a = values[:, h * HEAD_DIM : h * HEAD_DIM + half]
        b = values[:, h * HEAD_DIM + half : (h + 1) * HEAD_DIM]
        parts += [a * cosines - sign * b * sines, b * cosines + sign * a * sines]
    return jnp.concatenate(parts, axis=1)


def gather(v, axes, axis=0):
    return lax.all_gather(v, axes, axis=axis, tiled=True)


def scatter_sum(v, axes):
    return lax.psum_scatter(v, axes, scatter_dimension=0, tiled=True)


def shards(
    hidden_in,
    out_grad,
    seg_ids,
    valid_mask,
    w_query,
    w_key,
    w_value,
    w_output,
    w_gate,
    w_up,
    w_down,
    gain_attn,
    gain_mlp,
):
    dpn = lax.axis_size("dp")
    cn = lax.axis_size("ctx")
    n = cn // 2
    x_local = hidden_in[0]
    dy_local = out_grad[0]
    rows, width = x_local.shape
    seq = rows * cn
    dr = w_query.shape[0]
    hw = width // cn
    heads = hw // HEAD_DIM
    ff_rows = w_down.shape[0]
    ff = ff_rows * dpn
    dma = pltpu.SemaphoreType.DMA
    mib = 2**20

    code = (seg_ids[0] * 2 + valid_mask[0]).astype(bf16)
    x_ext = jnp.concatenate([x_local, jnp.broadcast_to(code[:, None], (rows, 128))], axis=1)
    lanes = jnp.arange(128)[None, :]
    gain_cols = jnp.where(lanes == 0, gain_attn[:, None], gain_mlp[:, None]).astype(bf16)
    qkv_pack = jnp.concatenate(
        [w.astype(bf16).reshape(dr, cn, hw) for w in (w_query, w_key, w_value)]
        + [jnp.broadcast_to(gain_cols[:, None, :], (dr, cn, 128))],
        axis=2,
    ).transpose(1, 0, 2)
    pw = 3 * hw + 128
    x_all, qkv_rows = call(
        functools.partial(front_kernel, cn),
        (shape((cn, rows, width + 128)), shape((cn, dr, pw))),
        (x_ext, qkv_pack),
        [ANY] * 2,
        (ANY, ANY),
        [dma((5, n)), dma((2, cn)), dma((2,))],
        1,
        moved=160 * mib,
    )
    down = gather(w_down.astype(bf16), "dp")
    dys = gather(dy_local, "ctx")
    qkv_full = gather(qkv_rows.reshape(cn * dr, pw), "dp")
    qkv = qkv_full[:, : 3 * hw]
    gain_one = qkv_full[:, 3 * hw].astype(f32)[None]
    gain_two = qkv_full[:, 3 * hw + 1].astype(f32)[None]

    gu_pack = (
        jnp.concatenate(
            [w.astype(bf16).reshape(dr, dpn, cn, ff_rows) for w in (w_gate, w_up)], axis=1
        )
        .transpose(2, 0, 1, 3)
        .reshape(cn, dr, 2 * ff)
    )
    gu_rows, wo = call(
        functools.partial(spread_kernel, cn, dpn),
        (shape((cn, dr, 2 * ff)), shape((dpn, dr, width))),
        (gu_pack, w_output.astype(bf16)),
        [ANY] * 2,
        (ANY, ANY),
        [dma((2, cn)), dma((2, dpn)), dma((2,))],
        2,
        moved=200 * mib,
    )
    gate_up = gather(gu_rows.reshape(cn * dr, 2 * ff), "dp")
    wo = wo.reshape(hw, width)

    all_codes = x_all[:, :, width].reshape(seq).astype(jnp.int32)
    seg = all_codes // 2
    valid = all_codes % 2
    index = jnp.arange(seq, dtype=jnp.int32)
    starts = jnp.sum((seg[None, :] < seg[:, None]).astype(jnp.int32), axis=1)
    cosines, sines = rope_tables((index - starts).astype(f32))
    allowed = (
        (seg[:, None] == seg[None, :])
        & (index[None, :] <= index[:, None])
        & (valid[None, :] == 1)
    )

    xs = x_all[:, :, :width].reshape(seq, width).astype(f32)
    an = (xs * rms(xs) * gain_one).astype(bf16)
    proj = dot(an, qkv)
    q = rotate(proj[:, :hw], cosines, sines, 1.0).astype(bf16)
    k = rotate(proj[:, hw : 2 * hw], cosines, sines, 1.0).astype(bf16)
    v = proj[:, 2 * hw :].astype(bf16)

    def per_head(t, h):
        return t[:, h * HEAD_DIM : (h + 1) * HEAD_DIM]

    outs = []
    mass = jnp.zeros((seq,), f32)
    for h in range(heads):
        s = dot(per_head(q, h), per_head(k, h), contract_cols) * score_scale - score_shift
        p = jnp.where(allowed, jax.nn.sigmoid(s), 0.0)
        mass = mass + jnp.sum(p, axis=1)
        outs.append(dot(p.astype(bf16), per_head(v, h)))
    o = jnp.concatenate(outs, axis=1).astype(bf16)

    line_scratch = sum_scratch(cn, rows, width)
    h1, bn = call(
        functools.partial(middle_kernel, cn),
        (shape((rows, width), f32), shape((cn, rows, width))),
        (o, wo, x_local, gain_two),
        [VMEM] * 4,
        (VMEM, ANY),
        [pltpu.VMEM((rows, width), bf16), dma((5, n)), dma] + line_scratch,
        3,
        moved=240 * mib,
    )
    bn = bn.reshape(seq, width)
    gu = dot(bn, gate_up)
    gate = gu[:, :ff]
    up = gu[:, ff:]
    sig = jax.nn.sigmoid(gate)
    silu = gate * sig
    hid = (silu * up).astype(bf16)
    dhid = dot(dys, down, contract_cols)
    dgate = (dhid * up * sig * (1.0 + gate * (1.0 - sig))).astype(bf16)
    dup = (dhid * silu).astype(bf16)
    dgu = jnp.concatenate([dgate, dup], axis=1)
    g_gu = scatter_sum(dot(bn, dgu, contract_rows).astype(bf16), "dp")
    g_down = scatter_sum(dot(hid, dys, contract_rows).astype(bf16), "dp")
    dh1, dob, term_two = call(
        functools.partial(back_kernel, cn),
        (shape((rows, width), f32), shape((cn, rows, width)), shape((1, width), f32)),
        (dgu, gate_up, h1, dy_local, gain_two),
        [VMEM] * 5,
        (VMEM, ANY, VMEM),
        [pltpu.VMEM((rows, width), bf16), dma((5, n)), dma] + line_scratch,
        4,
        moved=240 * mib,
    )
    dob = dob.reshape(seq, width)
    do = dot(dob, wo, contract_cols).astype(bf16)
    dqs, dks, dvs = [], [], []
    for h in range(heads):
        qh, kh, vh, doh = (per_head(t, h) for t in (q, k, v, do))
        s = dot(qh, kh, contract_cols) * score_scale - score_shift
        sg = jnp.where(allowed, jax.nn.sigmoid(s), 0.0)
        pb = sg.astype(bf16)
        ds = (dot(doh, vh, contract_cols) * sg * (1.0 - sg)).astype(bf16)
        dqs.append(dot(ds, kh) * score_scale)
        dks.append(dot(ds, qh, contract_rows) * score_scale)
        dvs.append(dot(pb, doh, contract_rows))
    dq = rotate(jnp.concatenate(dqs, axis=1), cosines, sines, -1.0).astype(bf16)
    dk = rotate(jnp.concatenate(dks, axis=1), cosines, sines, -1.0).astype(bf16)
    dv = jnp.concatenate(dvs, axis=1).astype(bf16)
    dqkv = jnp.concatenate([dq, dk, dv], axis=1)
    g_qkv = scatter_sum(dot(an, dqkv, contract_rows).astype(bf16), "dp")
    g_out = dot(o, dob, contract_rows).astype(bf16)
    grad_input, result, term_one = call(
        functools.partial(last_kernel, cn),
        (shape((rows, width)), shape((rows, width)), shape((1, width), f32)),
        (dqkv, qkv, dh1, x_local, gain_one, hid, down, h1),
        [VMEM] * 8,
        (VMEM, VMEM, VMEM),
        line_scratch + line_scratch,
        5,
        moved=240 * mib,
    )

    mass_part = jnp.sum(valid.astype(f32) * mass) / (heads * cn)
    pieces = [t.reshape(dpn, cn, dr).transpose(1, 0, 2) for t in (term_one, term_two)]
    pieces.append(jnp.broadcast_to(mass_part, (cn, dpn, dr)))
    tot = jnp.zeros((cn, dpn, 8, 128), f32).at[:, :, :3, :dr].set(jnp.stack(pieces, axis=2))
    q_all, u_all, o_all, totals = call(
        functools.partial(return_kernel, cn, dpn),
        (
            shape((cn, dr, 3 * hw)),
            shape((cn, dr, 2 * ff)),
            shape((dpn, dr, width)),
            shape((8, 128), f32),
        ),
        (
            g_qkv.reshape(cn, dr, 3 * hw),
            g_gu.reshape(cn, dr, 2 * ff),
            g_out.reshape(dpn, dr, width),
            tot,
        ),
        [ANY] * 3 + [VMEM],
        (ANY, ANY, ANY, VMEM),
        [
            pltpu.VMEM((cn, dpn, 8, 128), f32),
            pltpu.VMEM((dpn, 8, 128), f32),
            pltpu.VMEM((dpn, 8, 128), f32),
            dma((2, cn)),
            dma((2, cn)),
            dma((2, dpn)),
            dma((2, cn)),
            dma((2, dpn)),
            dma((4,)),
        ],
        6,
        moved=240 * mib,
    )
    q_all = q_all.astype(f32)
    u_all = u_all.astype(f32)
    g_q, g_k, g_v = (
        q_all[:, :, i * hw : (i + 1) * hw].transpose(1, 0, 2).reshape(dr, width) for i in range(3)
    )
    g_gate, g_up = (
        u_all[:, :, i * ff : (i + 1) * ff]
        .reshape(cn, dr, dpn, ff_rows)
        .transpose(1, 2, 0, 3)
        .reshape(dr, dpn * cn * ff_rows)
        for i in range(2)
    )
    mass_mean = totals[2, 0] / (dpn * seq)
    return (
        result[None],
        grad_input[None],
        g_q,
        g_k,
        g_v,
        jnp.sum(o_all.astype(f32), axis=0),
        g_gate,
        g_up,
        g_down.astype(f32),
        totals[0, :dr],
        totals[1, :dr],
        mass_mean,
    )


def solution(mesh):
    tok = P("dp", "ctx", None)
    ids = P("dp", "ctx")
    mat = P(("dp", "ctx"), None)
    vec = P(("dp", "ctx"))
    return jax.shard_map(
        shards,
        mesh=mesh,
        in_specs=(tok, tok, ids, ids) + (mat,) * 7 + (vec, vec),
        out_specs=(tok, tok) + (mat,) * 7 + (vec, vec, P()),
        check_vma=False,
    )
```

time: 1130 us -> 812 us (0.72); the launches traced: 1110 us -> 807 us
  waiting for transfers between devices: 625 us -> 30.6 us
  Pallas kernels: 0 us -> 577 us
  blocking collectives: 266 us -> 0 us
  matrix products: 116 us -> 85.7 us
  other arithmetic: 39.3 us -> 51.5 us
    pallas_call x0 -> x6, Pallas kernels: none -> 577 us  [call(): pl.pallas_call(kernel, out_shape=outs, in_specs=specs_in, out_specs=specs...]
    reduce_scatter x8 -> x3, waiting for transfers between devices: 300 us -> 0.01 us  [scatter_sum(): return lax.psum_scatter(v, axes, scatter_dimension=0, tiled=True)]
    all_gather x8 -> x4, waiting for transfers between devices: 323 us -> 30 us  [gather(): return lax.all_gather(v, axes, axis=axis, tiled=True)]
    all_to_all x3 -> x0, blocking collectives: 171 us -> none  [swap(): return lax.all_to_all(v, axes, split_axis=0, concat_axis=0, tiled=True)]
    all_gather x2 -> x0, blocking collectives: 53.5 us -> none  [gather(): return lax.all_gather(v, axes, axis=axis, tiled=True)]
    psum x1 -> x0, blocking collectives: 41.5 us -> none  [shards(): lax.psum((term_one, term_two, jnp.sum(valid.astype(f32) * mass) / (heads...]
    dot_general x24 -> x20, matrix products: 116 us -> 85.7 us  [dot(): return lax.dot_general(a, b, dims, preferred_element_type=f32)]
  transfers between devices with their start and end apart: 17 -> 7, of which waited for: 13 -> 1; matrix products, arithmetic and copies ran while one was open for 13% -> 16% of each run, Pallas kernels for 0% -> 52%
where the time goes in v2:
time: 812 us; the launch traced here: 807 us
  Pallas kernels  577 us (71%)
  matrix products  85.7 us (11%)
  other arithmetic  51.5 us (6%)
  local copies, waits for them, and re-layouts  43.5 us (5%)
  waiting for transfers between devices  30.6 us (4%)
  between operations  17.8 us (2%)
    pallas_call x6, Pallas kernels, call(): pl.pallas_call(kernel, out_shape=outs, in_specs=specs_in, out_specs=specs...  577 us
    dot_general x20, matrix products, dot(): return lax.dot_general(a, b, dims, preferred_element_type=f32)  85.7 us
    all_gather x4, waiting for transfers between devices, gather(): return lax.all_gather(v, axes, axis=axis, tiled=True)  30 us
    unnamed x97, local copies, waits for them, and re-layouts  17 us
  transfers between devices with their start and end apart: 7, of which 1 were waited for; matrix products, arithmetic and copies ran while one was open for 16% of the time, Pallas kernels for 52%

profile of v2, /device:TPU:9, one launch (start us, length us, event | category | flops | bytes accessed | tf_op | source)
XLA Modules:
  0.0 806.9 jit_solution(15534673623389235321)
XLA Ops:
  13.6 59.9 %shard_map.220 = (bf16[8,128,2176]{2,1,0:T(8,128)(2,1)}, bf16[8,64,896]{2,1,0:T(8,128)(2,1)}) custom-call(bf16[128,2176]{1,0:T(8,128)(2,1)} %pad_maximum_fusion.1.x, bf16[8,64,896]{2,1,0:T(8,128)(2,1)} %maximum_bitcast_fusion.1.pack), custom_call_target="tpu_custom_call" | custom-call | bytes 167772160 | tf_op jit(solution)/shard_map/pallas_call | solution.py:560
  79.5 110.3 %shard_map.221 = (bf16[8,64,2048]{2,1,0:T(8,128)(2,1)}, bf16[4,64,2048]{2,1,0:T(8,128)(2,1)}) custom-call(bf16[8,64,2048]{2,1,0:T(8,128)(2,1)} %reshape.332.pack, bf16[64,2048]{1,0:T(8,128)(2,1)} %convert_element_type.194.wo), custom_call_target="tpu_custom_call" | custom-call | bytes 209715200 | tf_op jit(solution)/shard_map/pallas_call | solution.py:560
  193.1 3.1 multiply_reduce_fusion
  196.7 7.5 slice_convert_fusion
  206.5 4.3 fusion.1
  211.0 4.9 fusion.106
  221.9 4.3 fusion.57
  236.4 99.6 %shard_map.222 = (f32[128,2048]{1,0:T(8,128)}, bf16[8,128,2048]{2,1,0:T(8,128)(2,1)}) custom-call(bf16[1024,256]{1,0:T(8,128)(2,1)} %pad_maximum_fusion.2.o, bf16[256,2048]{1,0:T(8,128)(2,1)} %bitcast.148, bf16[128,2048]{1,0:T(8,128)(2,1)} %bitcast.134, f32[1,2048]{1,0:T(1,128)} %bitcast.161), custom_call_target="tpu_custom_call" | custom-call | bytes 251658240 | tf_op jit(solution)/shard_map/pallas_call | solution.py:560
  336.0 14.5 %fusion.109 = f32[1024,2048]{1,0:T(8,128)} fusion(bf16[1024,2048]{1,0:T(8,128)(2,1)} %bitcast.167, bf16[2048,2048]{1,0:T(8,128)(2,1)} %all-gather.10.cloned.1.call-done.w), kind=kOutput, calls=%fused_computation.175 | convolution fusion | flops 8589934592 | bytes 20971520 | tf_op jit(solution)/shard_map/dot_general | solution.py:27
  350.5 30.0 %all-gather.12.cloned.1.call-done = bf16[1,1024,2048]{2,1,0:T(8,128)(2,1)} async-done(((bf16[1,128,2048]{2,1,0:T(8,128)(2,1)}), bf16[1,1024,2048]{2,1,0:T(8,128)(2,1)}) %all-gather.12.cloned.1.call-update) | async-done | bytes 4194320 | tf_op jit(solution)/shard_map/all_gather | solution.py:597
  380.5 13.3 %multiply_convert_fusion.4 = (bf16[1024,1024]{1,0:T(8,128)(2,1)S(1)}, bf16[1024,1024]{1,0:T(8,128)(2,1)}, bf16[1024,1024]{1,0:T(8,128)(2,1)S(1)}) fusion(f32[1024,2048]{1,0:T(8,128)} %fusion.109, bf16[1024,2048]{1,0:T(8,128)(2,1)} %all-gather.6.cloned.1.call-done.down, bf16[1,1024,2048]{2,1,0:T(8,128)(2,1)} %all-gather.12.cloned.1.call-done), kind=kOutput, calls=%fused_computation.14 | convolution fusion | flops 4310695936 | bytes 23068672 | tf_op jit(solution)/shard_map/dot_general | solution.py:27
  395.1 6.3 fusion.9
  401.5 4.1 pad_maximum_fusion.dgu
  405.6 107.4 %shard_map.223 = (f32[128,2048]{1,0:T(8,128)}, bf16[8,128,2048]{2,1,0:T(8,128)(2,1)}, f32[1,2048]{1,0:T(1,128)}) custom-call(bf16[1024,2048]{1,0:T(8,128)(2,1)} %pad_maximum_fusion.dgu, bf16[2048,2048]{1,0:T(8,128)(2,1)} %all-gather.10.cloned.1.call-done.w, f32[128,2048]{1,0:T(8,128)} %get-tuple-element.45.h1, bf16[128,2048]{1,0:T(8,128)(2,1)} %bitcast.141, ...), custom_call_target="tpu_custom_call" | custom-call | bytes 251658240 | tf_op jit(solution)/shard_map/pallas_call | solution.py:560
  513.0 3.6 convolution_convert_fusion.3
  524.3 3.6 fusion.79
  533.3 8.0 convolution_convert_fusion.1
  541.5 14.1 %convolution_convert_fusion = bf16[2048,2048]{1,0:T(8,128)(2,1)} fusion(bf16[1024,2048]{1,0:T(8,128)(2,1)} %bitcast.168, bf16[1024,1024]{1,0:T(8,128)(2,1)} %get-tuple-element.59, bf16[1024,1024]{1,0:T(8,128)(2,1)} %copy-done.13), kind=kOutput, calls=%fused_computation.4 | convolution fusion | flops 8602517504 | bytes 16777216 | tf_op jit(solution)/shard_map/dot_general | solution.py:27
  558.5 3.9 slice.199.w
  563.6 104.0 %shard_map.224 = (bf16[128,2048]{1,0:T(8,128)(2,1)}, bf16[128,2048]{1,0:T(8,128)(2,1)}, f32[1,2048]{1,0:T(1,128)}) custom-call(bf16[1024,768]{1,0:T(8,128)(2,1)} %copy-done.5, bf16[2048,768]{1,0:T(8,128)(2,1)} %slice.199.w, f32[128,2048]{1,0:T(8,128)} %get-tuple-element.47.dh1, bf16[128,2048]{1,0:T(8,128)(2,1)} %bitcast.135, f32[1,2048]{1,0:T(1,128)} %bitcast.160, ...), custom_call_target="tpu_custom_call" | custom-call | bytes 251658240 | tf_op jit(solution)/shard_map/pallas_call | solution.py:560
  669.9 4.5 convolution_convert_fusion.2
  674.4 2.8 convert_element_type.214
  677.2 95.9 %shard_map.225 = (bf16[8,64,768]{2,1,0:T(8,128)(2,1)}, bf16[8,64,2048]{2,1,0:T(8,128)(2,1)}, bf16[4,64,2048]{2,1,0:T(8,128)(2,1)}, f32[8,128]{1,0:T(8,128)}) custom-call(bf16[8,64,768]{2,1,0:T(8,128)(2,1)} %bitcast.154, bf16[8,64,2048]{2,1,0:T(8,128)(2,1)} %bitcast.143, bf16[4,64,2048]{2,1,0:T(8,128)(2,1)} %bitcast.152, f32[8,4,8,128]{3,2,1,0:T(8,128)} %scatter.4.tot), custom_call_target="tpu_custom_call" | custom-call | bytes 251658240 | tf_op jit(solution)/shard_map/pallas_call | solution.py:560
  793.7 2.5 copy.143
  (184 shorter events, 77.0 us)
Async XLA Ops:
  7.2 4.4 copy-start.7
  7.2 5.3 copy-start.38
  7.2 5.3 copy-start.39
  7.2 197.0 %all-gather.8.cloned.1.call-start = ((), (), s32[]{:S(2)}) async-start(), calls=%async_computation.4 | async-start | bytes 4587520 | tf_op jit(solution)/shard_map/all_gather | solution.py:597
  8.4 65.2 %copy-start.33 = (f32[64,2048]{1,0:T(8,128)S(1)}, f32[64,2048]{1,0:T(8,128)}, u32[]{:S(2)}) copy-start(f32[64,2048]{1,0:T(8,128)} %param.22) | copy-start | bytes 1572868
  9.6 64.8 %copy-start.9 = (f32[64,8192]{1,0:T(8,128)S(1)}, f32[64,8192]{1,0:T(8,128)}, u32[]{:S(2)}) copy-start(f32[64,8192]{1,0:T(8,128)} %param.23) | copy-start | bytes 6291460
  73.5 262.5 %all-gather.10.cloned.1.call-start = ((), (), s32[]{:S(2)}) async-start(), calls=%async_computation.5 | async-start | bytes 10485760 | tf_op jit(solution)/shard_map/all_gather | solution.py:597
  79.5 110.3 %copy-start.11 = (f32[256,2048]{1,0:T(8,128)S(1)}, f32[256,2048]{1,0:T(8,128)}, u32[]{:S(2)}) copy-start(f32[256,2048]{1,0:T(8,128)} %param.25) | copy-start | bytes 6291460
  189.8 160.7 %all-gather.6.cloned.1.call-start = ((), (), s32[]{:S(2)}) async-start(), calls=%async_computation.3 | async-start | bytes 5242880 | tf_op jit(solution)/shard_map/all_gather | solution.py:597
  191.0 189.5 %all-gather.12.cloned.1.call-start = ((), (), s32[]{:S(2)}) async-start(), calls=%async_computation.9 | async-start | bytes 4718592 | tf_op jit(solution)/shard_map/all_gather | solution.py:597
  191.6 482.8 %reduce-scatter.8.cloned.1.call-start = ((), (), s32[]{:S(2)}) async-start(), calls=%async_computation.8 | async-start | bytes 5242880 | tf_op jit(solution)/shard_map/reduce_scatter | solution.py:601
  206.5 4.4 copy-start.6
  211.0 4.9 copy-start.8
  229.8 5.6 copy-start.29
  380.5 14.6 %copy-start.40 = (bf16[1,1024,2048]{2,1,0:T(8,128)(2,1)S(1)}, bf16[1,1024,2048]{2,1,0:T(8,128)(2,1)}, u32[]{:S(2)}) copy-start(bf16[1,1024,2048]{2,1,0:T(8,128)(2,1)} %all-gather.12.cloned.1.call-done) | copy-start | bytes 12582916
  393.8 7.7 copy-start.13
  401.4 275.8 %reduce-scatter.4.cloned.1.call-start = ((), (), s32[]{:S(2)}) async-start(), calls=%async_computation.6 | async-start | bytes 3932160 | tf_op jit(solution)/shard_map/reduce_scatter | solution.py:601
  405.6 107.4 %copy-start.28 = (bf16[4,64,2048]{2,1,0:T(8,128)(2,1)S(1)}, bf16[4,64,2048]{2,1,0:T(8,128)(2,1)}, u32[]{:S(2)}) copy-start(bf16[4,64,2048]{2,1,0:T(8,128)(2,1)} %get-tuple-element.42) | copy-start | bytes 3145732
  533.2 8.0 copy-start.5
  541.3 135.9 %reduce-scatter.6.cloned.1.call-start = ((), (), s32[]{:S(2)}) async-start(), calls=%async_computation.7 | async-start | bytes 10485760 | tf_op jit(solution)/shard_map/reduce_scatter | solution.py:601
  555.6 7.2 copy-start.37
  563.6 106.2 %copy-start.30 = (bf16[1024,128]{1,0:T(8,128)(2,1)S(1)}, bf16[1024,128]{1,0:T(8,128)(2,1)}, u32[]{:S(2)}) copy-start(bf16[1024,128]{1,0:T(8,128)(2,1)} %copy-done.29) | copy-start | bytes 786436
  563.6 106.2 %copy-start.32 = (bf16[1024,128]{1,0:T(8,128)(2,1)S(1)}, bf16[1024,128]{1,0:T(8,128)(2,1)}, u32[]{:S(2)}) copy-start(bf16[1024,128]{1,0:T(8,128)(2,1)} %copy-done.31) | copy-start | bytes 786436
  792.5 5.2 copy-start.34
  (24 other events, 58.0 us)
Sparse Core Ops, SparseCore 0:
  73.7 102.0 all-gather.7
  189.9 87.8 all-gather.9
  280.3 52.6 all-gather.5
  334.5 46.0 all-gather.11
  401.5 52.5 reduce-scatter.7
  541.4 45.3 reduce-scatter.3
  590.2 86.3 reduce-scatter.5

commit v3 on v2

v3 whole, which is shorter than its diff:
```python
import functools
import math

import jax
import jax.numpy as jnp
from jax import lax
from jax.experimental import pallas as pl
from jax.experimental.pallas import tpu as pltpu
from jax.sharding import PartitionSpec as P

HEAD_DIM = 128
norm_eps = 1e-05
rope_base = 10000.0
score_shift = math.log(4096.0)
score_scale = 1.0 / math.sqrt(HEAD_DIM)
contract_rows = (((0,), (0,)), ((), ()))
contract_cols = (((1,), (1,)), ((), ()))
plain = (((1,), (0,)), ((), ()))
f32 = jnp.float32
bf16 = jnp.bfloat16
MESH = pl.DeviceIdType.MESH
ANY = pl.BlockSpec(memory_space=pl.ANY)
VMEM = pl.BlockSpec(memory_space=pltpu.VMEM)


def dot(a, b, dims=plain):
    return lax.dot_general(a, b, dims, preferred_element_type=f32)


def remote(src, dst, send, recv, target):
    return pltpu.make_async_remote_copy(
        src_ref=src,
        dst_ref=dst,
        send_sem=send,
        recv_sem=recv,
        device_id=target,
        device_id_type=MESH,
    )


def greet(target):
    pl.semaphore_signal(
        pltpu.get_barrier_semaphore(), inc=1, device_id=target, device_id_type=MESH
    )


def place(cn):
    c = lax.axis_index("ctx")
    j, k = c // 2, c % 2
    return c, j, k, cn // 2, 2 * j + 1 - k


def greet_line(cn, ring):
    c, j, _, n, sib = place(cn)
    ring.greet()
    greet({"ctx": sib})

    @pl.when(j < n - 1)
    def _():
        greet({"ctx": c + 2})

    @pl.when(j > 0)
    def _():
        greet({"ctx": c - 2})

    inner = jnp.where(j > 0, 1, 0) + jnp.where(j < n - 1, 1, 0)
    pl.semaphore_wait(pltpu.get_barrier_semaphore(), 3 + inner)


def greet_ctx(cn):
    c = lax.axis_index("ctx")
    for s in range(1, cn):
        greet({"ctx": lax.rem(c + s, cn)})


class LineGather:
    def __init__(self, cn, own, full, sem):
        self.cn, self.own, self.full, self.sem = cn, own, full, sem

    def copy(self, src, origin, kind, target):
        _, _, k, _, _ = place(self.cn)
        sem = self.sem
        return remote(
            src,
            self.full.at[2 * origin + k],
            sem.at[kind, origin],
            sem.at[3 if kind < 2 else 4, origin],
            {"ctx": target},
        )

    def start(self):
        c, j, _, n, sib = place(self.cn)

        @pl.when(j < n - 1)
        def _():
            self.copy(self.own, j, 0, c + 2).start()

        @pl.when(j > 0)
        def _():
            self.copy(self.own, j, 1, c - 2).start()

        self.copy(self.own, j, 2, sib).start()

    def forward(self, first=1, last=None):
        c, j, k, n, sib = place(self.cn)
        for s in range(first, n if last is None else last + 1):

            @pl.when(j - s >= 0)
            def _():
                o = j - s
                block = self.full.at[2 * o + k]
                self.copy(block, o, 0, sib).wait_recv()

                @pl.when(j < n - 1)
                def _():
                    self.copy(block, o, 0, c + 2).start()

                self.copy(block, o, 2, sib).start()

            @pl.when(j + s <= n - 1)
            def _():
                o = j + s
                block = self.full.at[2 * o + k]
                self.copy(block, o, 1, sib).wait_recv()

                @pl.when(j > 0)
                def _():
                    self.copy(block, o, 1, c - 2).start()

                self.copy(block, o, 2, sib).start()

    def finish(self):
        c, j, k, n, sib = place(self.cn)
        for o in range(n):
            block = self.full.at[2 * o + 1 - k]
            remote(
                block, block, self.sem.at[2, o], self.sem.at[4, o], {"ctx": sib}
            ).wait_recv()
        for o in range(n):
            block = self.full.at[2 * o + k]

            @pl.when((j < n - 1) & (o <= j))
            def _():
                self.copy(block, o, 0, sib).wait_send()

            @pl.when((j > 0) & (o >= j))
            def _():
                self.copy(block, o, 1, sib).wait_send()

            self.copy(block, o, 2, sib).wait_send()


class Swap:
    def __init__(self, cn, src, dst, sem, local, pick=None):
        self.cn, self.sem, self.local = cn, sem, local
        self.src = pick or (lambda c: src.at[c])
        self.dst = dst if callable(dst) else lambda c: dst.at[c]

    def copy(self, s):
        c = lax.axis_index("ctx")
        peer = lax.rem(c + s, self.cn)
        return remote(
            self.src(peer),
            self.dst(c),
            self.sem.at[0, s],
            self.sem.at[1, s],
            {"ctx": peer},
        )

    def start(self):
        c = lax.axis_index("ctx")
        for s in range(1, self.cn):
            self.copy(s).start()
        pltpu.make_async_copy(self.src(c), self.dst(c), self.local).start()

    def finish(self):
        c = lax.axis_index("ctx")
        pltpu.make_async_copy(self.src(c), self.dst(c), self.local).wait()
        for s in range(1, self.cn):
            source = lax.rem(c - s + self.cn, self.cn)
            block = self.dst(source)
            remote(
                block, block, self.sem.at[0, s], self.sem.at[1, s], {"ctx": source}
            ).wait_recv()
            self.copy(s).wait_send()


class RingGather:
    def __init__(self, dpn, own, full, sem):
        self.dpn, self.own, self.full, self.sem = dpn, own, full, sem
        self.hops = dpn // 2
        d = lax.axis_index("dp")
        self.p = d // 2 * 2 + lax.rem(lax.rem(d, 2) + d // 2, 2)

    def member(self, step):
        p = lax.rem(self.p + step + self.dpn, self.dpn)
        return p // 2 * 2 + lax.rem(lax.rem(p, 2) + p // 2, 2)

    def half(self, ref, h, right):
        if h < self.hops:
            return ref
        m = self.full.shape[1] // 2
        return ref.at[pl.ds(0 if right else m, m)]

    def copy(self, h, right):
        way = 1 if right else -1
        origin = self.member(-way * (h - 1))
        src = self.own if h == 1 else self.full.at[origin]
        return remote(
            self.half(src, h, right),
            self.half(self.full.at[origin], h, right),
            self.sem.at[0 if right else 1, h],
            self.sem.at[2 if right else 3, h],
            {"dp": self.member(way)},
        )

    def arrival(self, h, right):
        way = 1 if right else -1
        block = self.half(self.full.at[self.member(-way * h)], h, right)
        return remote(
            block,
            block,
            self.sem.at[0 if right else 1, h],
            self.sem.at[2 if right else 3, h],
            {"dp": self.member(way)},
        )

    def greet(self):
        greet({"dp": self.member(1)})
        greet({"dp": self.member(-1)})

    def start(self):
        self.copy(1, True).start()
        self.copy(1, False).start()

    def forward(self):
        for h in range(1, self.hops):
            for right in (True, False):
                self.arrival(h, right).wait_recv()
                self.copy(h + 1, right).start()

    def finish(self):
        for right in (True, False):
            self.arrival(self.hops, right).wait_recv()
        for h in range(1, self.hops + 1):
            for right in (True, False):
                self.copy(h, right).wait_send()


class RingSum:
    def __init__(self, dpn, blocks, got, sem):
        self.dpn, self.blocks, self.got, self.sem = dpn, blocks, got, sem
        self.ring = RingGather(dpn, None, blocks, sem)
        self.hops = dpn // 2

    def part(self, s, right):
        m = self.blocks.shape[1] // 2
        if s > 1:
            return pl.ds(0, 2 * m)
        return pl.ds(0 if right else m, m)

    def copy(self, s, right):
        way = 1 if right else -1
        target = self.ring.member(way * (self.hops - s + 1))
        at = self.part(s, right)
        return remote(
            self.blocks.at[target, at],
            self.got.at[0 if right else 1, s - 1, at],
            self.sem.at[0 if right else 1, s],
            self.sem.at[2 if right else 3, s],
            {"dp": self.ring.member(way)},
        )

    def order(self):
        out = [self.ring.member(self.hops)]
        for s in range(self.hops - 1, 0, -1):
            out += [self.ring.member(s), self.ring.member(-s)]
        return out + [self.ring.member(0)]

    def start(self):
        self.copy(1, True).start()
        self.copy(1, False).start()

    def take(self, s, right, target):
        self.copy(s, right).wait_recv()
        at = self.part(s, right)
        side = 0 if right else 1
        block = self.blocks.at[target, at]
        block[...] = (block[...].astype(f32) + self.got[side, s - 1, at].astype(f32)).astype(bf16)

    def forward(self, s):
        for right in (True, False):
            way = 1 if right else -1
            self.take(s, right, self.ring.member(way * (self.hops - s)))
            self.copy(s + 1, right).start()

    def finish(self, out):
        for right in (True, False):
            self.copy(self.hops, right).wait_recv()
        mine = self.ring.member(0)
        if self.hops > 1:
            total = self.blocks[mine].astype(f32)
            for side in (0, 1):
                total = total + self.got[side, self.hops - 1].astype(f32)
            out[...] = total.reshape(out.shape).astype(out.dtype)
        for s in range(1, self.hops + 1):
            for right in (True, False):
                self.copy(s, right).wait_send()


def ring_scratch(dpn, m, width):
    return [
        pltpu.VMEM((dpn, m, width), bf16),
        pltpu.VMEM((2, dpn // 2, m, width), bf16),
        pltpu.SemaphoreType.DMA((4, dpn // 2 + 1)),
    ]


def outer(a_ref, b_ref, out, at, tile=512):
    a = a_ref[:, at]
    width = out.shape[-1]
    for lo in range(0, width, tile):
        to = slice(lo, min(lo + tile, width))
        out[:, to] = dot(a, b_ref[:, to], contract_rows).astype(bf16)


def outer_all(a_ref, b_ref, blocks, tile=512):
    count, m, width = blocks.shape
    many = max(1, 128 // m)
    for first in range(0, count, many):
        a = a_ref[:, first * m : (first + many) * m]
        for lo in range(0, width, tile):
            to = slice(lo, min(lo + tile, width))
            part = dot(a, b_ref[:, to], contract_rows).astype(bf16)
            for i in range(many):
                blocks[first + i, :, to] = part[i * m : (i + 1) * m]


class LineSum:
    def __init__(self, cn, compute, part, cross, cross_in, flow, arrived, sem):
        self.cn, self.compute, self.part = cn, compute, part
        self.cross, self.cross_in, self.flow = cross, cross_in, flow
        self.arrived, self.sem = arrived, sem

    def across(self, t):
        _, _, _, _, sib = place(self.cn)
        return remote(
            self.cross.at[t],
            self.cross_in.at[t],
            self.sem.at[0, t],
            self.sem.at[2, t],
            {"ctx": sib},
        )

    def along(self, t, slot, target):
        return remote(
            self.flow.at[t],
            self.arrived.at[slot],
            self.sem.at[1, t],
            self.sem.at[3, slot],
            {"ctx": target},
        )

    def produce(self, t, slot):
        _, _, k, _, _ = place(self.cn)
        part = self.part.at[slot]
        self.compute(t, part)
        self.cross[t] = part[1 - k].astype(bf16)
        self.across(t).start()

    def collect(self, t, slot):
        _, j, k, n, sib = place(self.cn)
        part = self.part.at[slot, k]
        self.across(t).wait_recv()
        part[...] += self.cross_in[t].astype(f32)

        @pl.when((j > 0) & (t >= j))
        def _():
            self.along(t, t, sib).wait_recv()
            part[...] += self.arrived[t].astype(f32)

        @pl.when((j < n - 1) & (t <= j))
        def _():
            slot_in = jnp.where(t == j, n, t)
            self.along(t, slot_in, sib).wait_recv()
            part[...] += self.arrived[slot_in].astype(f32)

    def send(self, t, slot, up):
        c, j, k, n, _ = place(self.cn)
        self.flow[t] = self.part[slot, k].astype(bf16)
        there = t if up else jnp.where(t == j - 1, n, t)
        self.along(t, there, c + 2 if up else c - 2).start()

    def drain(self):
        _, j, _, n, sib = place(self.cn)

        @pl.loop(0, n)
        def _(t):
            self.across(t).wait_send()

            @pl.when(t != j)
            def _():
                self.along(t, t, sib).wait_send()


def line_sums(cn, sums, between=None):
    _, j, _, n, _ = place(cn)

    @pl.loop(0, n - 1)
    def _(s):
        to_up, to_down = n - 1 - s + j, s - (n - 1 - j)
        for total in sums:

            @pl.when(s >= j)
            def _():
                total.produce(to_up, 0)

            @pl.when(s >= n - 1 - j)
            def _():
                total.produce(to_down, 1)

        for total in sums:

            @pl.when(s >= j)
            def _():
                total.collect(to_up, 0)
                total.send(to_up, 0, True)

            @pl.when(s >= n - 1 - j)
            def _():
                total.collect(to_down, 1)
                total.send(to_down, 1, False)

        if between is not None:
            between(s)

    for total in sums:
        total.produce(j, 0)
    for total in sums:
        total.collect(j, 0)


def sum_scratch(cn, rows, width):
    n = cn // 2
    return [
        pltpu.VMEM((2, 2, rows, width), f32),
        pltpu.VMEM((n, rows, width), bf16),
        pltpu.VMEM((n, rows, width), bf16),
        pltpu.VMEM((n, rows, width), bf16),
        pltpu.VMEM((n + 1, rows, width), bf16),
        pltpu.SemaphoreType.DMA((4, n + 1)),
    ]


def product(a_ref, b_ref, dims, rows, width):
    tile = min(512, width)

    def compute(t, out):
        a = a_ref[pl.ds(pl.multiple_of(t * 2 * rows, 2 * rows), 2 * rows), :]

        @pl.loop(0, width // tile)
        def _(i):
            at = pl.ds(pl.multiple_of(i * tile, tile), tile)
            b = b_ref[:, at] if dims == plain else b_ref[at, 0 : a_ref.shape[1]]
            out[:, :, at] = dot(a, b, dims).reshape(2, rows, tile)

    return compute


def rms(v):
    return lax.rsqrt(jnp.mean(v * v, axis=-1, keepdims=True) + norm_eps)


def front_kernel(
    cn, dpn, x, pack, down, x_all, pack_all, down_all, gsem, ssem, rsem, dsem, local
):
    c, d = lax.axis_index("ctx"), lax.axis_index("dp")
    mine = pack_all.at[d]
    swap = Swap(cn, pack, mine, ssem, local.at[0])
    gather = LineGather(cn, x, x_all, gsem)
    ring = RingGather(dpn, mine, pack_all, rsem)
    down_ring = RingGather(dpn, down, down_all, dsem)
    greet_ctx(cn)
    ring.greet()
    pl.semaphore_wait(pltpu.get_barrier_semaphore(), cn - 1 + 2)
    swap.start()
    gather.start()
    down_ring.start()
    keep = pltpu.make_async_copy(x, x_all.at[c], local.at[1])
    keep.start()
    keep_down = pltpu.make_async_copy(down, down_all.at[d], local.at[2])
    keep_down.start()
    gather.forward(1, 1)
    swap.finish()
    ring.start()
    down_ring.forward()
    gather.forward(2)
    ring.forward()
    keep.wait()
    keep_down.wait()
    gather.finish()
    ring.finish()
    down_ring.finish()


def project(x_all, w, gain, cosines, sines, an, qkv, hw, block):
    width = an.shape[1]
    per = block // x_all.shape[1]

    @pl.loop(0, an.shape[0] // block)
    def _(i):
        at = pl.ds(pl.multiple_of(i * block, block), block)
        x = x_all[pl.ds(i * per, per), :, 0:width].reshape(block, width).astype(f32)
        normed = (x * rms(x) * gain[...]).astype(bf16)
        an[at, :] = normed
        proj = dot(normed, w[:, 0 : 3 * hw])
        cos_b, sin_b = cosines[at, :], sines[at, :]
        for h in range(2 * hw // HEAD_DIM):
            lanes = slice(h * HEAD_DIM, (h + 1) * HEAD_DIM)
            v = proj[:, lanes]
            turned = v * cos_b + pltpu.roll(v, HEAD_DIM // 2, 1) * sin_b
            qkv[at, lanes] = turned.astype(bf16)
        qkv[at, 2 * hw :] = proj[:, 2 * hw :].astype(bf16)


def mask_block(q_seg, k_code, i, j, block):
    rows = lax.broadcasted_iota(jnp.int32, (block, block), 0) + i * block
    cols = lax.broadcasted_iota(jnp.int32, (block, block), 1) + j * block
    return (q_seg == k_code) & (cols <= rows)


def attend(qkv, q_info, k_code, out, mass, hw, block):
    mass[...] = jnp.zeros_like(mass)

    @pl.loop(0, qkv.shape[0] // block)
    def _(i):
        at = pl.ds(pl.multiple_of(i * block, block), block)
        q_seg, q_valid = q_info[at, 0:1], q_info[at, 1:2].astype(f32)
        for h in range(hw // HEAD_DIM):
            lane = [slice(t * hw + h * HEAD_DIM, t * hw + (h + 1) * HEAD_DIM) for t in range(3)]
            q = qkv[at, lane[0]]

            def step(j, acc):
                to = pl.ds(pl.multiple_of(j * block, block), block)
                s = dot(q, qkv[to, lane[1]], contract_cols) * score_scale - score_shift
                allowed = mask_block(q_seg, k_code[0:1, to], i, j, block)
                p = jnp.where(allowed, jax.nn.sigmoid(s), 0.0)
                mass[...] += jnp.sum(p * q_valid, axis=0, keepdims=True)
                return acc + dot(p.astype(bf16), qkv[to, lane[2]])

            acc = lax.fori_loop(0, i + 1, step, jnp.zeros((block, HEAD_DIM), f32))
            out[at, lane[0]] = acc.astype(bf16)


def attn_kernel(
    cn, dpn, x_all, w, gain, cosines, sines, q_info, k_code, gate, up, wo,
    an, qkv, o, mass, gate_all, up_own, wo_all, ssem, rsem, hsem, wsem, local,
):
    c, d = lax.axis_index("ctx"), lax.axis_index("dp")
    mine, wanted = d * cn + c, c * dpn + d
    stays = mine == wanted
    hop = remote(
        wo,
        wo_all.at[lax.rem(mine, dpn)],
        hsem.at[0],
        hsem.at[1],
        {"dp": lax.rem(mine, dpn), "ctx": mine // dpn},
    )
    keep = pltpu.make_async_copy(wo, wo_all.at[d], local.at[2])
    wo_ring = RingGather(dpn, wo_all.at[d], wo_all, wsem)
    rows = x_all.shape[1]
    hw = qkv.shape[1] // 3
    swap_gate = Swap(cn, gate, gate_all.at[d], ssem.at[0], local.at[0])
    swap_up = Swap(cn, up, up_own, ssem.at[1], local.at[1])
    ring = RingGather(dpn, gate_all.at[d], gate_all, rsem)
    greet_ctx(cn)
    ring.greet()

    @pl.when(jnp.logical_not(stays))
    def _():
        greet({"dp": wanted // cn, "ctx": lax.rem(wanted, cn)})

    pl.semaphore_wait(
        pltpu.get_barrier_semaphore(), cn - 1 + 2 + jnp.where(stays, 0, 1)
    )

    @pl.when(stays)
    def _():
        keep.start()
        keep.wait()

    @pl.when(jnp.logical_not(stays))
    def _():
        hop.start()

    swap_gate.start()
    swap_up.start()

    @pl.when(jnp.logical_not(stays))
    def _():
        arrived = wo_all.at[d]
        remote(arrived, arrived, hsem.at[0], hsem.at[1], {"dp": d, "ctx": c}).wait_recv()

    wo_ring.start()
    project(x_all, w, gain, cosines, sines, an, qkv, hw, 2 * rows)
    wo_ring.forward()
    swap_gate.finish()
    ring.start()
    attend(qkv, q_info, k_code, o, mass, hw, 2 * rows)
    ring.forward()
    swap_up.finish()
    wo_ring.finish()
    ring.finish()

    @pl.when(jnp.logical_not(stays))
    def _():
        hop.wait_send()


def middle_kernel(
    cn, dpn, o, wo, x, gain, up, h1, bn_all, up_all, own, gsem, rsem, local, *sum_refs
):
    c, d = lax.axis_index("ctx"), lax.axis_index("dp")
    _, _, k, n, _ = place(cn)
    rows, width = x.shape
    gather = LineGather(cn, own, bn_all, gsem)
    ring = RingGather(dpn, up, up_all, rsem)
    total = LineSum(cn, product(o, wo, plain, rows, width), *sum_refs)
    greet_line(cn, ring)
    ring.start()
    keep_up = pltpu.make_async_copy(up, up_all.at[d], local.at[0])
    keep_up.start()
    line_sums(cn, [total])
    mid = x[...].astype(f32) + total.part[0, k]
    h1[...] = mid
    own[...] = (mid * rms(mid) * gain[...]).astype(bf16)
    gather.start()
    keep = pltpu.make_async_copy(own, bn_all.at[c], local.at[1])
    keep.start()
    ring.forward()
    gather.forward()
    total.drain()
    keep.wait()
    keep_up.wait()
    gather.finish()
    ring.finish()


def back_kernel(
    cn, dpn, bn, dgu, wg, wu, h1, dy, gain, dh1, dob_all, term, g_own,
    own, gsem, lsem, *scratch,
):
    sum_refs, ring_refs = scratch[:-3], scratch[-3:]
    rows, width = dy.shape
    ff = wg.shape[1]
    tile = min(512, width)
    c, _, k, n, _ = place(cn)

    def compute(t, out):
        at = pl.ds(pl.multiple_of(t * 2 * rows, 2 * rows), 2 * rows)

        @pl.loop(0, width // tile)
        def _(i):
            to = pl.ds(pl.multiple_of(i * tile, tile), tile)
            part = dot(dgu[at, 0:ff], wg[to, :], contract_cols)
            part = part + dot(dgu[at, ff:], wu[to, :], contract_cols)
            out[:, :, to] = part.reshape(2, rows, tile)

    total = LineSum(cn, compute, *sum_refs)
    ring = RingSum(dpn, *ring_refs)
    blocks = ring_refs[0]
    m = blocks.shape[1]
    greet_line(cn, ring.ring)
    order = ring.order()

    def weight_grad(member):
        outer(bn, dgu, blocks.at[member], pl.ds(pl.multiple_of(member * m, m), m))

    weight_grad(order[0])
    ring.start()

    def between(s):
        for i in range(ring.hops - 1):

            @pl.when(s == min(i, n - 2))
            def _():
                weight_grad(order[1 + 2 * i])
                weight_grad(order[2 + 2 * i])

            @pl.when(s == min(i + 1, n - 2))
            def _():
                ring.forward(i + 1)

    line_sums(cn, [total], between)
    dbn = total.part[0, k]
    mid = h1[...]
    r2 = rms(mid)
    xh2 = mid * r2
    term[...] = jnp.sum(dbn * xh2, axis=0, keepdims=True)
    u2 = dbn * gain[...]
    grad = dy[...].astype(f32) + r2 * (u2 - xh2 * jnp.mean(u2 * xh2, axis=-1, keepdims=True))
    dh1[...] = grad
    own[...] = grad.astype(bf16)
    gather = LineGather(cn, own, dob_all, gsem)
    gather.start()
    keep = pltpu.make_async_copy(own, dob_all.at[c], lsem)
    keep.start()
    weight_grad(order[-1])
    gather.forward()
    total.drain()
    keep.wait()
    gather.finish()
    ring.finish(g_own)


def attend_back(qkv, do, cosines, sines, q_info, k_info, dq, dqkv, hw, block):
    count = qkv.shape[0] // block
    dq[...] = jnp.zeros_like(dq)

    def turn_back(g, at):
        return g * cosines[at, :] - pltpu.roll(g, HEAD_DIM // 2, 1) * sines[at, :]

    @pl.loop(0, count)
    def _(j):
        to = pl.ds(pl.multiple_of(j * block, block), block)
        k_code = k_info[to, :]
        for h in range(hw // HEAD_DIM):
            lane = [slice(t * hw + h * HEAD_DIM, t * hw + (h + 1) * HEAD_DIM) for t in range(3)]
            k, v = qkv[to, lane[1]], qkv[to, lane[2]]

            def step(i, carry):
                dk, dv = carry
                at = pl.ds(pl.multiple_of(i * block, block), block)
                q, do_i = qkv[at, lane[0]], do[at, lane[0]]
                s = dot(k, q, contract_cols) * score_scale - score_shift
                keys = lax.broadcasted_iota(jnp.int32, (block, block), 0) + j * block
                queries = lax.broadcasted_iota(jnp.int32, (block, block), 1) + i * block
                allowed = (k_code == q_info[0:1, at]) & (keys <= queries)
                sg = jnp.where(allowed, jax.nn.sigmoid(s), 0.0)
                dp = dot(v, do_i, contract_cols)
                ds = (dp * sg * (1.0 - sg)).astype(bf16)
                dq[at, lane[0]] += dot(ds, k, contract_rows)
                return dk + dot(ds, q), dv + dot(sg.astype(bf16), do_i)

            zero = jnp.zeros((block, HEAD_DIM), f32)
            dk, dv = lax.fori_loop(j, count, step, (zero, zero))
            dqkv[to, lane[1]] = turn_back(dk * score_scale, to).astype(bf16)
            dqkv[to, lane[2]] = dv.astype(bf16)

    @pl.loop(0, count)
    def _(i):
        at = pl.ds(pl.multiple_of(i * block, block), block)
        for h in range(hw // HEAD_DIM):
            lanes = slice(h * HEAD_DIM, (h + 1) * HEAD_DIM)
            dqkv[at, lanes] = turn_back(dq[at, lanes] * score_scale, at).astype(bf16)


def last_kernel(
    cn, dpn, do, g_gu, g_down, g_out, qkv, cosines, sines, q_info, k_info, an, w, dh1, x, gain,
    grad_in, term, gu_all, down_own, out_own, qkv_own,
    dq, dqkv, usem, local, *scratch,
):
    sum_refs, rings = scratch[:-9], (scratch[-9:-6], scratch[-6:-3], scratch[-3:])
    rows, width = x.shape
    hw = width // cn
    _, _, k, n, _ = place(cn)
    down_ring, out_ring, qkv_ring = (RingSum(dpn, *refs) for refs in rings)
    swap_gu = Swap(cn, g_gu, gu_all, usem, local.at[0])
    greet_ctx(cn)
    down_ring.ring.greet()
    pl.semaphore_wait(pltpu.get_barrier_semaphore(), cn - 1 + 2)
    swap_gu.start()
    fill_down = pltpu.make_async_copy(g_down, rings[0][0], local.at[1])
    fill_out = pltpu.make_async_copy(g_out, rings[1][0], local.at[2])
    fill_down.start()
    fill_out.start()
    fill_down.wait()
    down_ring.start()
    fill_out.wait()
    out_ring.start()
    m_qkv = rings[2][0].shape[1]
    order = qkv_ring.order()

    def grad_qkv(member):
        outer(an, dqkv, rings[2][0].at[member], pl.ds(pl.multiple_of(member * m_qkv, m_qkv), m_qkv))

    attend_back(qkv, do, cosines, sines, q_info, k_info, dq, dqkv, hw, 2 * rows)
    for i in range(down_ring.hops - 1):
        down_ring.forward(i + 1)
        out_ring.forward(i + 1)
    grad_qkv(order[0])
    qkv_ring.start()
    total = LineSum(cn, product(dqkv, w, contract_cols, rows, width), *sum_refs)

    def between(s):
        for i in range(qkv_ring.hops - 1):

            @pl.when(s == min(i, n - 2))
            def _():
                grad_qkv(order[1 + 2 * i])
                grad_qkv(order[2 + 2 * i])

            @pl.when(s == min(i + 1, n - 2))
            def _():
                qkv_ring.forward(i + 1)

    line_sums(cn, [total], between)
    grad_qkv(order[-1])
    dan = total.part[0, k]
    xf = x[...].astype(f32)
    r1 = rms(xf)
    xh1 = xf * r1
    term[...] = jnp.sum(dan * xh1, axis=0, keepdims=True)
    u1 = dan * gain[...]
    grad = dh1[...] + r1 * (u1 - xh1 * jnp.mean(u1 * xh1, axis=-1, keepdims=True))
    grad_in[...] = grad.astype(bf16)
    total.drain()
    down_ring.finish(down_own)
    out_ring.finish(out_own)
    qkv_ring.finish(qkv_own)
    swap_gu.finish()


def return_kernel(
    cn, dpn, qkv, out, tot, qkv_all, out_all, tot_out,
    tot_in, tot_sum, tot_last, qsem, tsem, dsem, osem, local,
):
    c, d = lax.axis_index("ctx"), lax.axis_index("dp")
    mine, goal = d * cn + c, c * dpn + d
    stays = mine == goal
    greet_ctx(cn)

    @pl.when(jnp.logical_not(stays))
    def _():
        greet({"dp": lax.rem(mine, dpn), "ctx": mine // dpn})

    hop = remote(
        out, out_all, osem.at[0], osem.at[1], {"dp": goal // cn, "ctx": lax.rem(goal, cn)}
    )
    keep = pltpu.make_async_copy(out, out_all, local.at[2])
    for s in range(1, dpn):
        greet({"dp": lax.rem(d + s, dpn)})
    pl.semaphore_wait(
        pltpu.get_barrier_semaphore(), cn - 1 + dpn - 1 + jnp.where(stays, 0, 1)
    )

    @pl.when(stays)
    def _():
        keep.start()

    @pl.when(jnp.logical_not(stays))
    def _():
        hop.start()

    totals = Swap(cn, tot, tot_in, tsem, local.at[0])
    totals.start()
    first = Swap(cn, qkv, qkv_all, qsem, local.at[1])
    first.start()
    totals.finish()
    tot_sum[...] = jnp.sum(tot_in[...], axis=0)

    def share(s):
        peer = lax.rem(d + s, dpn)
        return remote(
            tot_sum.at[peer], tot_last.at[d], dsem.at[0, s], dsem.at[1, s], {"dp": peer}
        )

    for s in range(1, dpn):
        share(s).start()
    tot_last[d] = tot_sum[d]
    for s in range(1, dpn):
        source = lax.rem(d - s + dpn, dpn)
        block = tot_last.at[source]
        remote(
            block, block, dsem.at[0, s], dsem.at[1, s], {"dp": source}
        ).wait_recv()
    for s in range(1, dpn):
        share(s).wait_send()
    tot_out[...] = jnp.sum(tot_last[...], axis=0)
    first.finish()

    @pl.when(stays)
    def _():
        keep.wait()

    @pl.when(jnp.logical_not(stays))
    def _():
        hop.wait_recv()
        hop.wait_send()


def spread_kernel(cn, dpn, qkv, gu, down, out, gq, gk, gv, go, gg, gu_out, gd):
    hw = qkv.shape[2] // 3
    ff_rows = gd.shape[0]
    ff = ff_rows * dpn
    gd[...] = down[...].astype(f32)
    go[...] = out[...].astype(f32)
    for c in range(cn):
        for i, ref in enumerate((gq, gk, gv)):
            ref[:, c * hw : (c + 1) * hw] = qkv[c, :, i * hw : (i + 1) * hw].astype(f32)
        for i, ref in enumerate((gg, gu_out)):
            for d in range(dpn):
                to = (d * cn + c) * ff_rows
                lo = i * ff + d * ff_rows
                ref[:, to : to + ff_rows] = gu[c, :, lo : lo + ff_rows].astype(f32)


def call(kernel, outs, ins, specs_in, specs_out, scratch, number, flops=0, moved=0):
    return pl.pallas_call(
        kernel,
        out_shape=outs,
        in_specs=specs_in,
        out_specs=specs_out,
        scratch_shapes=scratch,
        compiler_params=pltpu.CompilerParams(
            collective_id=number, has_side_effects=True, vmem_limit_bytes=60 * 2**20
        ),
        cost_estimate=pl.CostEstimate(flops=flops, bytes_accessed=moved, transcendentals=0),
    )(*ins)


def shape(dims, dtype=bf16):
    return jax.ShapeDtypeStruct(dims, dtype)


def rope_tables(positions):
    half_dim = HEAD_DIM // 2
    inverse = jnp.exp(
        jnp.arange(half_dim, dtype=f32) * (-2.0 * math.log(rope_base) / HEAD_DIM)
    )
    angles = positions[:, None] * inverse[None, :]
    return jnp.cos(angles), jnp.sin(angles)


def rotate(values, cosines, sines, sign):
    half = HEAD_DIM // 2
    parts = []
    for h in range(values.shape[1] // HEAD_DIM):
        a = values[:, h * HEAD_DIM : h * HEAD_DIM + half]
        b = values[:, h * HEAD_DIM + half : (h + 1) * HEAD_DIM]
        parts += [a * cosines - sign * b * sines, b * cosines + sign * a * sines]
    return jnp.concatenate(parts, axis=1)


def gather(v, axes, axis=0):
    return lax.all_gather(v, axes, axis=axis, tiled=True)


def scatter_sum(v, axes):
    return lax.psum_scatter(v, axes, scatter_dimension=0, tiled=True)


def shards(
    hidden_in,
    out_grad,
    seg_ids,
    valid_mask,
    w_query,
    w_key,
    w_value,
    w_output,
    w_gate,
    w_up,
    w_down,
    gain_attn,
    gain_mlp,
):
    dpn = lax.axis_size("dp")
    cn = lax.axis_size("ctx")
    n = cn // 2
    x_local = hidden_in[0]
    dy_local = out_grad[0]
    rows, width = x_local.shape
    seq = rows * cn
    dr = w_query.shape[0]
    hw = width // cn
    heads = hw // HEAD_DIM
    ff_rows = w_down.shape[0]
    ff = ff_rows * dpn
    dma = pltpu.SemaphoreType.DMA
    mib = 2**20

    code = (seg_ids[0] * 2 + valid_mask[0]).astype(bf16)
    x_ext = jnp.concatenate([x_local, jnp.broadcast_to(code[:, None], (rows, 128))], axis=1)
    lanes = jnp.arange(128)[None, :]
    gain_cols = jnp.where(lanes == 0, gain_attn[:, None], gain_mlp[:, None]).astype(bf16)
    qkv_pack = jnp.concatenate(
        [w.astype(bf16).reshape(dr, cn, hw) for w in (w_query, w_key, w_value)]
        + [jnp.broadcast_to(gain_cols[:, None, :], (dr, cn, 128))],
        axis=2,
    ).transpose(1, 0, 2)
    pw = 3 * hw + 128
    gate_pack, up_pack = (
        w.astype(bf16).reshape(dr, dpn, cn, ff_rows).transpose(2, 0, 1, 3).reshape(cn, dr, ff)
        for w in (w_gate, w_up)
    )
    ring_sem = dma((4, dpn // 2 + 1))
    x_all, qkv_full, down = call(
        functools.partial(front_kernel, cn, dpn),
        (shape((cn, rows, width + 128)), shape((dpn, cn, dr, pw)), shape((dpn, ff_rows, width))),
        (x_ext, qkv_pack, w_down.astype(bf16)),
        [ANY] * 3,
        (ANY, ANY, ANY),
        [dma((5, n)), dma((2, cn)), ring_sem, ring_sem, dma((3,))],
        1,
        moved=160 * mib,
    )
    down = down.reshape(ff, width)
    x_all, dy_own = lax.optimization_barrier((x_all, dy_local))
    dys = gather(dy_own, "ctx")
    qkv_full = qkv_full.reshape(width, pw)
    w_qkv = qkv_full
    gains = qkv_full[:, 3 * hw : 3 * hw + 2].astype(f32).T
    gain_one, gain_two = gains[0:1], gains[1:2]

    all_codes = x_all[:, :, width].reshape(seq).astype(jnp.int32)
    seg = all_codes // 2
    valid = all_codes % 2
    index = jnp.arange(seq, dtype=jnp.int32)
    starts = jnp.sum((seg[None, :] < seg[:, None]).astype(jnp.int32), axis=1)
    cosines, sines = rope_tables((index - starts).astype(f32))
    k_code = jnp.where(valid == 1, seg, -1)[None]
    q_info = jnp.stack([seg, valid], axis=1)
    cos_two = jnp.concatenate([cosines, cosines], axis=1)
    sin_two = jnp.concatenate([-sines, sines], axis=1)

    line_scratch = sum_scratch(cn, rows, width)
    an, proj, o, mass, w_gate_c, up_own, wo = call(
        functools.partial(attn_kernel, cn, dpn),
        (
            shape((seq, width)),
            shape((seq, 3 * hw)),
            shape((seq, hw)),
            shape((1, 2 * rows), f32),
            shape((dpn, cn, dr, ff)),
            shape((cn, dr, ff)),
            shape((dpn, dr, width)),
        ),
        (
            x_all, w_qkv, gain_one, cos_two, sin_two, q_info, k_code, gate_pack, up_pack,
            w_output.astype(bf16),
        ),
        [VMEM] * 7 + [ANY] * 3,
        (VMEM,) * 4 + (ANY,) * 3,
        [dma((2, 2, cn)), ring_sem, dma((2,)), ring_sem, dma((3,))],
        2,
        moved=160 * mib,
    )
    h1, bn, w_up_c = call(
        functools.partial(middle_kernel, cn, dpn),
        (
            shape((rows, width), f32),
            shape((cn, rows, width)),
            shape((dpn, cn, dr, ff)),
        ),
        (o, wo.reshape(hw, width), x_local, gain_two, up_own),
        [VMEM] * 4 + [ANY],
        (VMEM, ANY, ANY),
        [pltpu.VMEM((rows, width), bf16), dma((5, n)), ring_sem, dma((2,))] + line_scratch,
        3,
        moved=160 * mib,
    )
    wo = wo.reshape(hw, width)
    w_gate_c = w_gate_c.reshape(width, ff)
    w_up_c = w_up_c.reshape(width, ff)
    bn = bn.reshape(seq, width)
    gate = dot(bn, w_gate_c)
    up = dot(bn, w_up_c)
    sig = jax.nn.sigmoid(gate)
    silu = gate * sig
    hid = (silu * up).astype(bf16)
    dhid = dot(dys, down, contract_cols)
    dgate = (dhid * up * sig * (1.0 + gate * (1.0 - sig))).astype(bf16)
    dup = (dhid * silu).astype(bf16)
    dgu = jnp.concatenate([dgate, dup], axis=1)
    branch = dot(hid, down).astype(bf16)
    dgu, branch = lax.optimization_barrier((dgu, branch))
    branch = scatter_sum(branch, "ctx")
    result = (h1 + branch.astype(f32)).astype(bf16)
    dh1, dob, term_two, g_gu = call(
        functools.partial(back_kernel, cn, dpn),
        (
            shape((rows, width), f32),
            shape((cn, rows, width)),
            shape((1, width), f32),
            shape((cn, dr, 2 * ff)),
        ),
        (bn, dgu, w_gate_c, w_up_c, h1, dy_local, gain_two),
        [VMEM] * 7,
        (VMEM, ANY, VMEM, VMEM),
        [pltpu.VMEM((rows, width), bf16), dma((5, n)), dma]
        + line_scratch
        + ring_scratch(dpn, cn * dr, 2 * ff),
        4,
        moved=160 * mib,
    )
    dob = dob.reshape(seq, width)
    do = dot(dob, wo, contract_cols).astype(bf16)
    g_out = dot(o, dob, contract_rows).astype(bf16).reshape(dpn, dr, width)
    g_down = dot(hid, dys, contract_rows).astype(bf16).reshape(dpn, ff_rows, width)
    grad_input, term_one, gu_back, g_down, out_own, qkv_own = call(
        functools.partial(last_kernel, cn, dpn),
        (
            shape((rows, width)),
            shape((1, width), f32),
            shape((cn, dr, 2 * ff)),
            shape((ff_rows, width)),
            shape((dr, width)),
            shape((cn, dr, 3 * hw)),
        ),
        (
            do, g_gu, g_down, g_out, proj, cos_two, sin_two, seg[None], k_code.T, an, w_qkv,
            dh1, x_local, gain_one,
        ),
        [VMEM] + [ANY] * 3 + [VMEM] * 10,
        (VMEM, VMEM, ANY, VMEM, VMEM, VMEM),
        [
            pltpu.VMEM((seq, hw), f32),
            pltpu.VMEM((seq, 3 * hw), bf16),
            dma((2, cn)),
            dma((3,)),
        ]
        + line_scratch
        + ring_scratch(dpn, ff_rows, width)
        + ring_scratch(dpn, dr, width)
        + ring_scratch(dpn, cn * dr, 3 * hw),
        5,
        moved=160 * mib,
    )

    mass_part = jnp.sum(mass) / (heads * cn)
    pieces = [t.reshape(dpn, cn, dr).transpose(1, 0, 2) for t in (term_one, term_two)]
    pieces.append(jnp.broadcast_to(mass_part, (cn, dpn, dr)))
    tot = jnp.zeros((cn, dpn, 8, 128), f32).at[:, :, :3, :dr].set(jnp.stack(pieces, axis=2))
    q_all, g_out, totals = call(
        functools.partial(return_kernel, cn, dpn),
        (shape((cn, dr, 3 * hw)), shape((dr, width)), shape((8, 128), f32)),
        (qkv_own, out_own, tot),
        [ANY, ANY, VMEM],
        (ANY, ANY, VMEM),
        [
            pltpu.VMEM((cn, dpn, 8, 128), f32),
            pltpu.VMEM((dpn, 8, 128), f32),
            pltpu.VMEM((dpn, 8, 128), f32),
            dma((2, cn)),
            dma((2, cn)),
            dma((2, dpn)),
            dma((2,)),
            dma((3,)),
        ],
        6,
        moved=80 * mib,
    )
    g_q, g_k, g_v, g_o, g_gate, g_up, g_down = pl.pallas_call(
        functools.partial(spread_kernel, cn, dpn),
        out_shape=tuple(shape((dr, width), f32) for _ in range(4))
        + tuple(shape((dr, ff * cn), f32) for _ in range(2))
        + (shape((ff_rows, width), f32),),
        in_specs=[VMEM] * 4,
        out_specs=(VMEM,) * 7,
        compiler_params=pltpu.CompilerParams(vmem_limit_bytes=48 * 2**20),
    )(q_all, gu_back, g_down, g_out)
    mass_mean = totals[2, 0] / (dpn * seq)
    return (
        result[None],
        grad_input[None],
        g_q,
        g_k,
        g_v,
        g_o,
        g_gate,
        g_up,
        g_down,
        totals[0, :dr],
        totals[1, :dr],
        mass_mean,
    )


def solution(mesh):
    tok = P("dp", "ctx", None)
    ids = P("dp", "ctx")
    mat = P(("dp", "ctx"), None)
    vec = P(("dp", "ctx"))
    return jax.shard_map(
        shards,
        mesh=mesh,
        in_specs=(tok, tok, ids, ids) + (mat,) * 7 + (vec, vec),
        out_specs=(tok, tok) + (mat,) * 7 + (vec, vec, P()),
        check_vma=False,
    )
```

time: 812 us -> 633 us (0.78)
  Pallas kernels: 577 us -> 518 us
  matrix products: 85.7 us -> 44.1 us
  waiting for transfers between devices: 30.6 us -> 0.04 us
  local copies, waits for them, and re-layouts: 43.5 us -> 18 us
  other arithmetic: 51.5 us -> 26.8 us
    pallas_call x6, Pallas kernels: 577 us -> 514 us  [call(): pl.pallas_call(kernel, out_shape=outs, in_specs=specs_in, out_specs=specs...]
    dot_general x20 -> x7, matrix products: 85.7 us -> 44.1 us  [dot(): return lax.dot_general(a, b, dims, preferred_element_type=f32)]
    all_gather x4 -> x1, waiting for transfers between devices: 30 us -> 0.01 us  [gather(): return lax.all_gather(v, axes, axis=axis, tiled=True)]
    convert_element_type x8 -> x3, other arithmetic: 19.6 us -> 1.32 us  [the longest x1 1.11 us: shards(): w_down.astype(bf16)]
    unnamed x97 -> x58, local copies, waits for them, and re-layouts: 17 us -> 9.51 us
  transfers between devices with their start and end apart: 7 -> 2, of which waited for: 1 -> 0; matrix products, arithmetic and copies ran while one was open for 16% -> 7% of each run, Pallas kernels for 52% -> 70%
where the time goes in v3:
time: 633 us; the launch traced here: 624 us
  Pallas kernels  518 us (82%)
  matrix products  44.1 us (7%)
  other arithmetic  26.8 us (4%)
  local copies, waits for them, and re-layouts  18 us (3%)
  between operations  17.1 us (3%)
    pallas_call x6, Pallas kernels, call(): pl.pallas_call(kernel, out_shape=outs, in_specs=specs_in, out_specs=specs...  514 us
    dot_general x7, matrix products, dot(): return lax.dot_general(a, b, dims, preferred_element_type=f32)  44.1 us
  transfers between devices with their start and end apart: 2, of which 0 were waited for; matrix products, arithmetic and copies ran while one was open for 7% of the time, Pallas kernels for 70%

profile of v3, /device:TPU:9, one launch (start us, length us, event | category | flops | bytes accessed | tf_op | source)
XLA Modules:
  0.0 624.0 jit_solution(8975833197462752926)
XLA Ops:
  14.0 79.3 %shard_map.220 = (bf16[8,128,2176]{2,1,0:T(8,128)(2,1)}, bf16[4,8,64,896]{3,2,1,0:T(8,128)(2,1)}, bf16[4,256,2048]{2,1,0:T(8,128)(2,1)}) custom-call(bf16[128,2176]{1,0:T(8,128)(2,1)} %pad_maximum_fusion.1.x, bf16[8,64,896]{2,1,0:T(8,128)(2,1)} %maximum_bitcast_fusion.pack, bf16[256,2048]{1,0:T(8,128)(2,1)} %convert_element_type.126.down), custom_call_target="tpu_custom_call" | custom-call | bytes 167772160 | tf_op jit(solution)/shard_map/pallas_call | solution.py:909
  94.9 1.5 reshape.374.gate
  97.2 1.5 reshape.376.up
  102.0 1.9 fusion.7
  105.9 2.3 compare_select_fusion
  110.4 110.6 %shard_map.221 = (bf16[1024,2048]{1,0:T(8,128)(2,1)}, bf16[1024,768]{1,0:T(8,128)(2,1)}, bf16[1024,256]{1,0:T(8,128)(2,1)}, f32[1,256]{1,0:T(1,128)}, bf16[4,8,6...) custom-call(bf16[8,128,2176]{2,1,0:T(8,128)(2,1)} %get-tuple-element.62.x_all, ...), custom_call_target="tpu_custom_call" | custom-call | bytes 167772160 | tf_op jit(solution)/shard_map/pallas_call | solution.py:909
  221.1 82.8 %shard_map.222 = (f32[128,2048]{1,0:T(8,128)}, bf16[8,128,2048]{2,1,0:T(8,128)(2,1)}, bf16[4,8,64,1024]{3,2,1,0:T(8,128)(2,1)}) custom-call(bf16[1024,256]{1,0:T(8,128)(2,1)} %get-tuple-element.64.o, bf16[256,2048]{1,0:T(8,128)(2,1)} %bitcast.142, bf16[128,2048]{1,0:T(8,128)(2,1)} %bitcast.123, f32[1,2048]{1,0:T(1,128)} %get-tuple-element.106.gain, ...), custom_call_target="tpu_custom_call" | custom-call | bytes 167772160 | tf_op jit(solution)/shard_map/pallas_call | solution.py:909
  303.9 9.9 %fusion.13 = f32[1024,1024]{1,0:T(8,128)} fusion(bf16[1024,2048]{1,0:T(8,128)(2,1)} %bitcast.134, bf16[2048,1024]{1,0:T(8,128)(2,1)} %bitcast.132), kind=kOutput, calls=%fused_computation.66 | convolution fusion | flops 4294967296 | bytes 12582912 | tf_op jit(solution)/shard_map/dot_general | solution.py:27
  313.8 7.7 %fusion.12 = f32[1024,1024]{1,0:T(8,128)S(1)} fusion(bf16[1024,2048]{1,0:T(8,128)(2,1)} %all-gather.2.cloned.1.call-done, bf16[1024,2048]{1,0:T(8,128)(2,1)} %bitcast.154), kind=kOutput, calls=%fused_computation.65 | convolution fusion | flops 4294967296 | bytes 12582912 | tf_op jit(solution)/shard_map/dot_general | solution.py:27
  321.6 7.4 %multiply_convert_fusion = (bf16[1024,1024]{1,0:T(8,128)(2,1)S(1)}, bf16[1024,1024]{1,0:T(8,128)(2,1)S(1)}, bf16[1024,1024]{1,0:T(8,128)(2,1)}) fusion(f32[1024,1024]{1,0:T(8,128)S(1)} %copy-done.26, f32[1024,1024]{1,0:T(8,128)S(1)} %fusion.12, bf16[1024,2048]{1,0:T(8,128)(2,1)S(1)} %bitcast.136, bf16[2048,1024]{1,0:T(8,128)(2,1)S(1)} %bitcast.138), kind=kOutput, calls=%fused_computation.1 | convolution fusion | flops 4310695936 | bytes 23068672 | tf_op jit(solution)/shard_map/dot_general | solution.py:27
  329.0 1.3 copy-done.24
  330.3 6.1 convolution_convert_fusion.1
  336.4 4.1 pad_maximum_fusion.dgu
  342.5 122.1 %shard_map.223 = (f32[128,2048]{1,0:T(8,128)}, bf16[8,128,2048]{2,1,0:T(8,128)(2,1)}, f32[1,2048]{1,0:T(1,128)}, bf16[8,64,2048]{2,1,0:T(8,128)(2,1)}) custom-call(bf16[1024,2048]{1,0:T(8,128)(2,1)} %bitcast.135, bf16[1024,2048]{1,0:T(8,128)(2,1)} %pad_maximum_fusion.dgu, bf16[2048,1024]{1,0:T(8,128)(2,1)} %bitcast.133, bf16[2048,1024]{1,0:T(8,128)(2,1)} %bitcast.137, ...), custom_call_target="tpu_custom_call" | custom-call | bytes 167772160 | tf_op jit(solution)/shard_map/pallas_call | solution.py:909
  464.6 4.6 convolution_convert_fusion.2
  469.2 2.1 convolution_convert_fusion.3.do
  472.2 6.3 %convolution_convert_fusion = bf16[1024,2048]{1,0:T(8,128)(2,1)} fusion(bf16[1024,1024]{1,0:T(8,128)(2,1)S(1)} %copy-done.25, bf16[1024,2048]{1,0:T(8,128)(2,1)S(1)} %copy-done.19), kind=kOutput, calls=%fused_computation.7 | convolution fusion | flops 4297064448 | bytes 10485760 | tf_op jit(solution)/shard_map/dot_general | solution.py:27
  478.5 88.9 %shard_map.224 = (bf16[128,2048]{1,0:T(8,128)(2,1)}, f32[1,2048]{1,0:T(1,128)}, bf16[8,64,2048]{2,1,0:T(8,128)(2,1)}, bf16[256,2048]{1,0:T(8,128)(2,1)}, bf16[64...) custom-call(bf16[1024,256]{1,0:T(8,128)(2,1)} %convolution_convert_fusion.3.do, ...), custom_call_target="tpu_custom_call" | custom-call | bytes 167772160 | tf_op jit(solution)/shard_map/pallas_call | solution.py:909
  567.9 1.4 reduce.12
  570.9 30.3 %shard_map.225 = (bf16[8,64,768]{2,1,0:T(8,128)(2,1)}, bf16[64,2048]{1,0:T(8,128)(2,1)}, f32[8,128]{1,0:T(8,128)}) custom-call(bf16[8,64,768]{2,1,0:T(8,128)(2,1)} %get-tuple-element.81.qkv, bf16[64,2048]{1,0:T(8,128)(2,1)} %get-tuple-element.82.out, f32[8,4,8,128]{3,2,1,0:T(8,128)} %scatter.4.tot), custom_call_target="tpu_custom_call" | custom-call | bytes 83886080 | tf_op jit(solution)/shard_map/pallas_call | solution.py:909
  603.1 1.6 copy-done
  608.0 3.8 shard_map.226
  611.8 1.3 slice_bitcast_fusion
  613.0 1.9 fusion.1
  (102 shorter events, 26.2 us)
Async XLA Ops:
  7.2 3.5 copy-start.8
  7.2 4.6 copy-start.22
  7.2 4.6 copy-start.23
  7.2 4.8 copy-start.4
  7.2 5.6 copy-start.17
  7.2 5.6 copy-start.18
  7.2 306.6 %all-gather.2.cloned.1.call-start = ((), (), s32[]{:S(2)}) async-start(), calls=%async_computation.1 | async-start | bytes 4718592 | tf_op jit(solution)/shard_map/all_gather | solution.py:946
  11.8 81.5 %copy-start.12 = (f32[64,2048]{1,0:T(8,128)S(1)}, f32[64,2048]{1,0:T(8,128)}, u32[]{:S(2)}) copy-start(f32[64,2048]{1,0:T(8,128)} %param.22) | copy-start | bytes 1572868
  11.8 82.3 %copy-start.9 = (f32[64,8192]{1,0:T(8,128)S(1)}, f32[64,8192]{1,0:T(8,128)}, u32[]{:S(2)}) copy-start(f32[64,8192]{1,0:T(8,128)} %param.23) | copy-start | bytes 6291460
  93.3 519.7 %reduce-scatter.2.cloned.1.call-start = ((), (), s32[]{:S(2)}) async-start(), calls=%async_computation.2 | async-start | bytes 4718592 | tf_op jit(solution)/shard_map/reduce_scatter | solution.py:950
  94.2 2.2 copy-start.10
  313.8 7.8 %copy-start.6 = (bf16[8,128,2048]{2,1,0:T(8,128)(2,1)S(1)}, bf16[8,128,2048]{2,1,0:T(8,128)(2,1)}, u32[]{:S(2)}) copy-start(bf16[8,128,2048]{2,1,0:T(8,128)(2,1)} %get-tuple-element.70) | copy-start | bytes 12582916
  313.8 7.8 %copy-start.7 = (bf16[4,8,64,1024]{3,2,1,0:T(8,128)(2,1)S(1)}, bf16[4,8,64,1024]{3,2,1,0:T(8,128)(2,1)}, u32[]{:S(2)}) copy-start(bf16[4,8,64,1024]{3,2,1,0:T(8,128)(2,1)} %get-tuple-element.71) | copy-start | bytes 12582916
  313.8 7.8 %copy-start.26 = (f32[1024,1024]{1,0:T(8,128)S(1)}, f32[1024,1024]{1,0:T(8,128)}, u32[]{:S(2)}) copy-start(f32[1024,1024]{1,0:T(8,128)} %fusion.13) | copy-start | bytes 12582916
  321.6 8.7 %copy-start.20 = (bf16[4,256,2048]{2,1,0:T(8,128)(2,1)S(1)}, bf16[4,256,2048]{2,1,0:T(8,128)(2,1)}, u32[]{:S(2)}) copy-start(bf16[4,256,2048]{2,1,0:T(8,128)(2,1)} %get-tuple-element.69) | copy-start | bytes 12582916
  342.5 122.1 %copy-start.14 = (bf16[1024,256]{1,0:T(8,128)(2,1)S(1)}, bf16[1024,256]{1,0:T(8,128)(2,1)}, u32[]{:S(2)}) copy-start(bf16[1024,256]{1,0:T(8,128)(2,1)} %get-tuple-element.64.o) | copy-start | bytes 1572868
  464.6 4.6 copy-start.11
  464.6 4.6 copy-start.21
  469.2 2.2 copy-start.19
  469.2 3.1 copy-start.25
  478.5 90.8 %copy-start.15 = (f32[1,2048]{1,0:T(1,128)S(1)}, f32[1,2048]{1,0:T(1,128)}, u32[]{:S(2)}) copy-start(f32[1,2048]{1,0:T(1,128)} %get-tuple-element.84) | copy-start | bytes 24580
  567.4 45.6 %copy-start.5 = (f32[128,2048]{1,0:T(8,128)S(1)}, f32[128,2048]{1,0:T(8,128)}, u32[]{:S(2)}) copy-start(f32[128,2048]{1,0:T(8,128)} %get-tuple-element.67.h1) | copy-start | bytes 3145732
  567.4 47.5 %copy-start.13 = (bf16[128,2048]{1,0:T(8,128)(2,1)S(1)}, bf16[128,2048]{1,0:T(8,128)(2,1)}, u32[]{:S(2)}) copy-start(bf16[128,2048]{1,0:T(8,128)(2,1)} %get-tuple-element.80) | copy-start | bytes 1572868
  603.1 1.6 copy-start
  (5 other events, 5.3 us)
Sparse Core Ops, SparseCore 0:
  93.4 72.5 all-gather.1
  340.6 65.0 reduce-scatter.1

commit v4 on v3

v4 whole, which is shorter than its diff:
```python
import functools
import math

import jax
import jax.numpy as jnp
from jax import lax
from jax.experimental import pallas as pl
from jax.experimental.pallas import tpu as pltpu
from jax.sharding import PartitionSpec as P

HEAD_DIM = 128
norm_eps = 1e-05
rope_base = 10000.0
score_shift = math.log(4096.0)
score_scale = 1.0 / math.sqrt(HEAD_DIM)
contract_rows = (((0,), (0,)), ((), ()))
contract_cols = (((1,), (1,)), ((), ()))
plain = (((1,), (0,)), ((), ()))
f32 = jnp.float32
bf16 = jnp.bfloat16
MESH = pl.DeviceIdType.MESH
ANY = pl.BlockSpec(memory_space=pl.ANY)
VMEM = pl.BlockSpec(memory_space=pltpu.VMEM)


def dot(a, b, dims=plain):
    return lax.dot_general(a, b, dims, preferred_element_type=f32)


def remote(src, dst, send, recv, target):
    return pltpu.make_async_remote_copy(
        src_ref=src,
        dst_ref=dst,
        send_sem=send,
        recv_sem=recv,
        device_id=target,
        device_id_type=MESH,
    )


def greet(target):
    pl.semaphore_signal(
        pltpu.get_barrier_semaphore(), inc=1, device_id=target, device_id_type=MESH
    )


def by_rows(count, work, step=16):
    @pl.loop(0, count // step)
    def _(i):
        work(pl.ds(pl.multiple_of(i * step, step), step))


def place(cn):
    c = lax.axis_index("ctx")
    j, k = c // 2, c % 2
    return c, j, k, cn // 2, 2 * j + 1 - k


def greet_line(cn, ring):
    c, j, _, n, sib = place(cn)
    ring.greet()
    greet({"ctx": sib})

    @pl.when(j < n - 1)
    def _():
        greet({"ctx": c + 2})

    @pl.when(j > 0)
    def _():
        greet({"ctx": c - 2})

    inner = jnp.where(j > 0, 1, 0) + jnp.where(j < n - 1, 1, 0)
    pl.semaphore_wait(pltpu.get_barrier_semaphore(), 3 + inner)


def greet_ctx(cn):
    c = lax.axis_index("ctx")
    for s in range(1, cn):
        greet({"ctx": lax.rem(c + s, cn)})


class LineGather:
    def __init__(self, cn, own, full, sem):
        self.cn, self.own, self.full, self.sem = cn, own, full, sem

    def copy(self, src, origin, kind, target):
        _, _, k, _, _ = place(self.cn)
        sem = self.sem
        return remote(
            src,
            self.full.at[2 * origin + k],
            sem.at[kind, origin],
            sem.at[3 if kind < 2 else 4, origin],
            {"ctx": target},
        )

    def start(self):
        c, j, _, n, sib = place(self.cn)

        @pl.when(j < n - 1)
        def _():
            self.copy(self.own, j, 0, c + 2).start()

        @pl.when(j > 0)
        def _():
            self.copy(self.own, j, 1, c - 2).start()

        self.copy(self.own, j, 2, sib).start()

    def step(self, s):
        c, j, k, n, sib = place(self.cn)

        @pl.when(j - s >= 0)
        def _():
            o = j - s
            block = self.full.at[2 * o + k]
            self.copy(block, o, 0, sib).wait_recv()

            @pl.when(j < n - 1)
            def _():
                self.copy(block, o, 0, c + 2).start()

            self.copy(block, o, 2, sib).start()

        @pl.when(j + s <= n - 1)
        def _():
            o = j + s
            block = self.full.at[2 * o + k]
            self.copy(block, o, 1, sib).wait_recv()

            @pl.when(j > 0)
            def _():
                self.copy(block, o, 1, c - 2).start()

            self.copy(block, o, 2, sib).start()

    def forward(self, first=1, last=None):
        for s in range(first, self.cn // 2 if last is None else last + 1):
            self.step(s)

    def other(self, o):
        _, _, k, _, sib = place(self.cn)
        block = self.full.at[2 * o + 1 - k]
        remote(
            block, block, self.sem.at[2, o], self.sem.at[4, o], {"ctx": sib}
        ).wait_recv()

    def sent(self):
        c, j, k, n, sib = place(self.cn)
        for o in range(n):
            block = self.full.at[2 * o + k]

            @pl.when((j < n - 1) & (o <= j))
            def _():
                self.copy(block, o, 0, sib).wait_send()

            @pl.when((j > 0) & (o >= j))
            def _():
                self.copy(block, o, 1, sib).wait_send()

            self.copy(block, o, 2, sib).wait_send()

    def finish(self):
        for o in range(self.cn // 2):
            self.other(o)
        self.sent()


class Swap:
    def __init__(self, cn, src, dst, sem, local, pick=None):
        self.cn, self.sem, self.local = cn, sem, local
        self.src = pick or (lambda c: src.at[c])
        self.dst = dst if callable(dst) else lambda c: dst.at[c]

    def copy(self, s):
        c = lax.axis_index("ctx")
        peer = lax.rem(c + s, self.cn)
        return remote(
            self.src(peer),
            self.dst(c),
            self.sem.at[0, s],
            self.sem.at[1, s],
            {"ctx": peer},
        )

    def start(self):
        c = lax.axis_index("ctx")
        for s in range(1, self.cn):
            self.copy(s).start()
        pltpu.make_async_copy(self.src(c), self.dst(c), self.local).start()

    def receive(self, s):
        c = lax.axis_index("ctx")
        if s == 0:
            pltpu.make_async_copy(self.src(c), self.dst(c), self.local).wait()
            return c
        source = lax.rem(c - s + self.cn, self.cn)
        block = self.dst(source)
        remote(
            block, block, self.sem.at[0, s], self.sem.at[1, s], {"ctx": source}
        ).wait_recv()
        return source

    def sent(self):
        for s in range(1, self.cn):
            self.copy(s).wait_send()

    def finish(self):
        for s in range(self.cn):
            self.receive(s)
        self.sent()


class RingGather:
    def __init__(self, dpn, own, full, sem):
        self.dpn, self.own, self.full, self.sem = dpn, own, full, sem
        self.hops = dpn // 2
        d = lax.axis_index("dp")
        self.p = d // 2 * 2 + lax.rem(lax.rem(d, 2) + d // 2, 2)

    def member(self, step):
        p = lax.rem(self.p + step + self.dpn, self.dpn)
        return p // 2 * 2 + lax.rem(lax.rem(p, 2) + p // 2, 2)

    def half(self, ref, h, right):
        if h < self.hops:
            return ref
        m = self.full.shape[1] // 2
        if len(self.full.shape) == 3 and m % 16:
            m = self.full.shape[2] // 2
            return ref.at[:, pl.ds(0 if right else m, m)]
        return ref.at[pl.ds(0 if right else m, m)]

    def copy(self, h, right):
        way = 1 if right else -1
        origin = self.member(-way * (h - 1))
        src = self.own if h == 1 else self.full.at[origin]
        return remote(
            self.half(src, h, right),
            self.half(self.full.at[origin], h, right),
            self.sem.at[0 if right else 1, h],
            self.sem.at[2 if right else 3, h],
            {"dp": self.member(way)},
        )

    def arrival(self, h, right):
        way = 1 if right else -1
        block = self.half(self.full.at[self.member(-way * h)], h, right)
        return remote(
            block,
            block,
            self.sem.at[0 if right else 1, h],
            self.sem.at[2 if right else 3, h],
            {"dp": self.member(way)},
        )

    def greet(self):
        greet({"dp": self.member(1)})
        greet({"dp": self.member(-1)})

    def start(self):
        self.copy(1, True).start()
        self.copy(1, False).start()

    def forward(self):
        for h in range(1, self.hops):
            for right in (True, False):
                self.arrival(h, right).wait_recv()
                self.copy(h + 1, right).start()

    def finish(self):
        for right in (True, False):
            self.arrival(self.hops, right).wait_recv()
        for h in range(1, self.hops + 1):
            for right in (True, False):
                self.copy(h, right).wait_send()


class RingPieces(RingGather):
    def __init__(self, dpn, full, sem):
        super().__init__(dpn, None, full, sem)

    def piece(self, i, h, right, back):
        way = 1 if right else -1
        ref = self.full.at[self.member(-way * back), i]
        return remote(
            ref,
            ref,
            self.sem.at[0 if right else 1, h, i],
            self.sem.at[2 if right else 3, h, i],
            {"dp": self.member(way)},
        )

    def moves(self, i, h, right, act):
        if h < self.hops:
            act()
        else:
            first = i < self.full.shape[1] // 2
            pl.when(first if right else jnp.logical_not(first))(act)

    def start(self, i):
        for right in (True, False):
            self.moves(i, 1, right, lambda r=right: self.piece(i, 1, r, 0).start())

    def forward(self, i):
        for h in range(1, self.hops):
            for right in (True, False):
                self.piece(i, h, right, h).wait_recv()
                self.moves(
                    i, h + 1, right, lambda h=h, r=right: self.piece(i, h + 1, r, h).start()
                )

    def finish(self, i):
        for right in (True, False):
            h = self.hops
            self.moves(i, h, right, lambda r=right: self.piece(i, h, r, h).wait_recv())
        for h in range(1, self.hops + 1):
            for right in (True, False):
                self.moves(
                    i, h, right, lambda h=h, r=right: self.piece(i, h, r, h - 1).wait_send()
                )


class RingSum:
    def __init__(self, dpn, blocks, got, got_half, sem):
        self.dpn, self.blocks, self.sem = dpn, blocks, sem
        self.got, self.got_half = got, got_half
        self.ring = RingGather(dpn, None, blocks, sem)
        self.hops = dpn // 2

    def part(self, s, right):
        m, width = self.blocks.shape[1:]
        if s > 1:
            return 0, m, pl.ds(0, width)
        if (m // 2) % 16:
            return 0, m, pl.ds(0 if right else width // 2, width // 2)
        return 0 if right else m // 2, m // 2, pl.ds(0, width)

    def copy(self, s, right):
        way = 1 if right else -1
        target = self.ring.member(way * (self.hops - s + 1))
        start, size, lanes = self.part(s, right)
        return remote(
            self.blocks.at[target, pl.ds(start, size), lanes],
            self.arrived(s, right),
            self.sem.at[0 if right else 1, s],
            self.sem.at[2 if right else 3, s],
            {"dp": self.ring.member(way)},
        )

    def arrived(self, s, right):
        side = 0 if right else 1
        return self.got_half.at[side] if s == 1 else self.got.at[side, s - 2]

    def order(self):
        out = [self.ring.member(self.hops)]
        for s in range(self.hops - 1, 0, -1):
            out += [self.ring.member(s), self.ring.member(-s)]
        return out + [self.ring.member(0)]

    def start(self):
        self.copy(1, True).start()
        self.copy(1, False).start()

    def take(self, s, right, target):
        self.copy(s, right).wait_recv()
        start, size, lanes = self.part(s, right)
        block = self.blocks.at[target, pl.ds(start, size), lanes]
        came = self.arrived(s, right)

        def add(r):
            block[r, :] = (block[r, :].astype(f32) + came[r, :].astype(f32)).astype(bf16)

        by_rows(size, add)

    def forward(self, s):
        for right in (True, False):
            way = 1 if right else -1
            self.take(s, right, self.ring.member(way * (self.hops - s)))
            self.copy(s + 1, right).start()

    def finish(self, out):
        for right in (True, False):
            self.copy(self.hops, right).wait_recv()
        mine = self.ring.member(0)
        ends = [self.arrived(self.hops, right) for right in (True, False)]
        per = out.shape[-2]

        @pl.loop(0, self.blocks.shape[1] // 16)
        def _(i):
            r = pl.ds(pl.multiple_of(i * 16, 16), 16)
            total = self.blocks[mine, r, :].astype(f32)
            for end in ends:
                total = total + end[r, :].astype(f32)
            if len(out.shape) == 3:
                to = pl.ds(pl.multiple_of(lax.rem(i * 16, per), 16), 16)
                out[i * 16 // per, to, :] = total.astype(out.dtype)
            else:
                out[r, :] = total.astype(out.dtype)

        for s in range(1, self.hops + 1):
            for right in (True, False):
                self.copy(s, right).wait_send()


def ring_scratch(dpn, m, width):
    return [
        pltpu.VMEM((dpn, m, width), bf16),
        pltpu.VMEM((2, dpn // 2 - 1, m, width), bf16),
        pltpu.VMEM((2, m // 2, width) if m % 32 == 0 else (2, m, width // 2), bf16),
        pltpu.SemaphoreType.DMA((4, dpn // 2 + 1)),
    ]


def outer(a_ref, b_ref, out, at, tile=512):
    a = a_ref[:, at]
    width = out.shape[-1]
    for lo in range(0, width, tile):
        to = slice(lo, min(lo + tile, width))
        out[:, to] = dot(a, b_ref[:, to], contract_rows).astype(bf16)


def outer_all(a_ref, staged, halves, blocks, tile=512):
    count, m, width = blocks.shape
    many = max(1, 128 // m)
    for first in range(0, count, many):
        at = slice(first * m, (first + many) * m)
        for lo in range(0, width, tile):
            to = slice(lo, min(lo + tile, width))
            part = dot(a_ref[halves[0], at], staged(0, to), contract_rows)
            part = part + dot(a_ref[halves[1], at], staged(1, to), contract_rows)
            part = part.astype(bf16)
            for i in range(many):
                blocks[first + i, :, to] = part[i * m : (i + 1) * m]


class LineSum:
    def __init__(self, cn, compute, part, cross, cross_in, flow, arrived, sem):
        self.cn, self.compute, self.part = cn, compute, part
        self.cross, self.cross_in, self.flow = cross, cross_in, flow
        self.arrived, self.sem = arrived, sem

    def across(self, t):
        _, _, _, _, sib = place(self.cn)
        return remote(
            self.cross.at[t],
            self.cross_in.at[t],
            self.sem.at[0, t],
            self.sem.at[2, t],
            {"ctx": sib},
        )

    def along(self, t, slot, target):
        return remote(
            self.flow.at[t],
            self.arrived.at[slot],
            self.sem.at[1, t],
            self.sem.at[3, slot],
            {"ctx": target},
        )

    def produce(self, t, slot):
        _, _, k, _, _ = place(self.cn)
        part = self.part.at[slot]
        self.compute(t, part)

        def low(r):
            self.cross[t, r, :] = part[1 - k, r, :].astype(bf16)

        by_rows(self.cross.shape[1], low)
        self.across(t).start()

    def add(self, part, came):
        def more(r):
            part[r, :] += came[r, :].astype(f32)

        by_rows(part.shape[0], more)

    def collect(self, t, slot):
        _, j, k, n, sib = place(self.cn)
        part = self.part.at[slot, k]
        self.across(t).wait_recv()
        self.add(part, self.cross_in.at[t])

        @pl.when((j > 0) & (t >= j))
        def _():
            self.along(t, t, sib).wait_recv()
            self.add(part, self.arrived.at[t])

        @pl.when((j < n - 1) & (t <= j))
        def _():
            slot_in = jnp.where(t == j, n, t)
            self.along(t, slot_in, sib).wait_recv()
            self.add(part, self.arrived.at[slot_in])

    def send(self, t, slot, up):
        c, j, k, n, _ = place(self.cn)

        def low(r):
            self.flow[t, r, :] = self.part[slot, k, r, :].astype(bf16)

        by_rows(self.flow.shape[1], low)
        there = t if up else jnp.where(t == j - 1, n, t)
        self.along(t, there, c + 2 if up else c - 2).start()

    def drain(self):
        _, j, _, n, sib = place(self.cn)

        @pl.loop(0, n)
        def _(t):
            self.across(t).wait_send()

            @pl.when(t != j)
            def _():
                self.along(t, t, sib).wait_send()


class LineSumRows(LineSum):
    def __init__(self, cn, terms, stage, loads, *refs):
        super().__init__(cn, None, *refs)
        self.terms, self.stage, self.loads = terms, stage, loads

    def produce(self, t, slot):
        _, _, k, _, _ = place(self.cn)
        other = pltpu.make_async_copy(
            self.terms.at[2 * t + 1 - k], self.cross.at[t], self.loads.at[0]
        )
        own = pltpu.make_async_copy(self.terms.at[2 * t + k], self.stage, self.loads.at[1])
        other.start()
        own.start()
        other.wait()
        self.across(t).start()
        own.wait()

        def wide(r):
            self.part[slot, k, r, :] = self.stage[r, :].astype(f32)

        by_rows(self.stage.shape[0], wide)


def line_sums(cn, sums, between=None):
    _, j, _, n, _ = place(cn)

    @pl.loop(0, n - 1)
    def _(s):
        to_up, to_down = n - 1 - s + j, s - (n - 1 - j)
        for total in sums:

            @pl.when(s >= j)
            def _():
                total.produce(to_up, 0)

            @pl.when(s >= n - 1 - j)
            def _():
                total.produce(to_down, 1)

        for total in sums:

            @pl.when(s >= j)
            def _():
                total.collect(to_up, 0)
                total.send(to_up, 0, True)

            @pl.when(s >= n - 1 - j)
            def _():
                total.collect(to_down, 1)
                total.send(to_down, 1, False)

        if between is not None:
            between(s)

    for total in sums:
        total.produce(j, 0)
    for total in sums:
        total.collect(j, 0)


def sum_scratch(cn, rows, width):
    n = cn // 2
    return [
        pltpu.VMEM((2, 2, rows, width), f32),
        pltpu.VMEM((n, rows, width), bf16),
        pltpu.VMEM((n, rows, width), bf16),
        pltpu.VMEM((n, rows, width), bf16),
        pltpu.VMEM((n + 1, rows, width), bf16),
        pltpu.SemaphoreType.DMA((4, n + 1)),
    ]


def product(a_ref, b_ref, dims, rows, width):
    tile = min(512, width)

    def compute(t, out):
        a = a_ref[pl.ds(pl.multiple_of(t * 2 * rows, 2 * rows), 2 * rows), :]

        @pl.loop(0, width // tile)
        def _(i):
            at = pl.ds(pl.multiple_of(i * tile, tile), tile)
            b = b_ref[:, at] if dims == plain else b_ref[at, 0 : a_ref.shape[1]]
            out[:, :, at] = dot(a, b, dims).reshape(2, rows, tile)

    return compute


def rms(v):
    return lax.rsqrt(jnp.mean(v * v, axis=-1, keepdims=True) + norm_eps)


def front_kernel(
    cn, dpn, x, wq, wk, wv, gains, wo, gate_in, up_in, down_in,
    x_all, pack_all, gate, up, down_all, wo_low,
    pack, wide, tall, down, gsem, ssem, rsem, dsem, local,
):
    c, d = lax.axis_index("ctx"), lax.axis_index("dp")
    hw = wq.shape[1] // cn
    part = gate_in.shape[1] // (cn * dpn)
    mine = pack_all.at[d]
    swap = Swap(cn, pack, mine, ssem, local.at[0])
    gather = LineGather(cn, x, x_all, gsem)
    ring = RingPieces(dpn, pack_all, rsem)
    down_ring = RingGather(dpn, down, down_all, dsem)
    greet_ctx(cn)
    ring.greet()
    loads = [
        pltpu.make_async_copy(src, dst, local.at[i])
        for i, (src, dst) in enumerate(
            ((gate_in, wide.at[0]), (up_in, wide.at[1]), (down_in, tall)), 2
        )
    ]
    for load in loads:
        load.start()
    for to in range(cn):
        for i, w in enumerate((wq, wk, wv)):
            pack[to, :, i * hw : (i + 1) * hw] = w[:, to * hw : (to + 1) * hw].astype(bf16)
        pack[to, :, 3 * hw :] = gains[...]
    pl.semaphore_wait(pltpu.get_barrier_semaphore(), cn - 1 + 2)
    swap.start()
    gather.start()
    loads[2].wait()
    down[...] = tall[...].astype(bf16)
    down_ring.start()
    keep_down = pltpu.make_async_copy(down, down_all.at[d], local.at[5])
    keep_down.start()
    keep = pltpu.make_async_copy(x, x_all.at[c], local.at[1])
    keep.start()
    wo_low[...] = wo[...].astype(bf16)

    def lay(i, out):
        loads[i].wait()
        for to in range(cn):
            for row in range(dpn):
                lo = (row * cn + to) * part
                out[to, :, row * part : (row + 1) * part] = wide[i, :, lo : lo + part].astype(bf16)

    half = cn // 2
    sources = [swap.receive(0)]
    ring.start(sources[0])
    lay(0, gate)
    for s in range(1, half):
        sources.append(swap.receive(s))
        ring.start(sources[s])
    gather.forward(1, 1)
    lay(1, up)
    for s in range(half, cn):
        sources.append(swap.receive(s))
        ring.start(sources[s])
    down_ring.forward()
    gather.forward(2, 2)
    for source in sources:
        ring.forward(source)
    gather.forward(3)
    keep.wait()
    keep_down.wait()
    gather.finish()
    for source in sources:
        ring.finish(source)
    swap.sent()
    down_ring.finish()


def prepare(w, x_all, gains, info_rows, hw, block):
    width = w.shape[0]
    per = block // x_all.shape[1]

    @pl.loop(0, width // block)
    def _(i):
        at = pl.ds(pl.multiple_of(i * block, block), block)
        gains[:, at] = w[at, 3 * hw : 3 * hw + 128].astype(f32).T[0:8]

    @pl.loop(0, info_rows.shape[1] // block)
    def _(i):
        at = pl.ds(pl.multiple_of(i * block, block), block)
        codes = x_all[pl.ds(i * per, per), :, width:].reshape(block, 128).astype(f32).T[0:8]
        seg = jnp.floor(codes * 0.5)
        code = jnp.where(codes - 2.0 * seg == 1.0, seg, -1.0)
        first = lax.broadcasted_iota(jnp.int32, (8, block), 0) == 0
        info_rows[:, at] = jnp.where(first, seg, code)


def tables(x_all, inverse, info_rows, info_cols, cosines, sines, width, i, block):
    per = block // x_all.shape[1]
    at = pl.ds(pl.multiple_of(i * block, block), block)
    codes = x_all[pl.ds(i * per, per), :, width:].reshape(block, 128).astype(f32)
    seg = jnp.floor(codes * 0.5)
    valid = codes - 2.0 * seg
    lane = lax.broadcasted_iota(jnp.int32, (block, 128), 1)
    code = jnp.where(valid == 1.0, seg, -1.0)
    info_cols[at, :] = jnp.where(lane == 0, seg, jnp.where(lane == 1, valid, code))
    before = jnp.where(info_rows[0:1, :] < seg[:, 0:1], 1.0, 0.0)
    index = lax.broadcasted_iota(jnp.int32, (block, 128), 0) + i * block
    place_in = index.astype(f32) - jnp.sum(before, axis=1, keepdims=True)
    angles = place_in * inverse[...]
    cosines[at, :] = jnp.cos(angles)
    sines[at, :] = jnp.where(lane < HEAD_DIM // 2, -1.0, 1.0) * jnp.sin(angles)


def project(x_all, w, gain, inverse, rows_in, cols, cosines, sines, an, qkv, hw, block, hook):
    width = an.shape[1]
    per = block // x_all.shape[1]

    @pl.loop(0, an.shape[0] // block)
    def _(i):
        at = pl.ds(pl.multiple_of(i * block, block), block)
        tables(x_all, inverse, rows_in, cols, cosines, sines, width, i, block)
        x = x_all[pl.ds(i * per, per), :, 0:width].reshape(block, width).astype(f32)
        normed = (x * rms(x) * gain[...]).astype(bf16)
        an[at, :] = normed
        proj = dot(normed, w[:, 0 : 3 * hw])
        cos_b, sin_b = cosines[at, :], sines[at, :]
        for h in range(2 * hw // HEAD_DIM):
            lanes = slice(h * HEAD_DIM, (h + 1) * HEAD_DIM)
            v = proj[:, lanes]
            turned = v * cos_b + pltpu.roll(v, HEAD_DIM // 2, 1) * sin_b
            qkv[at, lanes] = turned.astype(bf16)
        qkv[at, 2 * hw :] = proj[:, 2 * hw :].astype(bf16)
        hook(i)


def mask_block(q_seg, k_code, i, j, block):
    rows = lax.broadcasted_iota(jnp.int32, (block, block), 0) + i * block
    cols = lax.broadcasted_iota(jnp.int32, (block, block), 1) + j * block
    return (q_seg == k_code) & (cols <= rows)


def attend(qkv, q_info, k_code, out, mass, hw, block, hook):
    mass[...] = jnp.zeros_like(mass)

    @pl.loop(0, qkv.shape[0] // block)
    def _(i):
        at = pl.ds(pl.multiple_of(i * block, block), block)
        q_seg, q_valid = q_info[at, 0:1], q_info[at, 1:2]
        for h in range(hw // HEAD_DIM):
            lane = [slice(t * hw + h * HEAD_DIM, t * hw + (h + 1) * HEAD_DIM) for t in range(3)]
            q = qkv[at, lane[0]]

            def step(j, acc):
                to = pl.ds(pl.multiple_of(j * block, block), block)
                s = dot(q, qkv[to, lane[1]], contract_cols) * score_scale - score_shift
                allowed = mask_block(q_seg, k_code[1:2, to], i, j, block)
                p = jnp.where(allowed, jax.nn.sigmoid(s), 0.0)
                mass[...] += jnp.sum(p * q_valid, axis=0, keepdims=True)
                return acc + dot(p.astype(bf16), qkv[to, lane[2]])

            acc = lax.fori_loop(0, i + 1, step, jnp.zeros((block, HEAD_DIM), f32))
            out[at, lane[0]] = acc.astype(bf16)
        hook(i)


def attn_kernel(
    cn, dpn, x_all, w, inverse, gate, up, wo,
    an, qkv, o, mass, gains, cosines, sines, cols, rows_in,
    gate_all, up_own, wo_all, ssem, rsem, hsem, wsem, local,
):
    c, d = lax.axis_index("ctx"), lax.axis_index("dp")
    mine, wanted = d * cn + c, c * dpn + d
    stays = mine == wanted
    hop = remote(
        wo,
        wo_all.at[lax.rem(mine, dpn)],
        hsem.at[0],
        hsem.at[1],
        {"dp": lax.rem(mine, dpn), "ctx": mine // dpn},
    )
    keep = pltpu.make_async_copy(wo, wo_all.at[d], local.at[2])
    wo_ring = RingGather(dpn, wo_all.at[d], wo_all, wsem)
    rows = x_all.shape[1]
    hw = qkv.shape[1] // 3
    swap_gate = Swap(cn, gate, gate_all.at[d], ssem.at[0], local.at[0])
    swap_up = Swap(cn, up, up_own, ssem.at[1], local.at[1])
    ring = RingPieces(dpn, gate_all, rsem)
    sources = [lax.rem(c - s + cn, cn) for s in range(cn)]
    greet_ctx(cn)
    ring.greet()

    @pl.when(jnp.logical_not(stays))
    def _():
        greet({"dp": wanted // cn, "ctx": lax.rem(wanted, cn)})

    pl.semaphore_wait(
        pltpu.get_barrier_semaphore(), cn - 1 + 2 + jnp.where(stays, 0, 1)
    )

    @pl.when(stays)
    def _():
        keep.start()
        keep.wait()

    @pl.when(jnp.logical_not(stays))
    def _():
        hop.start()

    swap_gate.start()

    def hop_done():
        @pl.when(jnp.logical_not(stays))
        def _():
            arrived = wo_all.at[d]
            remote(arrived, arrived, hsem.at[0], hsem.at[1], {"dp": d, "ctx": c}).wait_recv()

        wo_ring.start()

    def in_project(i):
        pl.when(i == 0)(hop_done)

        @pl.when(i == 1)
        def _():
            for s in range(cn // 2):
                ring.start(swap_gate.receive(s))

        @pl.when(i == 2)
        def _():
            for s in range(cn // 2, cn):
                ring.start(swap_gate.receive(s))
            swap_up.start()

    def in_attend(i):
        @pl.when(i == 1)
        def _():
            wo_ring.forward()

        @pl.when(i == 2)
        def _():
            for source in sources[: cn // 2]:
                ring.forward(source)

    prepare(w, x_all, gains, rows_in, hw, 2 * rows)
    project(
        x_all, w, gains.at[0:1], inverse, rows_in, cols, cosines, sines, an, qkv, hw, 2 * rows,
        in_project,
    )
    attend(qkv, cols, rows_in, o, mass, hw, 2 * rows, in_attend)
    for source in sources[cn // 2 :]:
        ring.forward(source)
    swap_up.finish()
    wo_ring.finish()
    for source in sources:
        ring.finish(source)
    swap_gate.sent()

    @pl.when(jnp.logical_not(stays))
    def _():
        hop.wait_send()


def middle_kernel(
    cn, dpn, o, wo, x, gain, dy, up, gate_all, down_all,
    h1, bn_all, up_all, hid, dgu, branch_all, dys_all,
    own, bn, dys, wg, wu, down, branch, gsem, ysem, rsem, local, *sum_refs,
):
    c, d = lax.axis_index("ctx"), lax.axis_index("dp")
    _, j, k, n, _ = place(cn)
    rows, width = x.shape
    ff = hid.shape[1]
    block = 2 * rows
    gather = LineGather(cn, own, bn, gsem)
    gather_dy = LineGather(cn, dy, dys, ysem)
    ring = RingGather(dpn, up, up_all, rsem)
    total = LineSum(cn, product(o, wo, plain, rows, width), *sum_refs)
    greet_line(cn, ring)
    ring.start()
    keep_up = pltpu.make_async_copy(up, up_all.at[d], local.at[0])
    loads = [
        pltpu.make_async_copy(src, dst, local.at[i])
        for i, (src, dst) in enumerate(((gate_all, wg), (down_all, down)), 2)
    ]
    keep_up.start()
    for load in loads:
        load.start()
    gather_dy.start()
    dys[c] = dy[...]

    def between(s):
        gather_dy.step(s + 1)

        @pl.when(s == n - 2)
        def _():
            ring.forward()

    line_sums(cn, [total], between)

    def norm(r):
        mid = x[r, :].astype(f32) + total.part[0, k, r, :]
        h1[r, :] = mid
        own[r, :] = (mid * rms(mid) * gain[1:2, :]).astype(bf16)

    by_rows(rows, norm)
    gather.start()
    bn[c] = own[...]
    gather_dy.finish()
    store_dy = pltpu.make_async_copy(dys, dys_all, local.at[4])
    store_dy.start()
    total.drain()
    keep_up.wait()
    for load in loads:
        load.wait()
    ring.finish()
    load_up = pltpu.make_async_copy(up_all, wu, local.at[0])
    load_up.start()
    load_up.wait()
    wgate, wup = wg, wu.reshape(width, ff)
    tile = min(512, ff)
    wide = min(512, width)

    def feed(t):
        gather.other(t)
        at = pl.ds(pl.multiple_of(t * block, block), block)
        pair = pl.ds(t * 2, 2)
        send = pltpu.make_async_copy(bn.at[pair], bn_all.at[pair], local.at[1])
        send.start()
        a = bn[pair].reshape(block, width)
        g_out = dys[pair].reshape(block, width)

        @pl.loop(0, ff // tile)
        def _(i):
            to = pl.ds(pl.multiple_of(i * tile, tile), tile)
            gate = dot(a, wgate[:, to])
            up_v = dot(a, wup[:, to])
            dhid = dot(g_out, down[to, :], contract_cols)
            sig = jax.nn.sigmoid(gate)
            silu = gate * sig
            hid[at, to] = (silu * up_v).astype(bf16)
            dgate = dhid * up_v * sig * (1.0 + gate * (1.0 - sig))
            dgu[at, to] = dgate.astype(bf16)
            dgu[at, pl.ds(pl.multiple_of(ff + i * tile, tile), tile)] = (dhid * silu).astype(bf16)

        h = hid[at, :]

        @pl.loop(0, width // wide)
        def _(i):
            to = pl.ds(pl.multiple_of(i * wide, wide), wide)
            branch[:, to] = dot(h, down[:, to]).astype(bf16)

        out = pltpu.make_async_copy(branch, branch_all.at[at], local.at[0])
        out.start()
        out.wait()
        send.wait()

    feed(j)

    @pl.loop(1, n)
    def _(s):
        gather.step(s)

        @pl.when(j - s >= 0)
        def _():
            feed(j - s)

        @pl.when(j + s <= n - 1)
        def _():
            feed(j + s)

    gather.sent()
    store_dy.wait()


def back_kernel(
    cn, dpn, bn, dgu, wg, wu, h1, dy, gain, branch_all, dh1, dob_all, term, g_own, result,
    own, branch, cross_in, arrived, bsem, gsem, loads, keep_sem, *scratch,
):
    sum_refs, ring_refs = scratch[:-4], scratch[-4:]
    rows, width = dy.shape
    ff = wg.shape[1]
    tile = min(512, width)
    c, _, k, n, _ = place(cn)

    def compute(t, out):
        at = pl.ds(pl.multiple_of(t * 2 * rows, 2 * rows), 2 * rows)

        @pl.loop(0, width // tile)
        def _(i):
            to = pl.ds(pl.multiple_of(i * tile, tile), tile)
            part = dot(dgu[at, 0:ff], wg[to, :], contract_cols)
            part = part + dot(dgu[at, ff:], wu[to, :], contract_cols)
            out[:, :, to] = part.reshape(2, rows, tile)

    total = LineSum(cn, compute, *sum_refs)
    ring = RingSum(dpn, *ring_refs)
    blocks = ring_refs[0]
    m = blocks.shape[1]
    greet_line(cn, ring.ring)
    order = ring.order()

    def weight_grad(member):
        outer(bn, dgu, blocks.at[member], pl.ds(pl.multiple_of(member * m, m), m))

    weight_grad(order[0])
    ring.start()

    def between(s):
        for i in range(ring.hops - 1):

            @pl.when(s == min(i, n - 2))
            def _():
                weight_grad(order[1 + 2 * i])
                weight_grad(order[2 + 2 * i])

            @pl.when(s == min(i + 1, n - 2))
            def _():
                ring.forward(i + 1)

    line_sums(cn, [total], between)
    term[...] = jnp.zeros_like(term)

    def norm_back(r):
        dbn = total.part[0, k, r, :]
        mid = h1[r, :]
        r2 = rms(mid)
        xh2 = mid * r2
        term[...] += jnp.sum(dbn * xh2, axis=0, keepdims=True)
        u2 = dbn * gain[1:2, :]
        mean = jnp.mean(u2 * xh2, axis=-1, keepdims=True)
        grad = dy[r, :].astype(f32) + r2 * (u2 - xh2 * mean)
        dh1[r, :] = grad
        own[r, :] = grad.astype(bf16)

    by_rows(rows, norm_back)
    gather = LineGather(cn, own, dob_all, gsem)
    gather.start()
    keep = pltpu.make_async_copy(own, dob_all.at[c], keep_sem)
    keep.start()
    total.drain()

    part, cross, _, flow, _, _ = sum_refs
    second = LineSumRows(
        cn, branch_all, branch, loads, part, cross, cross_in, flow, arrived, bsem
    )

    def pass_on(s):
        gather.step(s + 1)

        @pl.when(s == 0)
        def _():
            weight_grad(order[-1])

    line_sums(cn, [second], pass_on)

    def close(r):
        result[r, :] = (h1[r, :] + second.part[0, k, r, :]).astype(bf16)

    by_rows(rows, close)
    second.drain()
    keep.wait()
    gather.finish()
    ring.finish(g_own)


def attend_back(qkv, do, cosines, sines, q_info, k_info, dq, dqkv, hw, block):
    count = qkv.shape[0] // block
    dq[...] = jnp.zeros_like(dq)

    def turn_back(g, at):
        return g * cosines[at, :] - pltpu.roll(g, HEAD_DIM // 2, 1) * sines[at, :]

    @pl.loop(0, count)
    def _(j):
        to = pl.ds(pl.multiple_of(j * block, block), block)
        k_code = k_info[to, 2:3]
        for h in range(hw // HEAD_DIM):
            lane = [slice(t * hw + h * HEAD_DIM, t * hw + (h + 1) * HEAD_DIM) for t in range(3)]
            k, v = qkv[to, lane[1]], qkv[to, lane[2]]

            def step(i, carry):
                dk, dv = carry
                at = pl.ds(pl.multiple_of(i * block, block), block)
                q, do_i = qkv[at, lane[0]], do[at, lane[0]]
                s = dot(k, q, contract_cols) * score_scale - score_shift
                keys = lax.broadcasted_iota(jnp.int32, (block, block), 0) + j * block
                queries = lax.broadcasted_iota(jnp.int32, (block, block), 1) + i * block
                allowed = (k_code == q_info[0:1, at]) & (keys <= queries)
                sg = jnp.where(allowed, jax.nn.sigmoid(s), 0.0)
                dp = dot(v, do_i, contract_cols)
                ds = (dp * sg * (1.0 - sg)).astype(bf16)
                dq[at, lane[0]] += dot(ds, k, contract_rows)
                return dk + dot(ds, q), dv + dot(sg.astype(bf16), do_i)

            zero = jnp.zeros((block, HEAD_DIM), f32)
            dk, dv = lax.fori_loop(j, count, step, (zero, zero))
            dqkv[to, lane[1]] = turn_back(dk * score_scale, to).astype(bf16)
            dqkv[to, lane[2]] = dv.astype(bf16)

    @pl.loop(0, count)
    def _(i):
        at = pl.ds(pl.multiple_of(i * block, block), block)
        for h in range(hw // HEAD_DIM):
            lanes = slice(h * HEAD_DIM, (h + 1) * HEAD_DIM)
            dqkv[at, lanes] = turn_back(dq[at, lanes] * score_scale, at).astype(bf16)


def last_kernel(
    cn, dpn, g_gu, dob_all, dys_all, hid, o, wo, qkv, cosines, sines, q_info, k_info, an, w,
    dh1, x, gain, term_two, mass, grad_in, tot_out, gu_all, down_own, out_all, qkv_all,
    do, dq, dqkv, out_own, qkv_own, tot, tot_in, tot_sum, tot_last,
    usem, qsem, tsem, psem, osem, local, *scratch,
):
    sum_refs, rings = scratch[:-12], (scratch[-12:-8], scratch[-8:-4], scratch[-4:])
    rows, width = x.shape
    hw = width // cn
    _, _, k, n, _ = place(cn)
    down_ring, out_ring, qkv_ring = (RingSum(dpn, *refs) for refs in rings)
    swap_gu = Swap(cn, g_gu, gu_all, usem, local.at[0])
    swap_qkv = Swap(cn, qkv_own, qkv_all, qsem, local.at[4])
    totals = Swap(cn, None, tot_in, tsem, local.at[3], lambda i: tot)
    c, d = lax.axis_index("ctx"), lax.axis_index("dp")
    mine, goal = d * cn + c, c * dpn + d
    stays = mine == goal
    hop = remote(
        out_own, out_all, osem.at[0], osem.at[1], {"dp": goal // cn, "ctx": lax.rem(goal, cn)}
    )
    keep = pltpu.make_async_copy(out_own, out_all, local.at[5])

    def share(s):
        return remote(
            tot_sum, tot_last.at[d], psem.at[0, s], psem.at[1, s], {"dp": lax.rem(d + s, dpn)}
        )

    greet_ctx(cn)
    for s in range(1, dpn):
        greet({"dp": lax.rem(d + s, dpn)})

    @pl.when(jnp.logical_not(stays))
    def _():
        greet({"dp": lax.rem(mine, dpn), "ctx": mine // dpn})

    pl.semaphore_wait(
        pltpu.get_barrier_semaphore(), cn - 1 + dpn - 1 + jnp.where(stays, 0, 1)
    )
    swap_gu.start()
    seq = an.shape[0]
    stage = (sum_refs[1], sum_refs[3])
    halves = (slice(0, seq // 2), slice(seq // 2, seq))

    def fill(src):
        copies = [
            pltpu.make_async_copy(src.at[pl.ds(i * n, n)], stage[i], local.at[1 + i])
            for i in range(2)
        ]
        for copy in copies:
            copy.start()
        for copy in copies:
            copy.wait()

    def staged(i, to=slice(None)):
        return stage[i][:, :, to].reshape(seq // 2, -1)

    fill(dys_all)
    outer_all(hid, staged, halves, rings[0][0])
    down_ring.start()
    fill(dob_all)
    for i in range(2):
        do[halves[i], :] = dot(staged(i), wo[...], contract_cols).astype(bf16)
    outer_all(o, staged, halves, rings[1][0])
    out_ring.start()
    m_qkv = rings[2][0].shape[1]
    order = qkv_ring.order()

    def grad_qkv(member):
        outer(an, dqkv, rings[2][0].at[member], pl.ds(pl.multiple_of(member * m_qkv, m_qkv), m_qkv))

    attend_back(qkv, do, cosines, sines, q_info, k_info, dq, dqkv, hw, 2 * rows)
    for i in range(down_ring.hops - 1):
        down_ring.forward(i + 1)
        out_ring.forward(i + 1)
    grad_qkv(order[0])
    qkv_ring.start()
    total = LineSum(cn, product(dqkv, w, contract_cols, rows, width), *sum_refs)

    def between(s):
        for i in range(qkv_ring.hops - 1):

            @pl.when(s == min(i, n - 2))
            def _():
                grad_qkv(order[1 + 2 * i])
                grad_qkv(order[2 + 2 * i])

            @pl.when(s == min(i + 1, n - 2))
            def _():
                qkv_ring.forward(i + 1)

    line_sums(cn, [total], between)
    grad_qkv(order[-1])
    tot[0] = jnp.zeros((1, width), f32)

    def norm_back(r):
        dan = total.part[0, k, r, :]
        xf = x[r, :].astype(f32)
        r1 = rms(xf)
        xh1 = xf * r1
        tot[0] += jnp.sum(dan * xh1, axis=0, keepdims=True)
        u1 = dan * gain[0:1, :]
        mean = jnp.mean(u1 * xh1, axis=-1, keepdims=True)
        grad = dh1[r, :] + r1 * (u1 - xh1 * mean)
        grad_in[r, :] = grad.astype(bf16)

    by_rows(rows, norm_back)
    tot[1] = term_two[...]
    tot[2] = jnp.broadcast_to(jnp.sum(mass[...], axis=1, keepdims=True), (1, width))
    totals.start()
    qkv_ring.finish(qkv_own)
    swap_qkv.start()
    out_ring.finish(out_own)

    @pl.when(stays)
    def _():
        keep.start()

    @pl.when(jnp.logical_not(stays))
    def _():
        hop.start()

    totals.finish()
    tot_sum[...] = jnp.sum(tot_in[...], axis=0)
    for s in range(1, dpn):
        share(s).start()
    down_ring.finish(down_own)
    total.drain()
    swap_gu.finish()
    tot_last[d] = tot_sum[...]
    for s in range(1, dpn):
        source = lax.rem(d - s + dpn, dpn)
        block = tot_last.at[source]
        remote(block, block, psem.at[0, s], psem.at[1, s], {"dp": source}).wait_recv()
    for s in range(1, dpn):
        share(s).wait_send()
    tot_out[...] = jnp.sum(tot_last[...], axis=0)
    swap_qkv.finish()

    @pl.when(stays)
    def _():
        keep.wait()

    @pl.when(jnp.logical_not(stays))
    def _():
        hop.wait_recv()
        hop.wait_send()


def spread_kernel(
    cn, dpn, qkv_in, gu_in, down_in, out_in, gq, gk, gv, go, gg, gu_out, gd, qkv, gu, down, out, sem
):
    hw = qkv.shape[2] // 3
    ff_rows = gd.shape[0]
    ff = ff_rows * dpn
    pairs = ((down_in, down), (out_in, out), (qkv_in, qkv), (gu_in, gu))
    loads = [pltpu.make_async_copy(a, b, sem.at[i]) for i, (a, b) in enumerate(pairs)]
    for load in loads:
        load.start()
    for load in loads[:3]:
        load.wait()
    gd[...] = down[...].astype(f32)
    go[...] = out[...].astype(f32)
    for c in range(cn):
        for i, ref in enumerate((gq, gk, gv)):
            ref[:, c * hw : (c + 1) * hw] = qkv[c, :, i * hw : (i + 1) * hw].astype(f32)
    loads[3].wait()
    for c in range(cn):
        for i, ref in enumerate((gg, gu_out)):
            for d in range(dpn):
                to = (d * cn + c) * ff_rows
                lo = i * ff + d * ff_rows
                ref[:, to : to + ff_rows] = gu[c, :, lo : lo + ff_rows].astype(f32)


def call(kernel, outs, ins, specs_in, specs_out, scratch, number, flops=0, moved=0):
    return pl.pallas_call(
        kernel,
        out_shape=outs,
        in_specs=specs_in,
        out_specs=specs_out,
        scratch_shapes=scratch,
        compiler_params=pltpu.CompilerParams(
            collective_id=number, has_side_effects=True, vmem_limit_bytes=61 * 2**20
        ),
        cost_estimate=pl.CostEstimate(flops=flops, bytes_accessed=moved, transcendentals=0),
    )(*ins)


def shape(dims, dtype=bf16):
    return jax.ShapeDtypeStruct(dims, dtype)


def shards(
    hidden_in,
    out_grad,
    seg_ids,
    valid_mask,
    w_query,
    w_key,
    w_value,
    w_output,
    w_gate,
    w_up,
    w_down,
    gain_attn,
    gain_mlp,
):
    dpn = lax.axis_size("dp")
    cn = lax.axis_size("ctx")
    n = cn // 2
    x_local = hidden_in[0]
    dy_local = out_grad[0]
    rows, width = x_local.shape
    seq = rows * cn
    dr = w_query.shape[0]
    hw = width // cn
    heads = hw // HEAD_DIM
    ff_rows = w_down.shape[0]
    ff = ff_rows * dpn
    dma = pltpu.SemaphoreType.DMA
    mib = 2**20

    code = (seg_ids[0] * 2 + valid_mask[0]).astype(bf16)
    x_ext = jnp.concatenate([x_local, jnp.broadcast_to(code[:, None], (rows, 128))], axis=1)
    lanes = jnp.arange(128)[None, :]
    gain_cols = jnp.where(lanes == 0, gain_attn[:, None], gain_mlp[:, None]).astype(bf16)
    pw = 3 * hw + 128
    ring_sem = dma((4, dpn // 2 + 1))
    x_all, w_qkv, gate_pack, up_pack, down, wo_low = call(
        functools.partial(front_kernel, cn, dpn),
        (
            shape((cn, rows, width + 128)),
            shape((dpn, cn, dr, pw)),
            shape((cn, dr, ff)),
            shape((cn, dr, ff)),
            shape((dpn, ff_rows, width)),
            shape((dr, width)),
        ),
        (x_ext, w_query, w_key, w_value, gain_cols, w_output, w_gate, w_up, w_down),
        [ANY] + [VMEM] * 5 + [ANY] * 3,
        (ANY, ANY, VMEM, VMEM, ANY, VMEM),
        [
            pltpu.VMEM((cn, dr, pw), bf16),
            pltpu.VMEM((2, dr, ff * cn), f32),
            pltpu.VMEM((ff_rows, width), f32),
            pltpu.VMEM((ff_rows, width), bf16),
            dma((5, n)),
            dma((2, cn)),
            dma((4, dpn // 2 + 1, cn)),
            ring_sem,
            dma((6,)),
        ],
        1,
        moved=160 * mib,
    )
    w_qkv = w_qkv.reshape(width, pw)
    inverse = jnp.exp(
        jnp.arange(HEAD_DIM // 2, dtype=f32) * (-2.0 * math.log(rope_base) / HEAD_DIM)
    )
    inverse = jnp.concatenate([inverse, inverse])[None]

    line_scratch = sum_scratch(cn, rows, width)
    an, proj, o, mass, gains, cosines, sines, cols, infos, w_gate_c, up_own, wo = call(
        functools.partial(attn_kernel, cn, dpn),
        (
            shape((seq, width)),
            shape((seq, 3 * hw)),
            shape((seq, hw)),
            shape((1, 2 * rows), f32),
            shape((8, width), f32),
            shape((seq, HEAD_DIM), f32),
            shape((seq, HEAD_DIM), f32),
            shape((seq, 128), f32),
            shape((8, seq), f32),
            shape((dpn, cn, dr, ff)),
            shape((cn, dr, ff)),
            shape((dpn, dr, width)),
        ),
        (x_all, w_qkv, inverse, gate_pack, up_pack, wo_low),
        [VMEM] * 3 + [ANY] * 3,
        (VMEM,) * 9 + (ANY,) * 3,
        [dma((2, 2, cn)), dma((4, dpn // 2 + 1, cn)), dma((2,)), ring_sem, dma((3,))],
        2,
        moved=160 * mib,
    )
    down = down.reshape(ff, width)
    h1, bn, w_up_c, hid, dgu, branch, dys = call(
        functools.partial(middle_kernel, cn, dpn),
        (
            shape((rows, width), f32),
            shape((cn, rows, width)),
            shape((dpn, cn, dr, ff)),
            shape((seq, ff)),
            shape((seq, 2 * ff)),
            shape((seq, width)),
            shape((cn, rows, width)),
        ),
        (
            o, wo.reshape(hw, width), x_local, gains, dy_local, up_own,
            w_gate_c.reshape(width, ff), down,
        ),
        [VMEM] * 5 + [ANY] * 3,
        (VMEM, ANY, ANY, VMEM, VMEM, ANY, ANY),
        [
            pltpu.VMEM((rows, width), bf16),
            pltpu.VMEM((cn, rows, width), bf16),
            pltpu.VMEM((cn, rows, width), bf16),
            pltpu.VMEM((width, ff), bf16),
            pltpu.VMEM((dpn, cn, dr, ff), bf16),
            pltpu.VMEM((ff, width), bf16),
            pltpu.VMEM((2 * rows, width), bf16),
            dma((5, n)),
            dma((5, n)),
            ring_sem,
            dma((5,)),
        ]
        + line_scratch,
        3,
        moved=160 * mib,
    )
    wo = wo.reshape(hw, width)
    w_gate_c = w_gate_c.reshape(width, ff)
    w_up_c = w_up_c.reshape(width, ff)
    bn = bn.reshape(seq, width)
    dh1, dob, term_two, g_gu, result = call(
        functools.partial(back_kernel, cn, dpn),
        (
            shape((rows, width), f32),
            shape((cn, rows, width)),
            shape((1, width), f32),
            shape((cn, dr, 2 * ff)),
            shape((rows, width)),
        ),
        (bn, dgu, w_gate_c, w_up_c, h1, dy_local, gains, branch.reshape(cn, rows, width)),
        [VMEM] * 7 + [ANY],
        (VMEM, ANY, VMEM, VMEM, VMEM),
        [
            pltpu.VMEM((rows, width), bf16),
            pltpu.VMEM((rows, width), bf16),
            pltpu.VMEM((n, rows, width), bf16),
            pltpu.VMEM((n + 1, rows, width), bf16),
            dma((4, n + 1)),
            dma((5, n)),
            dma((2,)),
            dma,
        ]
        + line_scratch
        + ring_scratch(dpn, cn * dr, 2 * ff),
        4,
        moved=160 * mib,
    )
    grad_input, totals, gu_back, g_down, g_out, q_all = call(
        functools.partial(last_kernel, cn, dpn),
        (
            shape((rows, width)),
            shape((3, 1, width), f32),
            shape((cn, dr, 2 * ff)),
            shape((ff_rows, width)),
            shape((dr, width)),
            shape((cn, dr, 3 * hw)),
        ),
        (
            g_gu, dob, dys, hid, o, wo, proj, cosines, sines, infos, cols, an, w_qkv,
            dh1, x_local, gains, term_two, mass,
        ),
        [ANY] * 3 + [VMEM] * 15,
        (VMEM, VMEM, ANY, VMEM, ANY, ANY),
        [
            pltpu.VMEM((seq, hw), bf16),
            pltpu.VMEM((seq, hw), f32),
            pltpu.VMEM((seq, 3 * hw), bf16),
            pltpu.VMEM((dr, width), bf16),
            pltpu.VMEM((cn, dr, 3 * hw), bf16),
            pltpu.VMEM((3, 1, width), f32),
            pltpu.VMEM((cn, 3, 1, width), f32),
            pltpu.VMEM((3, 1, width), f32),
            pltpu.VMEM((dpn, 3, 1, width), f32),
            dma((2, cn)),
            dma((2, cn)),
            dma((2, cn)),
            dma((2, dpn)),
            dma((2,)),
            dma((6,)),
        ]
        + line_scratch
        + ring_scratch(dpn, ff_rows, width)
        + ring_scratch(dpn, dr, width)
        + ring_scratch(dpn, cn * dr, 3 * hw),
        5,
        moved=160 * mib,
    )

    g_q, g_k, g_v, g_o, g_gate, g_up, g_down = pl.pallas_call(
        functools.partial(spread_kernel, cn, dpn),
        out_shape=tuple(shape((dr, width), f32) for _ in range(4))
        + tuple(shape((dr, ff * cn), f32) for _ in range(2))
        + (shape((ff_rows, width), f32),),
        in_specs=[ANY] * 4,
        out_specs=(VMEM,) * 7,
        scratch_shapes=[
            pltpu.VMEM((cn, dr, 3 * hw), bf16),
            pltpu.VMEM((cn, dr, 2 * ff), bf16),
            pltpu.VMEM((ff_rows, width), bf16),
            pltpu.VMEM((dr, width), bf16),
            dma((4,)),
        ],
        compiler_params=pltpu.CompilerParams(vmem_limit_bytes=48 * 2**20),
    )(q_all, gu_back, g_down, g_out)
    mass_mean = totals[2, 0, 0] / (heads * cn * dpn * seq)
    owner = (lax.axis_index("dp") * cn + lax.axis_index("ctx")) * dr
    grad_gains = [lax.dynamic_slice_in_dim(totals[i, 0], owner, dr) for i in range(2)]
    return (
        result[None],
        grad_input[None],
        g_q,
        g_k,
        g_v,
        g_o,
        g_gate,
        g_up,
        g_down,
        grad_gains[0],
        grad_gains[1],
        mass_mean,
    )


def solution(mesh):
    tok = P("dp", "ctx", None)
    ids = P("dp", "ctx")
    mat = P(("dp", "ctx"), None)
    vec = P(("dp", "ctx"))
    return jax.shard_map(
        shards,
        mesh=mesh,
        in_specs=(tok, tok, ids, ids) + (mat,) * 7 + (vec, vec),
        out_specs=(tok, tok) + (mat,) * 7 + (vec, vec, P()),
        check_vma=False,
    )
```

time: 633 us -> 519 us (0.82)
  matrix products: 44.1 us -> 0 us
  other arithmetic: 26.8 us -> 4.53 us
  Pallas kernels: 518 us -> 499 us
  between operations: 17.1 us -> 2.51 us
  local copies, waits for them, and re-layouts: 18 us -> 9 us
    dot_general x7 -> x0, matrix products: 44.1 us -> none  [dot(): return lax.dot_general(a, b, dims, preferred_element_type=f32)]
    pallas_call x6 -> x5, Pallas kernels: 514 us -> 495 us  [call(): pl.pallas_call(kernel, out_shape=outs, in_specs=specs_in, out_specs=specs...]
    convert_element_type x9 -> x0, other arithmetic: 6.62 us -> none  [the longest x3 3.37 us: shards(): w.astype(bf16).reshape(dr, cn, hw)]
  transfers between devices with their start and end apart: 2 -> 0, of which waited for: 0 -> 0; matrix products, arithmetic and copies ran while one was open for 7% -> 0% of each run, Pallas kernels for 70% -> 0%
where the time goes in v4:
time: 519 us; the launch traced here: 515 us
  Pallas kernels  499 us (96%)
  local copies, waits for them, and re-layouts  9 us (2%)
    pallas_call x5, Pallas kernels, call(): pl.pallas_call(kernel, out_shape=outs, in_specs=specs_in, out_specs=specs...  495 us

profile of v4, /device:TPU:9, one launch (start us, length us, event | category | flops | bytes accessed | tf_op | source)
XLA Modules:
  0.0 514.8 jit_solution(14525507476759753068)
XLA Ops:
  0.6 0.7 convert_bitcast_fusion
  1.3 0.1 broadcast_in_dim.42
  1.4 1.9 pad_maximum_fusion.x
  3.3 1.4 select_convert_fusion.gains
  4.7 73.1 %shard_map.220 = (bf16[8,128,2176]{2,1,0:T(8,128)(2,1)}, bf16[4,8,64,896]{3,2,1,0:T(8,128)(2,1)}, bf16[8,64,1024]{2,1,0:T(8,128)(2,1)}, bf16[8,64,1024]{2,1,0:T(...) custom-call(bf16[128,2176]{1,0:T(8,128)(2,1)} %pad_maximum_fusion.x, f32[64,2048]{1,0:T(8,128)} %wq.1, ...), custom_call_target="tpu_custom_call" | custom-call | bytes 167772160 | tf_op jit(solution)/shard_map/pallas_call | solution.py:1284
  77.8 0.6 maximum_bitcast_fusion.inverse
  78.4 78.9 %shard_map.221 = (bf16[1024,2048]{1,0:T(8,128)(2,1)}, bf16[1024,768]{1,0:T(8,128)(2,1)}, bf16[1024,256]{1,0:T(8,128)(2,1)}, f32[1,256]{1,0:T(1,128)}, f32[8,2048...) custom-call(bf16[8,128,2176]{2,1,0:T(8,128)(2,1)} %get-tuple-element, ...), custom_call_target="tpu_custom_call" | custom-call | bytes 167772160 | tf_op jit(solution)/shard_map/pallas_call | solution.py:1284
  157.3 100.3 %shard_map.222 = (f32[128,2048]{1,0:T(8,128)}, bf16[8,128,2048]{2,1,0:T(8,128)(2,1)}, bf16[4,8,64,1024]{3,2,1,0:T(8,128)(2,1)}, bf16[1024,1024]{1,0:T(8,128)(2,1...) custom-call(bf16[1024,256]{1,0:T(8,128)(2,1)} %get-tuple-element.60.o, ...), custom_call_target="tpu_custom_call" | custom-call | bytes 167772160 | tf_op jit(solution)/shard_map/pallas_call | solution.py:1284
  257.6 118.5 %shard_map.223 = (f32[128,2048]{1,0:T(8,128)}, bf16[8,128,2048]{2,1,0:T(8,128)(2,1)}, f32[1,2048]{1,0:T(1,128)}, bf16[8,64,2048]{2,1,0:T(8,128)(2,1)}, bf16[128,2048]{1,0:T(8,128)(2,1)}) custom-call(bf16[1024,2048]{1,0:T(8,128)(2,1)} %bitcast.30, bf16[1024,2048]{1,0:T(8,128)(2,1)} %get-tuple-element.67.dgu, bf16[2048,1024]{1,0:T(8,128)(2,1)} %bitcast.21, ...), custom_call_target="tpu_custom_call" | custom-call | bytes 167772160 | tf_op jit(solution)/shard_map/pallas_call | solution.py:1284
  376.1 124.0 %shard_map.224 = (bf16[128,2048]{1,0:T(8,128)(2,1)}, f32[3,1,2048]{2,1,0:T(1,128)}, bf16[8,64,2048]{2,1,0:T(8,128)(2,1)}, bf16[256,2048]{1,0:T(8,128)(2,1)}, bf1...) custom-call(bf16[8,64,2048]{2,1,0:T(8,128)(2,1)} %get-tuple-element.72.g_gu, ...), custom_call_target="tpu_custom_call" | custom-call | bytes 167772160 | tf_op jit(solution)/shard_map/pallas_call | solution.py:1284
  500.2 0.7 fusion
  500.9 0.6 dynamic-slice_bitcast_fusion
  501.5 0.0 copy-start
  501.5 1.6 copy-done
  503.1 0.0 copy-start.1
  503.1 1.2 copy-done.1
  504.3 1.1 copy-done.2
  505.4 0.9 copy-done.3
  506.4 3.9 shard_map.225
  510.3 1.1 slice.11
  512.1 0.0 copy-done.4
  512.1 0.8 copy.27
  512.9 0.0 copy-done.5
  512.9 0.8 copy.28
  (6 shorter events, 0.0 us)
Async XLA Ops:
  501.5 1.6 copy-start
  503.1 1.2 copy-start.1
  504.3 1.1 copy-start.2
  505.4 0.9 copy-start.3
  506.4 5.7 %copy-start.4 = (bf16[128,2048]{1,0:T(8,128)(2,1)S(1)}, bf16[128,2048]{1,0:T(8,128)(2,1)}, u32[]{:S(2)}) copy-start(bf16[128,2048]{1,0:T(8,128)(2,1)} %get-tuple-element.71) | copy-start | bytes 1572868
  506.4 6.5 %copy-start.5 = (bf16[128,2048]{1,0:T(8,128)(2,1)S(1)}, bf16[128,2048]{1,0:T(8,128)(2,1)}, u32[]{:S(2)}) copy-start(bf16[128,2048]{1,0:T(8,128)(2,1)} %get-tuple-element.85) | copy-start | bytes 1572868

commit v5 on v4

--- a/solution.py
+++ b/solution.py
@@ -274,6 +274,118 @@
         for h in range(1, self.hops + 1):
             for right in (True, False):
                 self.copy(h, right).wait_send()
+
+
+def head_of(cn, heads, c, i):
+    return c // 2 + cn // 2 * (heads * (c % 2) + i)
+
+
+class HeadRows:
+    def __init__(self, cn, dpn, dr):
+        self.cn, self.dpn = cn, dpn
+        self.per = HEAD_DIM // dr
+        self.heads = dpn // self.per
+        self.c, self.d = lax.axis_index("ctx"), lax.axis_index("dp")
+        mine = self.d * cn + self.c
+        head, n = mine // self.per, cn // 2
+        turn = head // n
+        self.home = 2 * lax.rem(head, n) + turn // self.heads
+        self.slot = lax.rem(turn, self.heads) * self.per + lax.rem(mine, self.per)
+        self.links = dpn - jnp.where(self.home == self.c, 1, 0)
+
+    def owner(self, r):
+        i, q = r // self.per, r % self.per
+        head = self.c // 2 + self.cn // 2 * (self.heads * lax.rem(self.c, 2) + i)
+        g = head * self.per + q
+        return {"dp": g // self.cn, "ctx": lax.rem(g, self.cn)}
+
+    def from_here(self, r):
+        at = self.owner(r)
+        return (at["dp"] == self.d) & (at["ctx"] == self.c)
+
+    def to_here(self, to):
+        return (self.home == self.c) & (self.d == to)
+
+    def greet_owners(self):
+        for r in range(self.dpn):
+            pl.when(jnp.logical_not(self.from_here(r)))(lambda r=r: greet(self.owner(r)))
+
+    def greet_homes(self):
+        for to in range(self.dpn):
+            pl.when(jnp.logical_not(self.to_here(to)))(
+                lambda to=to: greet({"dp": to, "ctx": self.home})
+            )
+
+
+class RowGather(HeadRows):
+    def __init__(self, cn, dpn, rows, full, sem, local):
+        super().__init__(cn, dpn, rows.shape[0])
+        self.rows, self.full, self.sem = rows, full, sem
+        self.keep = pltpu.make_async_copy(rows, full.at[self.slot], local)
+
+    def copy(self, to):
+        return remote(
+            self.rows,
+            self.full.at[self.slot],
+            self.sem.at[0, to],
+            self.sem.at[1, self.slot],
+            {"dp": to, "ctx": self.home},
+        )
+
+    def start(self):
+        for to in range(self.dpn):
+            pl.when(jnp.logical_not(self.to_here(to)))(lambda to=to: self.copy(to).start())
+            pl.when(self.to_here(to))(self.keep.start)
+
+    def finish(self):
+        for r in range(self.dpn):
+            block = self.full.at[r]
+            came = remote(block, block, self.sem.at[0, r], self.sem.at[1, r], self.owner(r))
+            pl.when(jnp.logical_not(self.from_here(r)))(came.wait_recv)
+            pl.when(self.from_here(r))(self.keep.wait)
+        for to in range(self.dpn):
+            pl.when(jnp.logical_not(self.to_here(to)))(lambda to=to: self.copy(to).wait_send())
+
+
+class RowSum(HeadRows):
+    def __init__(self, cn, dpn, parts, got, sem):
+        super().__init__(cn, dpn, parts.shape[1])
+        self.parts, self.got, self.sem = parts, got, sem
+
+    def copy(self, r):
+        return remote(
+            self.parts.at[r],
+            self.got.at[self.d],
+            self.sem.at[0, r],
+            self.sem.at[1, self.d],
+            self.owner(r),
+        )
+
+    def start(self):
+        for r in range(self.dpn):
+            pl.when(jnp.logical_not(self.from_here(r)))(lambda r=r: self.copy(r).start())
+
+            @pl.when(self.from_here(r))
+            def _():
+                self.got[self.d] = self.parts[r]
+
+    def finish(self, out):
+        for s in range(self.dpn):
+            block = self.got.at[s]
+            came = remote(
+                block, block, self.sem.at[0, s], self.sem.at[1, s], {"dp": s, "ctx": self.home}
+            )
+            pl.when(jnp.logical_not(self.to_here(s)))(came.wait_recv)
+
+        def add(r):
+            total = self.got[0, r, :].astype(f32)
+            for s in range(1, self.dpn):
+                total = total + self.got[s, r, :].astype(f32)
+            out[r, :] = total
+
+        by_rows(out.shape[0], add)
+        for r in range(self.dpn):
+            pl.when(jnp.logical_not(self.from_here(r)))(lambda r=r: self.copy(r).wait_send())
 
 
 class RingPieces(RingGather):
@@ -631,7 +743,9 @@
         load.start()
     for to in range(cn):
         for i, w in enumerate((wq, wk, wv)):
-            pack[to, :, i * hw : (i + 1) * hw] = w[:, to * hw : (to + 1) * hw].astype(bf16)
+            for t in range(hw // HEAD_DIM):
+                lo, at = head_of(cn, hw // HEAD_DIM, to, t) * HEAD_DIM, i * hw + t * HEAD_DIM
+                pack[to, :, at : at + HEAD_DIM] = w[:, lo : lo + HEAD_DIM].astype(bf16)
         pack[to, :, 3 * hw :] = gains[...]
     pl.semaphore_wait(pltpu.get_barrier_semaphore(), cn - 1 + 2)
     swap.start()
@@ -769,20 +883,10 @@
 def attn_kernel(
     cn, dpn, x_all, w, inverse, gate, up, wo,
     an, qkv, o, mass, gains, cosines, sines, cols, rows_in,
-    gate_all, up_own, wo_all, ssem, rsem, hsem, wsem, local,
+    gate_all, up_own, wo_all, ssem, rsem, wsem, local,
 ):
     c, d = lax.axis_index("ctx"), lax.axis_index("dp")
-    mine, wanted = d * cn + c, c * dpn + d
-    stays = mine == wanted
-    hop = remote(
-        wo,
-        wo_all.at[lax.rem(mine, dpn)],
-        hsem.at[0],
-        hsem.at[1],
-        {"dp": lax.rem(mine, dpn), "ctx": mine // dpn},
-    )
-    keep = pltpu.make_async_copy(wo, wo_all.at[d], local.at[2])
-    wo_ring = RingGather(dpn, wo_all.at[d], wo_all, wsem)
+    wo_rows = RowGather(cn, dpn, wo, wo_all, wsem, local.at[2])
     rows = x_all.shape[1]
     hw = qkv.shape[1] // 3
     swap_gate = Swap(cn, gate, gate_all.at[d], ssem.at[0], local.at[0])
@@ -792,36 +896,12 @@
     greet_ctx(cn)
     ring.greet()
 
-    @pl.when(jnp.logical_not(stays))
-    def _():
-        greet({"dp": wanted // cn, "ctx": lax.rem(wanted, cn)})
-
-    pl.semaphore_wait(
-        pltpu.get_barrier_semaphore(), cn - 1 + 2 + jnp.where(stays, 0, 1)
-    )
-
-    @pl.when(stays)
-    def _():
-        keep.start()
-        keep.wait()
-
-    @pl.when(jnp.logical_not(stays))
-    def _():
-        hop.start()
-
+    wo_rows.greet_owners()
+    pl.semaphore_wait(pltpu.get_barrier_semaphore(), cn - 1 + 2 + wo_rows.links)
+    wo_rows.start()
     swap_gate.start()
 
-    def hop_done():
-        @pl.when(jnp.logical_not(stays))
-        def _():
-            arrived = wo_all.at[d]
-            remote(arrived, arrived, hsem.at[0], hsem.at[1], {"dp": d, "ctx": c}).wait_recv()
-
-        wo_ring.start()
-
     def in_project(i):
-        pl.when(i == 0)(hop_done)
-
         @pl.when(i == 1)
         def _():
             for s in range(cn // 2):
@@ -834,10 +914,6 @@
             swap_up.start()
 
     def in_attend(i):
-        @pl.when(i == 1)
-        def _():
-            wo_ring.forward()
-
         @pl.when(i == 2)
         def _():
             for source in sources[: cn // 2]:
@@ -852,14 +928,10 @@
     for source in sources[cn // 2 :]:
         ring.forward(source)
     swap_up.finish()
-    wo_ring.finish()
+    wo_rows.finish()
     for source in sources:
         ring.finish(source)
     swap_gate.sent()
-
-    @pl.when(jnp.logical_not(stays))
-    def _():
-        hop.wait_send()
 
 
 def middle_kernel(
@@ -1109,25 +1181,19 @@
 def last_kernel(
     cn, dpn, g_gu, dob_all, dys_all, hid, o, wo, qkv, cosines, sines, q_info, k_info, an, w,
     dh1, x, gain, term_two, mass, grad_in, tot_out, gu_all, down_own, out_all, qkv_all,
-    do, dq, dqkv, out_own, qkv_own, tot, tot_in, tot_sum, tot_last,
+    do, dq, dqkv, out_parts, out_got, qkv_own, tot, tot_in, tot_sum, tot_last,
     usem, qsem, tsem, psem, osem, local, *scratch,
 ):
-    sum_refs, rings = scratch[:-12], (scratch[-12:-8], scratch[-8:-4], scratch[-4:])
+    sum_refs, rings = scratch[:-8], (scratch[-8:-4], scratch[-4:])
     rows, width = x.shape
     hw = width // cn
     _, _, k, n, _ = place(cn)
-    down_ring, out_ring, qkv_ring = (RingSum(dpn, *refs) for refs in rings)
+    down_ring, qkv_ring = (RingSum(dpn, *refs) for refs in rings)
+    rows_out = RowSum(cn, dpn, out_parts, out_got, osem)
     swap_gu = Swap(cn, g_gu, gu_all, usem, local.at[0])
     swap_qkv = Swap(cn, qkv_own, qkv_all, qsem, local.at[4])
     totals = Swap(cn, None, tot_in, tsem, local.at[3], lambda i: tot)
     c, d = lax.axis_index("ctx"), lax.axis_index("dp")
-    mine, goal = d * cn + c, c * dpn + d
-    stays = mine == goal
-    hop = remote(
-        out_own, out_all, osem.at[0], osem.at[1], {"dp": goal // cn, "ctx": lax.rem(goal, cn)}
-    )
-    keep = pltpu.make_async_copy(out_own, out_all, local.at[5])
-
     def share(s):
         return remote(
             tot_sum, tot_last.at[d], psem.at[0, s], psem.at[1, s], {"dp": lax.rem(d + s, dpn)}
@@ -1137,12 +1203,9 @@
     for s in range(1, dpn):
         greet({"dp": lax.rem(d + s, dpn)})
 
-    @pl.when(jnp.logical_not(stays))
-    def _():
-        greet({"dp": lax.rem(mine, dpn), "ctx": mine // dpn})
-
+    rows_out.greet_homes()
     pl.semaphore_wait(
-        pltpu.get_barrier_semaphore(), cn - 1 + dpn - 1 + jnp.where(stays, 0, 1)
+        pltpu.get_barrier_semaphore(), cn - 1 + dpn - 1 + rows_out.links
     )
     swap_gu.start()
     seq = an.shape[0]
@@ -1168,18 +1231,17 @@
     fill(dob_all)
     for i in range(2):
         do[halves[i], :] = dot(staged(i), wo[...], contract_cols).astype(bf16)
-    outer_all(o, staged, halves, rings[1][0])
-    out_ring.start()
-    m_qkv = rings[2][0].shape[1]
+    outer_all(o, staged, halves, out_parts)
+    rows_out.start()
+    m_qkv = rings[1][0].shape[1]
     order = qkv_ring.order()
 
     def grad_qkv(member):
-        outer(an, dqkv, rings[2][0].at[member], pl.ds(pl.multiple_of(member * m_qkv, m_qkv), m_qkv))
+        outer(an, dqkv, rings[1][0].at[member], pl.ds(pl.multiple_of(member * m_qkv, m_qkv), m_qkv))
 
     attend_back(qkv, do, cosines, sines, q_info, k_info, dq, dqkv, hw, 2 * rows)
     for i in range(down_ring.hops - 1):
         down_ring.forward(i + 1)
-        out_ring.forward(i + 1)
     grad_qkv(order[0])
     qkv_ring.start()
     total = LineSum(cn, product(dqkv, w, contract_cols, rows, width), *sum_refs)
@@ -1217,16 +1279,7 @@
     totals.start()
     qkv_ring.finish(qkv_own)
     swap_qkv.start()
-    out_ring.finish(out_own)
-
-    @pl.when(stays)
-    def _():
-        keep.start()
-
-    @pl.when(jnp.logical_not(stays))
-    def _():
-        hop.start()
-
+    rows_out.finish(out_all)
     totals.finish()
     tot_sum[...] = jnp.sum(tot_in[...], axis=0)
     for s in range(1, dpn):
@@ -1244,15 +1297,6 @@
     tot_out[...] = jnp.sum(tot_last[...], axis=0)
     swap_qkv.finish()
 
-    @pl.when(stays)
-    def _():
-        keep.wait()
-
-    @pl.when(jnp.logical_not(stays))
-    def _():
-        hop.wait_recv()
-        hop.wait_send()
-
 
 def spread_kernel(
     cn, dpn, qkv_in, gu_in, down_in, out_in, gq, gk, gv, go, gg, gu_out, gd, qkv, gu, down, out, sem
@@ -1267,10 +1311,12 @@
     for load in loads[:3]:
         load.wait()
     gd[...] = down[...].astype(f32)
-    go[...] = out[...].astype(f32)
+    go[...] = out[...]
     for c in range(cn):
         for i, ref in enumerate((gq, gk, gv)):
-            ref[:, c * hw : (c + 1) * hw] = qkv[c, :, i * hw : (i + 1) * hw].astype(f32)
+            for t in range(hw // HEAD_DIM):
+                lo, at = head_of(cn, hw // HEAD_DIM, c, t) * HEAD_DIM, i * hw + t * HEAD_DIM
+                ref[:, lo : lo + HEAD_DIM] = qkv[c, :, at : at + HEAD_DIM].astype(f32)
     loads[3].wait()
     for c in range(cn):
         for i, ref in enumerate((gg, gu_out)):
@@ -1387,7 +1433,7 @@
         (x_all, w_qkv, inverse, gate_pack, up_pack, wo_low),
         [VMEM] * 3 + [ANY] * 3,
         (VMEM,) * 9 + (ANY,) * 3,
-        [dma((2, 2, cn)), dma((4, dpn // 2 + 1, cn)), dma((2,)), ring_sem, dma((3,))],
+        [dma((2, 2, cn)), dma((4, dpn // 2 + 1, cn)), dma((2, dpn)), dma((3,))],
         2,
         moved=160 * mib,
     )
@@ -1464,7 +1510,7 @@
             shape((3, 1, width), f32),
             shape((cn, dr, 2 * ff)),
             shape((ff_rows, width)),
-            shape((dr, width)),
+            shape((dr, width), f32),
             shape((cn, dr, 3 * hw)),
         ),
         (
@@ -1472,12 +1518,13 @@
             dh1, x_local, gains, term_two, mass,
         ),
         [ANY] * 3 + [VMEM] * 15,
-        (VMEM, VMEM, ANY, VMEM, ANY, ANY),
+        (VMEM, VMEM, ANY, VMEM, VMEM, ANY),
         [
             pltpu.VMEM((seq, hw), bf16),
             pltpu.VMEM((seq, hw), f32),
             pltpu.VMEM((seq, 3 * hw), bf16),
-            pltpu.VMEM((dr, width), bf16),
+            pltpu.VMEM((dpn, dr, width), bf16),
+            pltpu.VMEM((dpn, dr, width), bf16),
             pltpu.VMEM((cn, dr, 3 * hw), bf16),
             pltpu.VMEM((3, 1, width), f32),
             pltpu.VMEM((cn, 3, 1, width), f32),
@@ -1487,12 +1534,11 @@
             dma((2, cn)),
             dma((2, cn)),
             dma((2, dpn)),
-            dma((2,)),
-            dma((6,)),
+            dma((2, dpn)),
+            dma((5,)),
         ]
         + line_scratch
         + ring_scratch(dpn, ff_rows, width)
-        + ring_scratch(dpn, dr, width)
         + ring_scratch(dpn, cn * dr, 3 * hw),
         5,
         moved=160 * mib,
@@ -1509,7 +1555,7 @@
             pltpu.VMEM((cn, dr, 3 * hw), bf16),
             pltpu.VMEM((cn, dr, 2 * ff), bf16),
             pltpu.VMEM((ff_rows, width), bf16),
-            pltpu.VMEM((dr, width), bf16),
+            pltpu.VMEM((dr, width), f32),
             dma((4,)),
         ],
         compiler_params=pltpu.CompilerParams(vmem_limit_bytes=48 * 2**20),

time: 519 us -> 483 us (0.931)
  Pallas kernels: 499 us -> 466 us
    pallas_call x5, Pallas kernels: 495 us -> 462 us  [call(): pl.pallas_call(kernel, out_shape=outs, in_specs=specs_in, out_specs=specs...]
where the time goes in v5:
time: 483 us; the launch traced here: 482 us
  Pallas kernels  466 us (96%)
  local copies, waits for them, and re-layouts  9.09 us (2%)
    pallas_call x5, Pallas kernels, call(): pl.pallas_call(kernel, out_shape=outs, in_specs=specs_in, out_specs=specs...  462 us

profile of v5, /device:TPU:9, one launch (start us, length us, event | category | flops | bytes accessed | tf_op | source)
XLA Modules:
  0.0 481.9 jit_solution(6748080484601981350)
XLA Ops:
  0.6 0.7 convert_bitcast_fusion
  1.3 0.1 broadcast_in_dim.42
  1.4 1.9 pad_maximum_fusion.x
  3.3 1.4 select_convert_fusion.gains
  4.7 73.1 %shard_map.220 = (bf16[8,128,2176]{2,1,0:T(8,128)(2,1)}, bf16[4,8,64,896]{3,2,1,0:T(8,128)(2,1)}, bf16[8,64,1024]{2,1,0:T(8,128)(2,1)}, bf16[8,64,1024]{2,1,0:T(...) custom-call(bf16[128,2176]{1,0:T(8,128)(2,1)} %pad_maximum_fusion.x, f32[64,2048]{1,0:T(8,128)} %wq.1, ...), custom_call_target="tpu_custom_call" | custom-call | bytes 167772160 | tf_op jit(solution)/shard_map/pallas_call | solution.py:1330
  77.8 0.6 maximum_bitcast_fusion.inverse
  78.4 57.9 %shard_map.221 = (bf16[1024,2048]{1,0:T(8,128)(2,1)}, bf16[1024,768]{1,0:T(8,128)(2,1)}, bf16[1024,256]{1,0:T(8,128)(2,1)}, f32[1,256]{1,0:T(1,128)}, f32[8,2048...) custom-call(bf16[8,128,2176]{2,1,0:T(8,128)(2,1)} %get-tuple-element, ...), custom_call_target="tpu_custom_call" | custom-call | bytes 167772160 | tf_op jit(solution)/shard_map/pallas_call | solution.py:1330
  136.3 94.0 %shard_map.222 = (f32[128,2048]{1,0:T(8,128)}, bf16[8,128,2048]{2,1,0:T(8,128)(2,1)}, bf16[4,8,64,1024]{3,2,1,0:T(8,128)(2,1)}, bf16[1024,1024]{1,0:T(8,128)(2,1...) custom-call(bf16[1024,256]{1,0:T(8,128)(2,1)} %get-tuple-element.60.o, ...), custom_call_target="tpu_custom_call" | custom-call | bytes 167772160 | tf_op jit(solution)/shard_map/pallas_call | solution.py:1330
  230.3 119.1 %shard_map.223 = (f32[128,2048]{1,0:T(8,128)}, bf16[8,128,2048]{2,1,0:T(8,128)(2,1)}, f32[1,2048]{1,0:T(1,128)}, bf16[8,64,2048]{2,1,0:T(8,128)(2,1)}, bf16[128,2048]{1,0:T(8,128)(2,1)}) custom-call(bf16[1024,2048]{1,0:T(8,128)(2,1)} %bitcast.30, bf16[1024,2048]{1,0:T(8,128)(2,1)} %get-tuple-element.67.dgu, bf16[2048,1024]{1,0:T(8,128)(2,1)} %bitcast.21, ...), custom_call_target="tpu_custom_call" | custom-call | bytes 167772160 | tf_op jit(solution)/shard_map/pallas_call | solution.py:1330
  349.4 117.7 %shard_map.224 = (bf16[128,2048]{1,0:T(8,128)(2,1)}, f32[3,1,2048]{2,1,0:T(1,128)}, bf16[8,64,2048]{2,1,0:T(8,128)(2,1)}, bf16[256,2048]{1,0:T(8,128)(2,1)}, f32...) custom-call(bf16[8,64,2048]{2,1,0:T(8,128)(2,1)} %get-tuple-element.72.g_gu, ...), custom_call_target="tpu_custom_call" | custom-call | bytes 167772160 | tf_op jit(solution)/shard_map/pallas_call | solution.py:1330
  467.1 0.7 fusion
  467.8 0.6 dynamic-slice_bitcast_fusion
  468.4 1.6 copy-done
  470.0 0.0 copy-start.1
  470.0 1.2 copy-done.1
  471.2 0.0 copy-start.2
  471.2 1.1 copy-done.2
  472.3 1.0 copy-done.3
  473.4 4.0 shard_map.225
  477.4 1.1 slice.11
  479.2 0.0 copy-done.4
  479.2 0.8 copy.27
  480.0 0.0 copy-done.5
  480.0 0.8 copy.28
  (6 shorter events, 0.0 us)
Async XLA Ops:
  468.4 1.6 copy-start
  470.0 1.2 copy-start.1
  471.2 1.1 copy-start.2
  472.3 1.0 copy-start.3
  473.4 5.8 %copy-start.4 = (bf16[128,2048]{1,0:T(8,128)(2,1)S(1)}, bf16[128,2048]{1,0:T(8,128)(2,1)}, u32[]{:S(2)}) copy-start(bf16[128,2048]{1,0:T(8,128)(2,1)} %get-tuple-element.71) | copy-start | bytes 1572868
  473.4 6.6 %copy-start.5 = (bf16[128,2048]{1,0:T(8,128)(2,1)S(1)}, bf16[128,2048]{1,0:T(8,128)(2,1)}, u32[]{:S(2)}) copy-start(bf16[128,2048]{1,0:T(8,128)(2,1)} %get-tuple-element.85) | copy-start | bytes 1572868

commit v6 on v5

--- a/solution.py
+++ b/solution.py
@@ -741,15 +741,15 @@
     ]
     for load in loads:
         load.start()
+    pl.semaphore_wait(pltpu.get_barrier_semaphore(), cn - 1 + 2)
+    gather.start()
     for to in range(cn):
         for i, w in enumerate((wq, wk, wv)):
             for t in range(hw // HEAD_DIM):
                 lo, at = head_of(cn, hw // HEAD_DIM, to, t) * HEAD_DIM, i * hw + t * HEAD_DIM
                 pack[to, :, at : at + HEAD_DIM] = w[:, lo : lo + HEAD_DIM].astype(bf16)
         pack[to, :, 3 * hw :] = gains[...]
-    pl.semaphore_wait(pltpu.get_barrier_semaphore(), cn - 1 + 2)
     swap.start()
-    gather.start()
     loads[2].wait()
     down[...] = tall[...].astype(bf16)
     down_ring.start()
@@ -1028,18 +1028,27 @@
         send.wait()
 
     feed(j)
+    gather.step(1)
 
     @pl.loop(1, n)
     def _(s):
-        gather.step(s)
+        both = (j - s >= 0) & (j + s <= n - 1)
 
         @pl.when(j - s >= 0)
         def _():
             feed(j - s)
 
+        @pl.when(both & (s < n - 1))
+        def _():
+            gather.step(s + 1)
+
         @pl.when(j + s <= n - 1)
         def _():
             feed(j + s)
+
+        @pl.when(jnp.logical_not(both) & (s < n - 1))
+        def _():
+            gather.step(s + 1)
 
     gather.sent()
     store_dy.wait()
@@ -1075,10 +1084,13 @@
     def weight_grad(member):
         outer(bn, dgu, blocks.at[member], pl.ds(pl.multiple_of(member * m, m), m))
 
-    weight_grad(order[0])
-    ring.start()
 
     def between(s):
+        @pl.when(s == 0)
+        def _():
+            weight_grad(order[0])
+            ring.start()
+
         for i in range(ring.hops - 1):
 
             @pl.when(s == min(i, n - 2))
@@ -1086,7 +1098,7 @@
                 weight_grad(order[1 + 2 * i])
                 weight_grad(order[2 + 2 * i])
 
-            @pl.when(s == min(i + 1, n - 2))
+            @pl.when(s == min(i + 2, n - 2))
             def _():
                 ring.forward(i + 1)
 
@@ -1225,14 +1237,14 @@
     def staged(i, to=slice(None)):
         return stage[i][:, :, to].reshape(seq // 2, -1)
 
+    fill(dob_all)
+    outer_all(o, staged, halves, out_parts)
+    rows_out.start()
+    for i in range(2):
+        do[halves[i], :] = dot(staged(i), wo[...], contract_cols).astype(bf16)
     fill(dys_all)
     outer_all(hid, staged, halves, rings[0][0])
     down_ring.start()
-    fill(dob_all)
-    for i in range(2):
-        do[halves[i], :] = dot(staged(i), wo[...], contract_cols).astype(bf16)
-    outer_all(o, staged, halves, out_parts)
-    rows_out.start()
     m_qkv = rings[1][0].shape[1]
     order = qkv_ring.order()
 
@@ -1240,8 +1252,6 @@
         outer(an, dqkv, rings[1][0].at[member], pl.ds(pl.multiple_of(member * m_qkv, m_qkv), m_qkv))
 
     attend_back(qkv, do, cosines, sines, q_info, k_info, dq, dqkv, hw, 2 * rows)
-    for i in range(down_ring.hops - 1):
-        down_ring.forward(i + 1)
     grad_qkv(order[0])
     qkv_ring.start()
     total = LineSum(cn, product(dqkv, w, contract_cols, rows, width), *sum_refs)
@@ -1253,13 +1263,19 @@
             def _():
                 grad_qkv(order[1 + 2 * i])
                 grad_qkv(order[2 + 2 * i])
+                qkv_ring.forward(i + 1)
 
             @pl.when(s == min(i + 1, n - 2))
             def _():
-                qkv_ring.forward(i + 1)
+                down_ring.forward(i + 1)
+
+        @pl.when(s == n - 2)
+        def _():
+            grad_qkv(order[-1])
+            qkv_ring.finish(qkv_own)
+            swap_qkv.start()
 
     line_sums(cn, [total], between)
-    grad_qkv(order[-1])
     tot[0] = jnp.zeros((1, width), f32)
 
     def norm_back(r):
@@ -1277,8 +1293,6 @@
     tot[1] = term_two[...]
     tot[2] = jnp.broadcast_to(jnp.sum(mass[...], axis=1, keepdims=True), (1, width))
     totals.start()
-    qkv_ring.finish(qkv_own)
-    swap_qkv.start()
     rows_out.finish(out_all)
     totals.finish()
     tot_sum[...] = jnp.sum(tot_in[...], axis=0)
@@ -1558,7 +1572,7 @@
             pltpu.VMEM((dr, width), f32),
             dma((4,)),
         ],
-        compiler_params=pltpu.CompilerParams(vmem_limit_bytes=48 * 2**20),
+        compiler_params=pltpu.CompilerParams(vmem_limit_bytes=61 * 2**20),
     )(q_all, gu_back, g_down, g_out)
     mass_mean = totals[2, 0, 0] / (heads * cn * dpn * seq)
     owner = (lax.axis_index("dp") * cn + lax.axis_index("ctx")) * dr

time: 483 us -> 462 us (0.957)
  Pallas kernels: 466 us -> 447 us
  local copies, waits for them, and re-layouts: 9.09 us -> 4.11 us
    pallas_call x5, Pallas kernels: 462 us -> 442 us  [call(): pl.pallas_call(kernel, out_shape=outs, in_specs=specs_in, out_specs=specs...]
    unnamed x14 -> x6, local copies, waits for them, and re-layouts: 6.58 us -> 1.6 us
where the time goes in v6:
time: 462 us; the launch traced here: 459 us
  Pallas kernels  447 us (97%)
    pallas_call x5, Pallas kernels, call(): pl.pallas_call(kernel, out_shape=outs, in_specs=specs_in, out_specs=specs...  442 us

profile of v6, /device:TPU:9, one launch (start us, length us, event | category | flops | bytes accessed | tf_op | source)
XLA Modules:
  0.0 458.6 jit_solution(8835409427845442441)
XLA Ops:
  0.6 0.7 convert_bitcast_fusion
  1.3 0.1 broadcast_in_dim.42
  1.4 1.9 pad_maximum_fusion.x
  3.3 1.4 select_convert_fusion.gains
  4.7 72.8 %shard_map.220 = (bf16[8,128,2176]{2,1,0:T(8,128)(2,1)}, bf16[4,8,64,896]{3,2,1,0:T(8,128)(2,1)}, bf16[8,64,1024]{2,1,0:T(8,128)(2,1)}, bf16[8,64,1024]{2,1,0:T(...) custom-call(bf16[128,2176]{1,0:T(8,128)(2,1)} %pad_maximum_fusion.x, f32[64,2048]{1,0:T(8,128)} %wq.1, ...), custom_call_target="tpu_custom_call" | custom-call | bytes 167772160 | tf_op jit(solution)/shard_map/pallas_call | solution.py:1344
  77.5 0.6 maximum_bitcast_fusion.inverse
  78.1 57.8 %shard_map.221 = (bf16[1024,2048]{1,0:T(8,128)(2,1)}, bf16[1024,768]{1,0:T(8,128)(2,1)}, bf16[1024,256]{1,0:T(8,128)(2,1)}, f32[1,256]{1,0:T(1,128)}, f32[8,2048...) custom-call(bf16[8,128,2176]{2,1,0:T(8,128)(2,1)} %get-tuple-element, ...), custom_call_target="tpu_custom_call" | custom-call | bytes 167772160 | tf_op jit(solution)/shard_map/pallas_call | solution.py:1344
  135.9 90.3 %shard_map.222 = (f32[128,2048]{1,0:T(8,128)}, bf16[8,128,2048]{2,1,0:T(8,128)(2,1)}, bf16[4,8,64,1024]{3,2,1,0:T(8,128)(2,1)}, bf16[1024,1024]{1,0:T(8,128)(2,1...) custom-call(bf16[1024,256]{1,0:T(8,128)(2,1)} %get-tuple-element.60.o, ...), custom_call_target="tpu_custom_call" | custom-call | bytes 167772160 | tf_op jit(solution)/shard_map/pallas_call | solution.py:1344
  226.2 113.3 %shard_map.223 = (f32[128,2048]{1,0:T(8,128)}, bf16[8,128,2048]{2,1,0:T(8,128)(2,1)}, f32[1,2048]{1,0:T(1,128)}, bf16[8,64,2048]{2,1,0:T(8,128)(2,1)}, bf16[128,2048]{1,0:T(8,128)(2,1)}) custom-call(bf16[1024,2048]{1,0:T(8,128)(2,1)} %bitcast.30, bf16[1024,2048]{1,0:T(8,128)(2,1)} %get-tuple-element.67.dgu, bf16[2048,1024]{1,0:T(8,128)(2,1)} %bitcast.21, ...), custom_call_target="tpu_custom_call" | custom-call | bytes 167772160 | tf_op jit(solution)/shard_map/pallas_call | solution.py:1344
  339.5 107.5 %shard_map.224 = (bf16[128,2048]{1,0:T(8,128)(2,1)}, f32[3,1,2048]{2,1,0:T(1,128)}, bf16[8,64,2048]{2,1,0:T(8,128)(2,1)}, bf16[256,2048]{1,0:T(8,128)(2,1)}, f32...) custom-call(bf16[8,64,2048]{2,1,0:T(8,128)(2,1)} %get-tuple-element.72.g_gu, ...), custom_call_target="tpu_custom_call" | custom-call | bytes 167772160 | tf_op jit(solution)/shard_map/pallas_call | solution.py:1344
  447.0 0.7 fusion
  447.7 0.6 dynamic-slice_bitcast_fusion
  448.3 0.0 copy-start
  448.3 0.0 copy-start.1
  448.3 5.8 %shard_map.225 = (f32[64,2048]{1,0:T(8,128)}, f32[64,2048]{1,0:T(8,128)}, f32[64,2048]{1,0:T(8,128)}, f32[64,2048]{1,0:T(8,128)}, f32[64,8192]{1,0:T(8,128)}, /*index=5*/f32[64,8192]{1,0:T(8,128)}, f32[256,2048]{1,0:T(8,128)}) custom-call(bf16[8,64,768]{2,1,0:T(8,128)(2,1)} %get-tuple-element.86.qkv_in, bf16[8,64,2048]{2,1,0:T(8,128)(2,1)} %get-tuple-element.87.gu_in, ...), custom_call_target="tpu_custom_call" | custom-call | tf_op jit(solution)/shard_map/pallas_call | solution.py:1561
  454.1 1.1 slice.11
  455.9 0.0 copy-done
  455.9 0.8 copy.27
  456.7 0.0 copy-done.1
  456.7 0.8 copy.28
  (2 shorter events, 0.0 us)
Async XLA Ops:
  448.3 7.6 %copy-start = (bf16[128,2048]{1,0:T(8,128)(2,1)S(1)}, bf16[128,2048]{1,0:T(8,128)(2,1)}, u32[]{:S(2)}) copy-start(bf16[128,2048]{1,0:T(8,128)(2,1)} %get-tuple-element.71) | copy-start | bytes 1572868
  448.3 8.4 %copy-start.1 = (bf16[128,2048]{1,0:T(8,128)(2,1)S(1)}, bf16[128,2048]{1,0:T(8,128)(2,1)}, u32[]{:S(2)}) copy-start(bf16[128,2048]{1,0:T(8,128)(2,1)} %get-tuple-element.85) | copy-start | bytes 1572868

commit v7 on v6

--- a/solution.py
+++ b/solution.py
@@ -627,29 +627,6 @@
                 self.along(t, t, sib).wait_send()
 
 
-class LineSumRows(LineSum):
-    def __init__(self, cn, terms, stage, loads, *refs):
-        super().__init__(cn, None, *refs)
-        self.terms, self.stage, self.loads = terms, stage, loads
-
-    def produce(self, t, slot):
-        _, _, k, _, _ = place(self.cn)
-        other = pltpu.make_async_copy(
-            self.terms.at[2 * t + 1 - k], self.cross.at[t], self.loads.at[0]
-        )
-        own = pltpu.make_async_copy(self.terms.at[2 * t + k], self.stage, self.loads.at[1])
-        other.start()
-        own.start()
-        other.wait()
-        self.across(t).start()
-        own.wait()
-
-        def wide(r):
-            self.part[slot, k, r, :] = self.stage[r, :].astype(f32)
-
-        by_rows(self.stage.shape[0], wide)
-
-
 def line_sums(cn, sums, between=None):
     _, j, _, n, _ = place(cn)
 
@@ -719,9 +696,9 @@
 
 
 def front_kernel(
-    cn, dpn, x, wq, wk, wv, gains, wo, gate_in, up_in, down_in,
+    cn, dpn, x_in, seg, valid, gain_rows, wq, wk, wv, wo, gate_in, up_in, down_in,
     x_all, pack_all, gate, up, down_all, wo_low,
-    pack, wide, tall, down, gsem, ssem, rsem, dsem, local,
+    x, pack, wide, tall, down, gsem, ssem, rsem, dsem, local,
 ):
     c, d = lax.axis_index("ctx"), lax.axis_index("dp")
     hw = wq.shape[1] // cn
@@ -733,6 +710,19 @@
     down_ring = RingGather(dpn, down, down_all, dsem)
     greet_ctx(cn)
     ring.greet()
+    rows, width = x_in.shape
+    load_x = pltpu.make_async_copy(x_in, x.at[:, 0:width], local.at[1])
+    load_x.start()
+
+    def column(row):
+        return jnp.broadcast_to(row, (128, 128)).T
+
+    code = (seg[...] * 2 + valid[...]).astype(f32)
+    x[:, width:] = column(code).astype(bf16)
+    lane = lax.broadcasted_iota(jnp.int32, (128, 128), 1)
+    gains = jnp.where(lane == 0, column(gain_rows[0:1, :]), column(gain_rows[1:2, :]))
+    gains = gains[0 : wq.shape[0]].astype(bf16)
+    load_x.wait()
     loads = [
         pltpu.make_async_copy(src, dst, local.at[i])
         for i, (src, dst) in enumerate(
@@ -748,7 +738,7 @@
             for t in range(hw // HEAD_DIM):
                 lo, at = head_of(cn, hw // HEAD_DIM, to, t) * HEAD_DIM, i * hw + t * HEAD_DIM
                 pack[to, :, at : at + HEAD_DIM] = w[:, lo : lo + HEAD_DIM].astype(bf16)
-        pack[to, :, 3 * hw :] = gains[...]
+        pack[to, :, 3 * hw :] = gains
     swap.start()
     loads[2].wait()
     down[...] = tall[...].astype(bf16)
@@ -936,8 +926,8 @@
 
 def middle_kernel(
     cn, dpn, o, wo, x, gain, dy, up, gate_all, down_all,
-    h1, bn_all, up_all, hid, dgu, branch_all, dys_all,
-    own, bn, dys, wg, wu, down, branch, gsem, ysem, rsem, local, *sum_refs,
+    h1, bn_all, up_all, hid, dgu, dys_all,
+    own, bn, dys, wg, wu, down, gsem, ysem, rsem, local, *sum_refs,
 ):
     c, d = lax.axis_index("ctx"), lax.axis_index("dp")
     _, j, k, n, _ = place(cn)
@@ -991,7 +981,6 @@
     load_up.wait()
     wgate, wup = wg, wu.reshape(width, ff)
     tile = min(512, ff)
-    wide = min(512, width)
 
     def feed(t):
         gather.other(t)
@@ -1015,16 +1004,6 @@
             dgu[at, to] = dgate.astype(bf16)
             dgu[at, pl.ds(pl.multiple_of(ff + i * tile, tile), tile)] = (dhid * silu).astype(bf16)
 
-        h = hid[at, :]
-
-        @pl.loop(0, width // wide)
-        def _(i):
-            to = pl.ds(pl.multiple_of(i * wide, wide), wide)
-            branch[:, to] = dot(h, down[:, to]).astype(bf16)
-
-        out = pltpu.make_async_copy(branch, branch_all.at[at], local.at[0])
-        out.start()
-        out.wait()
         send.wait()
 
     feed(j)
@@ -1055,8 +1034,8 @@
 
 
 def back_kernel(
-    cn, dpn, bn, dgu, wg, wu, h1, dy, gain, branch_all, dh1, dob_all, term, g_own, result,
-    own, branch, cross_in, arrived, bsem, gsem, loads, keep_sem, *scratch,
+    cn, dpn, bn_in, dgu_in, hid, down, wg, wu, h1, dy, gain, dh1, dob_all, term, g_own, result,
+    own, bn, dgu, cross_in, arrived, bsem, gsem, loads, keep_sem, *scratch,
 ):
     sum_refs, ring_refs = scratch[:-4], scratch[-4:]
     rows, width = dy.shape
@@ -1078,8 +1057,13 @@
     ring = RingSum(dpn, *ring_refs)
     blocks = ring_refs[0]
     m = blocks.shape[1]
+    load_dgu = pltpu.make_async_copy(dgu_in, dgu, loads.at[0])
+    load_bn = pltpu.make_async_copy(bn_in, bn, loads.at[1])
+    load_dgu.start()
+    load_bn.start()
     greet_line(cn, ring.ring)
     order = ring.order()
+    load_dgu.wait()
 
     def weight_grad(member):
         outer(bn, dgu, blocks.at[member], pl.ds(pl.multiple_of(member * m, m), m))
@@ -1088,6 +1072,7 @@
     def between(s):
         @pl.when(s == 0)
         def _():
+            load_bn.wait()
             weight_grad(order[0])
             ring.start()
 
@@ -1102,7 +1087,15 @@
             def _():
                 ring.forward(i + 1)
 
+        @pl.when(s == n - 2)
+        def _():
+            weight_grad(order[-1])
+
     line_sums(cn, [total], between)
+    load_hid = pltpu.make_async_copy(hid, dgu.at[:, 0:ff], loads.at[0])
+    load_down = pltpu.make_async_copy(down, bn.at[0:ff], loads.at[1])
+    load_hid.start()
+    load_down.start()
     term[...] = jnp.zeros_like(term)
 
     def norm_back(r):
@@ -1125,16 +1118,16 @@
     total.drain()
 
     part, cross, _, flow, _, _ = sum_refs
-    second = LineSumRows(
-        cn, branch_all, branch, loads, part, cross, cross_in, flow, arrived, bsem
+    second = LineSum(
+        cn,
+        product(dgu.at[:, 0:ff], bn.at[0:ff], plain, rows, width),
+        part, cross, cross_in, flow, arrived, bsem,
     )
+    load_hid.wait()
+    load_down.wait()
 
     def pass_on(s):
         gather.step(s + 1)
-
-        @pl.when(s == 0)
-        def _():
-            weight_grad(order[-1])
 
     line_sums(cn, [second], pass_on)
 
@@ -1388,10 +1381,7 @@
     dma = pltpu.SemaphoreType.DMA
     mib = 2**20
 
-    code = (seg_ids[0] * 2 + valid_mask[0]).astype(bf16)
-    x_ext = jnp.concatenate([x_local, jnp.broadcast_to(code[:, None], (rows, 128))], axis=1)
-    lanes = jnp.arange(128)[None, :]
-    gain_cols = jnp.where(lanes == 0, gain_attn[:, None], gain_mlp[:, None]).astype(bf16)
+    gain_rows = jnp.pad(jnp.stack([gain_attn, gain_mlp]), ((0, 0), (0, 128 - dr)))
     pw = 3 * hw + 128
     ring_sem = dma((4, dpn // 2 + 1))
     x_all, w_qkv, gate_pack, up_pack, down, wo_low = call(
@@ -1404,10 +1394,14 @@
             shape((dpn, ff_rows, width)),
             shape((dr, width)),
         ),
-        (x_ext, w_query, w_key, w_value, gain_cols, w_output, w_gate, w_up, w_down),
-        [ANY] + [VMEM] * 5 + [ANY] * 3,
+        (
+            x_local, seg_ids, valid_mask, gain_rows, w_query, w_key, w_value, w_output,
+            w_gate, w_up, w_down,
+        ),
+        [ANY] + [VMEM] * 7 + [ANY] * 3,
         (ANY, ANY, VMEM, VMEM, ANY, VMEM),
         [
+            pltpu.VMEM((rows, width + 128), bf16),
             pltpu.VMEM((cn, dr, pw), bf16),
             pltpu.VMEM((2, dr, ff * cn), f32),
             pltpu.VMEM((ff_rows, width), f32),
@@ -1452,7 +1446,7 @@
         moved=160 * mib,
     )
     down = down.reshape(ff, width)
-    h1, bn, w_up_c, hid, dgu, branch, dys = call(
+    h1, bn, w_up_c, hid, dgu, dys = call(
         functools.partial(middle_kernel, cn, dpn),
         (
             shape((rows, width), f32),
@@ -1460,7 +1454,6 @@
             shape((dpn, cn, dr, ff)),
             shape((seq, ff)),
             shape((seq, 2 * ff)),
-            shape((seq, width)),
             shape((cn, rows, width)),
         ),
         (
@@ -1468,7 +1461,7 @@
             w_gate_c.reshape(width, ff), down,
         ),
         [VMEM] * 5 + [ANY] * 3,
-        (VMEM, ANY, ANY, VMEM, VMEM, ANY, ANY),
+        (VMEM, ANY, ANY, VMEM, VMEM, ANY),
         [
             pltpu.VMEM((rows, width), bf16),
             pltpu.VMEM((cn, rows, width), bf16),
@@ -1476,7 +1469,6 @@
             pltpu.VMEM((width, ff), bf16),
             pltpu.VMEM((dpn, cn, dr, ff), bf16),
             pltpu.VMEM((ff, width), bf16),
-            pltpu.VMEM((2 * rows, width), bf16),
             dma((5, n)),
             dma((5, n)),
             ring_sem,
@@ -1499,12 +1491,13 @@
             shape((cn, dr, 2 * ff)),
             shape((rows, width)),
         ),
-        (bn, dgu, w_gate_c, w_up_c, h1, dy_local, gains, branch.reshape(cn, rows, width)),
-        [VMEM] * 7 + [ANY],
+        (bn, dgu, hid, down, w_gate_c, w_up_c, h1, dy_local, gains),
+        [ANY] * 4 + [VMEM] * 5,
         (VMEM, ANY, VMEM, VMEM, VMEM),
         [
             pltpu.VMEM((rows, width), bf16),
-            pltpu.VMEM((rows, width), bf16),
+            pltpu.VMEM((seq, width), bf16),
+            pltpu.VMEM((seq, 2 * ff), bf16),
             pltpu.VMEM((n, rows, width), bf16),
             pltpu.VMEM((n + 1, rows, width), bf16),
             dma((4, n + 1)),

time: 462 us -> 456 us (0.987)
  no operation moved by 1% of the time
where the time goes in v7:
time: 456 us; the launch traced here: 454 us
  Pallas kernels  445 us (98%)
    pallas_call x5, Pallas kernels, call(): pl.pallas_call(kernel, out_shape=outs, in_specs=specs_in, out_specs=specs...  440 us

profile of v7, /device:TPU:9, one launch (start us, length us, event | category | flops | bytes accessed | tf_op | source)
XLA Modules:
  0.0 453.7 jit_solution(14005378778343537064)
XLA Ops:
  0.6 1.2 select_maximum_fusion.gain_rows
  1.9 73.5 %shard_map.220 = (bf16[8,128,2176]{2,1,0:T(8,128)(2,1)}, bf16[4,8,64,896]{3,2,1,0:T(8,128)(2,1)}, bf16[8,64,1024]{2,1,0:T(8,128)(2,1)}, bf16[8,64,1024]{2,1,0:T(...) custom-call(bf16[128,2048]{1,0:T(8,128)(2,1)} %bitcast.25, s32[1,128]{1,0:T(1,128)} %seg.1, ...), custom_call_target="tpu_custom_call" | custom-call | bytes 167772160 | tf_op jit(solution)/shard_map/pallas_call | solution.py:1337
  75.4 0.6 maximum_bitcast_fusion.inverse
  76.0 58.8 %shard_map.221 = (bf16[1024,2048]{1,0:T(8,128)(2,1)}, bf16[1024,768]{1,0:T(8,128)(2,1)}, bf16[1024,256]{1,0:T(8,128)(2,1)}, f32[1,256]{1,0:T(1,128)}, f32[8,2048...) custom-call(bf16[8,128,2176]{2,1,0:T(8,128)(2,1)} %get-tuple-element, ...), custom_call_target="tpu_custom_call" | custom-call | bytes 167772160 | tf_op jit(solution)/shard_map/pallas_call | solution.py:1337
  134.7 86.9 %shard_map.222 = (f32[128,2048]{1,0:T(8,128)}, bf16[8,128,2048]{2,1,0:T(8,128)(2,1)}, bf16[4,8,64,1024]{3,2,1,0:T(8,128)(2,1)}, bf16[1024,1024]{1,0:T(8,128)(2,1...) custom-call(bf16[1024,256]{1,0:T(8,128)(2,1)} %get-tuple-element.59.o, bf16[256,2048]{1,0:T(8,128)(2,1)} %bitcast.28, ...), custom_call_target="tpu_custom_call" | custom-call | bytes 167772160 | tf_op jit(solution)/shard_map/pallas_call | solution.py:1337
  221.6 112.4 %shard_map.223 = (f32[128,2048]{1,0:T(8,128)}, bf16[8,128,2048]{2,1,0:T(8,128)(2,1)}, f32[1,2048]{1,0:T(1,128)}, bf16[8,64,2048]{2,1,0:T(8,128)(2,1)}, bf16[128,2048]{1,0:T(8,128)(2,1)}) custom-call(bf16[1024,2048]{1,0:T(8,128)(2,1)} %bitcast.30, bf16[1024,2048]{1,0:T(8,128)(2,1)} %get-tuple-element.66.dgu_in, bf16[1024,1024]{1,0:T(8,128)(2,1)} %get-tuple-element.67.hid, ...), custom_call_target="tpu_custom_call" | custom-call | bytes 167772160 | tf_op jit(solution)/shard_map/pallas_call | solution.py:1337
  334.0 108.0 %shard_map.224 = (bf16[128,2048]{1,0:T(8,128)(2,1)}, f32[3,1,2048]{2,1,0:T(1,128)}, bf16[8,64,2048]{2,1,0:T(8,128)(2,1)}, bf16[256,2048]{1,0:T(8,128)(2,1)}, f32...) custom-call(bf16[8,64,2048]{2,1,0:T(8,128)(2,1)} %get-tuple-element.71.g_gu, ...), custom_call_target="tpu_custom_call" | custom-call | bytes 167772160 | tf_op jit(solution)/shard_map/pallas_call | solution.py:1337
  442.1 0.0 copy-start
  442.1 0.0 copy-start.1
  442.1 0.8 fusion
  442.9 0.6 dynamic-slice_bitcast_fusion
  443.5 5.7 %shard_map.225 = (f32[64,2048]{1,0:T(8,128)}, f32[64,2048]{1,0:T(8,128)}, f32[64,2048]{1,0:T(8,128)}, f32[64,2048]{1,0:T(8,128)}, f32[64,8192]{1,0:T(8,128)}, /*index=5*/f32[64,8192]{1,0:T(8,128)}, f32[256,2048]{1,0:T(8,128)}) custom-call(bf16[8,64,768]{2,1,0:T(8,128)(2,1)} %get-tuple-element.84.qkv_in, bf16[8,64,2048]{2,1,0:T(8,128)(2,1)} %get-tuple-element.85.gu_in, ...), custom_call_target="tpu_custom_call" | custom-call | tf_op jit(solution)/shard_map/pallas_call | solution.py:1554
  449.2 1.1 slice.11
  450.9 0.0 copy-done
  451.0 0.8 copy.27
  451.8 0.0 copy-done.1
  451.8 0.8 copy.28
  (1 shorter events, 0.0 us)
Async XLA Ops:
  442.1 8.9 %copy-start = (bf16[128,2048]{1,0:T(8,128)(2,1)S(1)}, bf16[128,2048]{1,0:T(8,128)(2,1)}, u32[]{:S(2)}) copy-start(bf16[128,2048]{1,0:T(8,128)(2,1)} %get-tuple-element.70) | copy-start | bytes 1572868
  442.1 9.7 %copy-start.1 = (bf16[128,2048]{1,0:T(8,128)(2,1)S(1)}, bf16[128,2048]{1,0:T(8,128)(2,1)}, u32[]{:S(2)}) copy-start(bf16[128,2048]{1,0:T(8,128)(2,1)} %get-tuple-element.83) | copy-start | bytes 1572868

commit v8 on v7

--- a/solution.py
+++ b/solution.py
@@ -697,7 +697,7 @@
 
 def front_kernel(
     cn, dpn, x_in, seg, valid, gain_rows, wq, wk, wv, wo, gate_in, up_in, down_in,
-    x_all, pack_all, gate, up, down_all, wo_low,
+    x_all, pack_all, gate, up, down_all, wo_low, down_rest,
     x, pack, wide, tall, down, gsem, ssem, rsem, dsem, local,
 ):
     c, d = lax.axis_index("ctx"), lax.axis_index("dp")
@@ -741,7 +741,9 @@
         pack[to, :, 3 * hw :] = gains
     swap.start()
     loads[2].wait()
-    down[...] = tall[...].astype(bf16)
+    split = down.shape[0]
+    down[...] = tall[0:split, :].astype(bf16)
+    down_rest[...] = tall[split:, :].astype(bf16)
     down_ring.start()
     keep_down = pltpu.make_async_copy(down, down_all.at[d], local.at[5])
     keep_down.start()
@@ -925,9 +927,9 @@
 
 
 def middle_kernel(
-    cn, dpn, o, wo, x, gain, dy, up, gate_all, down_all,
-    h1, bn_all, up_all, hid, dgu, dys_all,
-    own, bn, dys, wg, wu, down, gsem, ysem, rsem, local, *sum_refs,
+    cn, dpn, o, wo, x, gain, dy, up, gate_all, down_half, down_rest,
+    h1, bn_all, up_all, hid, dgu, dys_all, down_all,
+    own, bn, dys, wg, wu, down_by, gsem, ysem, rsem, dsem, local, *sum_refs,
 ):
     c, d = lax.axis_index("ctx"), lax.axis_index("dp")
     _, j, k, n, _ = place(cn)
@@ -937,13 +939,20 @@
     gather = LineGather(cn, own, bn, gsem)
     gather_dy = LineGather(cn, dy, dys, ysem)
     ring = RingGather(dpn, up, up_all, rsem)
+    split = down_rest.shape[0]
+    rest_ring = RingGather(dpn, down_rest, down_by.at[:, pl.ds(split, split)], dsem)
+    keep_rest = pltpu.make_async_copy(
+        down_rest, down_by.at[d, pl.ds(split, split)], local.at[5]
+    )
     total = LineSum(cn, product(o, wo, plain, rows, width), *sum_refs)
     greet_line(cn, ring)
     ring.start()
+    rest_ring.start()
+    keep_rest.start()
     keep_up = pltpu.make_async_copy(up, up_all.at[d], local.at[0])
     loads = [
         pltpu.make_async_copy(src, dst, local.at[i])
-        for i, (src, dst) in enumerate(((gate_all, wg), (down_all, down)), 2)
+        for i, (src, dst) in enumerate(((gate_all, wg), (down_half, down_by.at[:, pl.ds(0, split)])), 2)
     ]
     keep_up.start()
     for load in loads:
@@ -957,6 +966,7 @@
         @pl.when(s == n - 2)
         def _():
             ring.forward()
+            rest_ring.forward()
 
     line_sums(cn, [total], between)
 
@@ -975,11 +985,15 @@
     keep_up.wait()
     for load in loads:
         load.wait()
+    rest_ring.finish()
+    keep_rest.wait()
+    store_down = pltpu.make_async_copy(down_by, down_all, local.at[6])
+    store_down.start()
     ring.finish()
     load_up = pltpu.make_async_copy(up_all, wu, local.at[0])
     load_up.start()
     load_up.wait()
-    wgate, wup = wg, wu.reshape(width, ff)
+    wgate, wup, down = wg, wu.reshape(width, ff), down_by.reshape(ff, width)
     tile = min(512, ff)
 
     def feed(t):
@@ -1031,6 +1045,7 @@
 
     gather.sent()
     store_dy.wait()
+    store_down.wait()
 
 
 def back_kernel(
@@ -1384,28 +1399,29 @@
     gain_rows = jnp.pad(jnp.stack([gain_attn, gain_mlp]), ((0, 0), (0, 128 - dr)))
     pw = 3 * hw + 128
     ring_sem = dma((4, dpn // 2 + 1))
-    x_all, w_qkv, gate_pack, up_pack, down, wo_low = call(
+    x_all, w_qkv, gate_pack, up_pack, down_half, wo_low, down_rest = call(
         functools.partial(front_kernel, cn, dpn),
         (
             shape((cn, rows, width + 128)),
             shape((dpn, cn, dr, pw)),
             shape((cn, dr, ff)),
             shape((cn, dr, ff)),
-            shape((dpn, ff_rows, width)),
+            shape((dpn, ff_rows // 2, width)),
             shape((dr, width)),
+            shape((ff_rows // 2, width)),
         ),
         (
             x_local, seg_ids, valid_mask, gain_rows, w_query, w_key, w_value, w_output,
             w_gate, w_up, w_down,
         ),
         [ANY] + [VMEM] * 7 + [ANY] * 3,
-        (ANY, ANY, VMEM, VMEM, ANY, VMEM),
+        (ANY, ANY, VMEM, VMEM, ANY, VMEM, VMEM),
         [
             pltpu.VMEM((rows, width + 128), bf16),
             pltpu.VMEM((cn, dr, pw), bf16),
             pltpu.VMEM((2, dr, ff * cn), f32),
             pltpu.VMEM((ff_rows, width), f32),
-            pltpu.VMEM((ff_rows, width), bf16),
+            pltpu.VMEM((ff_rows // 2, width), bf16),
             dma((5, n)),
             dma((2, cn)),
             dma((4, dpn // 2 + 1, cn)),
@@ -1445,8 +1461,7 @@
         2,
         moved=160 * mib,
     )
-    down = down.reshape(ff, width)
-    h1, bn, w_up_c, hid, dgu, dys = call(
+    h1, bn, w_up_c, hid, dgu, dys, down = call(
         functools.partial(middle_kernel, cn, dpn),
         (
             shape((rows, width), f32),
@@ -1455,24 +1470,26 @@
             shape((seq, ff)),
             shape((seq, 2 * ff)),
             shape((cn, rows, width)),
+            shape((dpn, ff_rows, width)),
         ),
         (
             o, wo.reshape(hw, width), x_local, gains, dy_local, up_own,
-            w_gate_c.reshape(width, ff), down,
+            w_gate_c.reshape(width, ff), down_half, down_rest,
         ),
-        [VMEM] * 5 + [ANY] * 3,
-        (VMEM, ANY, ANY, VMEM, VMEM, ANY),
+        [VMEM] * 5 + [ANY] * 4,
+        (VMEM, ANY, ANY, VMEM, VMEM, ANY, ANY),
         [
             pltpu.VMEM((rows, width), bf16),
             pltpu.VMEM((cn, rows, width), bf16),
             pltpu.VMEM((cn, rows, width), bf16),
             pltpu.VMEM((width, ff), bf16),
             pltpu.VMEM((dpn, cn, dr, ff), bf16),
-            pltpu.VMEM((ff, width), bf16),
+            pltpu.VMEM((dpn, ff_rows, width), bf16),
             dma((5, n)),
             dma((5, n)),
             ring_sem,
-            dma((5,)),
+            ring_sem,
+            dma((7,)),
         ]
         + line_scratch,
         3,
@@ -1491,7 +1508,7 @@
             shape((cn, dr, 2 * ff)),
             shape((rows, width)),
         ),
-        (bn, dgu, hid, down, w_gate_c, w_up_c, h1, dy_local, gains),
+        (bn, dgu, hid, down.reshape(ff, width), w_gate_c, w_up_c, h1, dy_local, gains),
         [ANY] * 4 + [VMEM] * 5,
         (VMEM, ANY, VMEM, VMEM, VMEM),
         [

time: 456 us -> 451 us (0.989)
  Pallas kernels: 445 us -> 440 us
    pallas_call x5, Pallas kernels: 440 us -> 435 us  [call(): pl.pallas_call(kernel, out_shape=outs, in_specs=specs_in, out_specs=specs...]
where the time goes in v8:
time: 451 us; the launch traced here: 449 us
  Pallas kernels  440 us (98%)
    pallas_call x5, Pallas kernels, call(): pl.pallas_call(kernel, out_shape=outs, in_specs=specs_in, out_specs=specs...  435 us

profile of v8, /device:TPU:9, one launch (start us, length us, event | category | flops | bytes accessed | tf_op | source)
XLA Modules:
  0.0 448.8 jit_solution(13706537227183222671)
XLA Ops:
  0.6 1.2 select_maximum_fusion.gain_rows
  1.9 63.9 %shard_map.220 = (bf16[8,128,2176]{2,1,0:T(8,128)(2,1)}, bf16[4,8,64,896]{3,2,1,0:T(8,128)(2,1)}, bf16[8,64,1024]{2,1,0:T(8,128)(2,1)}, bf16[8,64,1024]{2,1,0:T(...) custom-call(bf16[128,2048]{1,0:T(8,128)(2,1)} %bitcast.23, ...), custom_call_target="tpu_custom_call" | custom-call | bytes 167772160 | tf_op jit(solution)/shard_map/pallas_call | solution.py:1352
  65.8 0.6 maximum_bitcast_fusion.inverse
  66.4 61.7 %shard_map.221 = (bf16[1024,2048]{1,0:T(8,128)(2,1)}, bf16[1024,768]{1,0:T(8,128)(2,1)}, bf16[1024,256]{1,0:T(8,128)(2,1)}, f32[1,256]{1,0:T(1,128)}, f32[8,2048...) custom-call(bf16[8,128,2176]{2,1,0:T(8,128)(2,1)} %get-tuple-element, ...), custom_call_target="tpu_custom_call" | custom-call | bytes 167772160 | tf_op jit(solution)/shard_map/pallas_call | solution.py:1352
  128.1 88.9 %shard_map.222 = (f32[128,2048]{1,0:T(8,128)}, bf16[8,128,2048]{2,1,0:T(8,128)(2,1)}, bf16[4,8,64,1024]{3,2,1,0:T(8,128)(2,1)}, bf16[1024,1024]{1,0:T(8,128)(2,1...) custom-call(bf16[1024,256]{1,0:T(8,128)(2,1)} %get-tuple-element.61.o, ...), custom_call_target="tpu_custom_call" | custom-call | bytes 167772160 | tf_op jit(solution)/shard_map/pallas_call | solution.py:1352
  217.0 112.4 %shard_map.223 = (f32[128,2048]{1,0:T(8,128)}, bf16[8,128,2048]{2,1,0:T(8,128)(2,1)}, f32[1,2048]{1,0:T(1,128)}, bf16[8,64,2048]{2,1,0:T(8,128)(2,1)}, bf16[128,2048]{1,0:T(8,128)(2,1)}) custom-call(bf16[1024,2048]{1,0:T(8,128)(2,1)} %bitcast.28, bf16[1024,2048]{1,0:T(8,128)(2,1)} %get-tuple-element.69.dgu_in, bf16[1024,1024]{1,0:T(8,128)(2,1)} %get-tuple-element.70.hid, ...), custom_call_target="tpu_custom_call" | custom-call | bytes 167772160 | tf_op jit(solution)/shard_map/pallas_call | solution.py:1352
  329.4 107.8 %shard_map.224 = (bf16[128,2048]{1,0:T(8,128)(2,1)}, f32[3,1,2048]{2,1,0:T(1,128)}, bf16[8,64,2048]{2,1,0:T(8,128)(2,1)}, bf16[256,2048]{1,0:T(8,128)(2,1)}, f32...) custom-call(bf16[8,64,2048]{2,1,0:T(8,128)(2,1)} %get-tuple-element.75.g_gu, ...), custom_call_target="tpu_custom_call" | custom-call | bytes 167772160 | tf_op jit(solution)/shard_map/pallas_call | solution.py:1352
  437.2 0.7 fusion
  438.0 0.6 dynamic-slice_bitcast_fusion
  438.6 0.0 copy-start
  438.6 0.0 copy-start.1
  438.6 5.8 %shard_map.225 = (f32[64,2048]{1,0:T(8,128)}, f32[64,2048]{1,0:T(8,128)}, f32[64,2048]{1,0:T(8,128)}, f32[64,2048]{1,0:T(8,128)}, f32[64,8192]{1,0:T(8,128)}, /*index=5*/f32[64,8192]{1,0:T(8,128)}, f32[256,2048]{1,0:T(8,128)}) custom-call(bf16[8,64,768]{2,1,0:T(8,128)(2,1)} %get-tuple-element.88.qkv_in, bf16[8,64,2048]{2,1,0:T(8,128)(2,1)} %get-tuple-element.89.gu_in, ...), custom_call_target="tpu_custom_call" | custom-call | tf_op jit(solution)/shard_map/pallas_call | solution.py:1571
  444.3 1.1 slice.11
  446.1 0.0 copy-done
  446.1 0.8 copy.27
  446.9 0.0 copy-done.1
  446.9 0.8 copy.28
  (1 shorter events, 0.0 us)
Async XLA Ops:
  438.6 7.6 %copy-start = (bf16[128,2048]{1,0:T(8,128)(2,1)S(1)}, bf16[128,2048]{1,0:T(8,128)(2,1)}, u32[]{:S(2)}) copy-start(bf16[128,2048]{1,0:T(8,128)(2,1)} %get-tuple-element.74) | copy-start | bytes 1572868
  438.6 8.4 %copy-start.1 = (bf16[128,2048]{1,0:T(8,128)(2,1)S(1)}, bf16[128,2048]{1,0:T(8,128)(2,1)}, u32[]{:S(2)}) copy-start(bf16[128,2048]{1,0:T(8,128)(2,1)} %get-tuple-element.87) | copy-start | bytes 1572868

commit v9 on v8

--- a/solution.py
+++ b/solution.py
@@ -44,10 +44,10 @@
     )
 
 
-def by_rows(count, work, step=16):
+def by_rows(count, work, step=16, start=0):
     @pl.loop(0, count // step)
     def _(i):
-        work(pl.ds(pl.multiple_of(i * step, step), step))
+        work(pl.ds(pl.multiple_of(start + i * step, step), step))
 
 
 def place(cn):
@@ -164,6 +164,39 @@
         for o in range(self.cn // 2):
             self.other(o)
         self.sent()
+
+
+class PairGather:
+    def __init__(self, cn, own, full, sem):
+        self.cn, half = cn, own.shape[0] // 2
+        self.parts = []
+        for i in range(2):
+            at = pl.ds(i * half, half)
+            self.parts.append(LineGather(cn, own.at[at], full.at[:, at], sem.at[i]))
+
+    def start(self):
+        for part in self.parts:
+            part.start()
+
+    def step(self, s):
+        for part in self.parts:
+            part.step(s)
+
+    def forward(self, first=1, last=None):
+        for s in range(first, self.cn // 2 if last is None else last + 1):
+            self.step(s)
+
+    def other(self, o):
+        for part in self.parts:
+            part.other(o)
+
+    def sent(self):
+        for part in self.parts:
+            part.sent()
+
+    def finish(self):
+        for part in self.parts:
+            part.finish()
 
 
 class Swap:
@@ -552,24 +585,32 @@
         self.cross, self.cross_in, self.flow = cross, cross_in, flow
         self.arrived, self.sem = arrived, sem
 
-    def across(self, t):
+    def half(self, h):
+        count = self.cross.shape[1] // 2
+        return pl.ds(h * count, count)
+
+    def across(self, t, h):
         _, _, _, _, sib = place(self.cn)
         return remote(
-            self.cross.at[t],
-            self.cross_in.at[t],
-            self.sem.at[0, t],
-            self.sem.at[2, t],
+            self.cross.at[t, self.half(h)],
+            self.cross_in.at[t, self.half(h)],
+            self.sem.at[0, t, h],
+            self.sem.at[2, t, h],
             {"ctx": sib},
         )
 
-    def along(self, t, slot, target):
+    def along(self, t, slot, target, h):
         return remote(
-            self.flow.at[t],
-            self.arrived.at[slot],
-            self.sem.at[1, t],
-            self.sem.at[3, slot],
+            self.flow.at[t, self.half(h)],
+            self.arrived.at[slot, self.half(h)],
+            self.sem.at[1, t, h],
+            self.sem.at[3, slot, h],
             {"ctx": target},
         )
+
+    def rows(self, h, work):
+        count = self.cross.shape[1] // 2
+        by_rows(count, work, min(16, count), h * count)
 
     def produce(self, t, slot):
         _, _, k, _, _ = place(self.cn)
@@ -579,52 +620,60 @@
         def low(r):
             self.cross[t, r, :] = part[1 - k, r, :].astype(bf16)
 
-        by_rows(self.cross.shape[1], low)
-        self.across(t).start()
-
-    def add(self, part, came):
+        for h in range(2):
+            self.rows(h, low)
+            self.across(t, h).start()
+
+    def add(self, part, came, h):
         def more(r):
             part[r, :] += came[r, :].astype(f32)
 
-        by_rows(part.shape[0], more)
-
-    def collect(self, t, slot):
+        self.rows(h, more)
+
+    def collect(self, t, slot, h):
         _, j, k, n, sib = place(self.cn)
         part = self.part.at[slot, k]
-        self.across(t).wait_recv()
-        self.add(part, self.cross_in.at[t])
+        self.across(t, h).wait_recv()
+        self.add(part, self.cross_in.at[t], h)
 
         @pl.when((j > 0) & (t >= j))
         def _():
-            self.along(t, t, sib).wait_recv()
-            self.add(part, self.arrived.at[t])
+            self.along(t, t, sib, h).wait_recv()
+            self.add(part, self.arrived.at[t], h)
 
         @pl.when((j < n - 1) & (t <= j))
         def _():
             slot_in = jnp.where(t == j, n, t)
-            self.along(t, slot_in, sib).wait_recv()
-            self.add(part, self.arrived.at[slot_in])
-
-    def send(self, t, slot, up):
+            self.along(t, slot_in, sib, h).wait_recv()
+            self.add(part, self.arrived.at[slot_in], h)
+
+    def send(self, t, slot, up, h):
         c, j, k, n, _ = place(self.cn)
 
         def low(r):
             self.flow[t, r, :] = self.part[slot, k, r, :].astype(bf16)
 
-        by_rows(self.flow.shape[1], low)
+        self.rows(h, low)
         there = t if up else jnp.where(t == j - 1, n, t)
-        self.along(t, there, c + 2 if up else c - 2).start()
+        self.along(t, there, c + 2 if up else c - 2, h).start()
+
+    def pass_on(self, t, slot, up):
+        for h in range(2):
+            self.collect(t, slot, h)
+            self.send(t, slot, up, h)
 
     def drain(self):
         _, j, _, n, sib = place(self.cn)
 
         @pl.loop(0, n)
         def _(t):
-            self.across(t).wait_send()
+            for h in range(2):
+                self.across(t, h).wait_send()
 
             @pl.when(t != j)
             def _():
-                self.along(t, t, sib).wait_send()
+                for h in range(2):
+                    self.along(t, t, sib, h).wait_send()
 
 
 def line_sums(cn, sums, between=None):
@@ -647,13 +696,11 @@
 
             @pl.when(s >= j)
             def _():
-                total.collect(to_up, 0)
-                total.send(to_up, 0, True)
+                total.pass_on(to_up, 0, True)
 
             @pl.when(s >= n - 1 - j)
             def _():
-                total.collect(to_down, 1)
-                total.send(to_down, 1, False)
+                total.pass_on(to_down, 1, False)
 
         if between is not None:
             between(s)
@@ -661,7 +708,8 @@
     for total in sums:
         total.produce(j, 0)
     for total in sums:
-        total.collect(j, 0)
+        for h in range(2):
+            total.collect(j, 0, h)
 
 
 def sum_scratch(cn, rows, width):
@@ -672,7 +720,7 @@
         pltpu.VMEM((n, rows, width), bf16),
         pltpu.VMEM((n, rows, width), bf16),
         pltpu.VMEM((n + 1, rows, width), bf16),
-        pltpu.SemaphoreType.DMA((4, n + 1)),
+        pltpu.SemaphoreType.DMA((4, n + 1, 2)),
     ]
 
 
@@ -705,7 +753,7 @@
     part = gate_in.shape[1] // (cn * dpn)
     mine = pack_all.at[d]
     swap = Swap(cn, pack, mine, ssem, local.at[0])
-    gather = LineGather(cn, x, x_all, gsem)
+    gather = PairGather(cn, x, x_all, gsem)
     ring = RingPieces(dpn, pack_all, rsem)
     down_ring = RingGather(dpn, down, down_all, dsem)
     greet_ctx(cn)
@@ -936,8 +984,8 @@
     rows, width = x.shape
     ff = hid.shape[1]
     block = 2 * rows
-    gather = LineGather(cn, own, bn, gsem)
-    gather_dy = LineGather(cn, dy, dys, ysem)
+    gather = PairGather(cn, own, bn, gsem)
+    gather_dy = PairGather(cn, dy, dys, ysem)
     ring = RingGather(dpn, up, up_all, rsem)
     split = down_rest.shape[0]
     rest_ring = RingGather(dpn, down_rest, down_by.at[:, pl.ds(split, split)], dsem)
@@ -1126,7 +1174,7 @@
         own[r, :] = grad.astype(bf16)
 
     by_rows(rows, norm_back)
-    gather = LineGather(cn, own, dob_all, gsem)
+    gather = PairGather(cn, own, dob_all, gsem)
     gather.start()
     keep = pltpu.make_async_copy(own, dob_all.at[c], keep_sem)
     keep.start()
@@ -1422,7 +1470,7 @@
             pltpu.VMEM((2, dr, ff * cn), f32),
             pltpu.VMEM((ff_rows, width), f32),
             pltpu.VMEM((ff_rows // 2, width), bf16),
-            dma((5, n)),
+            dma((2, 5, n)),
             dma((2, cn)),
             dma((4, dpn // 2 + 1, cn)),
             ring_sem,
@@ -1485,8 +1533,8 @@
             pltpu.VMEM((width, ff), bf16),
             pltpu.VMEM((dpn, cn, dr, ff), bf16),
             pltpu.VMEM((dpn, ff_rows, width), bf16),
-            dma((5, n)),
-            dma((5, n)),
+            dma((2, 5, n)),
+            dma((2, 5, n)),
             ring_sem,
             ring_sem,
             dma((7,)),
@@ -1517,8 +1565,8 @@
             pltpu.VMEM((seq, 2 * ff), bf16),
             pltpu.VMEM((n, rows, width), bf16),
             pltpu.VMEM((n + 1, rows, width), bf16),
-            dma((4, n + 1)),
-            dma((5, n)),
+            dma((4, n + 1, 2)),
+            dma((2, 5, n)),
             dma((2,)),
             dma,
         ]

time: 451 us -> 454 us (level); the launches traced: 449 us -> 446 us
  no operation moved by 1% of the time
where the time goes in v9:
time: 454 us; the launch traced here: 446 us
  Pallas kernels  437 us (96%)
    pallas_call x5, Pallas kernels, call(): pl.pallas_call(kernel, out_shape=outs, in_specs=specs_in, out_specs=specs...  432 us

profile of v9, /device:TPU:9, one launch (start us, length us, event | category | flops | bytes accessed | tf_op | source)
XLA Modules:
  0.0 446.1 jit_solution(1255214971526659436)
XLA Ops:
  0.6 1.2 select_maximum_fusion.gain_rows
  1.9 64.0 %shard_map.220 = (bf16[8,128,2176]{2,1,0:T(8,128)(2,1)}, bf16[4,8,64,896]{3,2,1,0:T(8,128)(2,1)}, bf16[8,64,1024]{2,1,0:T(8,128)(2,1)}, bf16[8,64,1024]{2,1,0:T(...) custom-call(bf16[128,2048]{1,0:T(8,128)(2,1)} %bitcast.23, ...), custom_call_target="tpu_custom_call" | custom-call | bytes 167772160 | tf_op jit(solution)/shard_map/pallas_call | solution.py:1400
  65.9 0.6 maximum_bitcast_fusion.inverse
  66.5 61.1 %shard_map.221 = (bf16[1024,2048]{1,0:T(8,128)(2,1)}, bf16[1024,768]{1,0:T(8,128)(2,1)}, bf16[1024,256]{1,0:T(8,128)(2,1)}, f32[1,256]{1,0:T(1,128)}, f32[8,2048...) custom-call(bf16[8,128,2176]{2,1,0:T(8,128)(2,1)} %get-tuple-element, ...), custom_call_target="tpu_custom_call" | custom-call | bytes 167772160 | tf_op jit(solution)/shard_map/pallas_call | solution.py:1400
  127.6 88.7 %shard_map.222 = (f32[128,2048]{1,0:T(8,128)}, bf16[8,128,2048]{2,1,0:T(8,128)(2,1)}, bf16[4,8,64,1024]{3,2,1,0:T(8,128)(2,1)}, bf16[1024,1024]{1,0:T(8,128)(2,1...) custom-call(bf16[1024,256]{1,0:T(8,128)(2,1)} %get-tuple-element.61.o, ...), custom_call_target="tpu_custom_call" | custom-call | bytes 167772160 | tf_op jit(solution)/shard_map/pallas_call | solution.py:1400
  216.3 111.2 %shard_map.223 = (f32[128,2048]{1,0:T(8,128)}, bf16[8,128,2048]{2,1,0:T(8,128)(2,1)}, f32[1,2048]{1,0:T(1,128)}, bf16[8,64,2048]{2,1,0:T(8,128)(2,1)}, bf16[128,2048]{1,0:T(8,128)(2,1)}) custom-call(bf16[1024,2048]{1,0:T(8,128)(2,1)} %bitcast.28, bf16[1024,2048]{1,0:T(8,128)(2,1)} %get-tuple-element.69.dgu_in, bf16[1024,1024]{1,0:T(8,128)(2,1)} %get-tuple-element.70.hid, ...), custom_call_target="tpu_custom_call" | custom-call | bytes 167772160 | tf_op jit(solution)/shard_map/pallas_call | solution.py:1400
  327.5 106.6 %shard_map.224 = (bf16[128,2048]{1,0:T(8,128)(2,1)}, f32[3,1,2048]{2,1,0:T(1,128)}, bf16[8,64,2048]{2,1,0:T(8,128)(2,1)}, bf16[256,2048]{1,0:T(8,128)(2,1)}, f32...) custom-call(bf16[8,64,2048]{2,1,0:T(8,128)(2,1)} %get-tuple-element.75.g_gu, ...), custom_call_target="tpu_custom_call" | custom-call | bytes 167772160 | tf_op jit(solution)/shard_map/pallas_call | solution.py:1400
  434.1 0.7 fusion
  434.8 0.6 dynamic-slice_bitcast_fusion
  435.4 0.0 copy-start
  435.4 0.0 copy-start.1
  435.4 5.8 %shard_map.225 = (f32[64,2048]{1,0:T(8,128)}, f32[64,2048]{1,0:T(8,128)}, f32[64,2048]{1,0:T(8,128)}, f32[64,2048]{1,0:T(8,128)}, f32[64,8192]{1,0:T(8,128)}, /*index=5*/f32[64,8192]{1,0:T(8,128)}, f32[256,2048]{1,0:T(8,128)}) custom-call(bf16[8,64,768]{2,1,0:T(8,128)(2,1)} %get-tuple-element.88.qkv_in, bf16[8,64,2048]{2,1,0:T(8,128)(2,1)} %get-tuple-element.89.gu_in, ...), custom_call_target="tpu_custom_call" | custom-call | tf_op jit(solution)/shard_map/pallas_call | solution.py:1619
  441.2 1.1 slice.11
  443.0 0.0 copy-done
  443.0 0.8 copy.27
  443.8 0.0 copy-done.1
  443.8 0.8 copy.28
  (1 shorter events, 0.0 us)
Async XLA Ops:
  435.4 7.6 %copy-start = (bf16[128,2048]{1,0:T(8,128)(2,1)S(1)}, bf16[128,2048]{1,0:T(8,128)(2,1)}, u32[]{:S(2)}) copy-start(bf16[128,2048]{1,0:T(8,128)(2,1)} %get-tuple-element.74) | copy-start | bytes 1572868
  435.4 8.4 %copy-start.1 = (bf16[128,2048]{1,0:T(8,128)(2,1)S(1)}, bf16[128,2048]{1,0:T(8,128)(2,1)}, u32[]{:S(2)}) copy-start(bf16[128,2048]{1,0:T(8,128)(2,1)} %get-tuple-element.87) | copy-start | bytes 1572868

commit v10 on v8

--- a/solution.py
+++ b/solution.py
@@ -166,6 +166,39 @@
         self.sent()
 
 
+class PairGather:
+    def __init__(self, cn, own, full, sem):
+        self.cn, half = cn, own.shape[0] // 2
+        self.parts = []
+        for i in range(2):
+            at = pl.ds(i * half, half)
+            self.parts.append(LineGather(cn, own.at[at], full.at[:, at], sem.at[i]))
+
+    def start(self):
+        for part in self.parts:
+            part.start()
+
+    def step(self, s):
+        for part in self.parts:
+            part.step(s)
+
+    def forward(self, first=1, last=None):
+        for s in range(first, self.cn // 2 if last is None else last + 1):
+            self.step(s)
+
+    def other(self, o):
+        for part in self.parts:
+            part.other(o)
+
+    def sent(self):
+        for part in self.parts:
+            part.sent()
+
+    def finish(self):
+        for part in self.parts:
+            part.finish()
+
+
 class Swap:
     def __init__(self, cn, src, dst, sem, local, pick=None):
         self.cn, self.sem, self.local = cn, sem, local
@@ -705,7 +738,7 @@
     part = gate_in.shape[1] // (cn * dpn)
     mine = pack_all.at[d]
     swap = Swap(cn, pack, mine, ssem, local.at[0])
-    gather = LineGather(cn, x, x_all, gsem)
+    gather = PairGather(cn, x, x_all, gsem)
     ring = RingPieces(dpn, pack_all, rsem)
     down_ring = RingGather(dpn, down, down_all, dsem)
     greet_ctx(cn)
@@ -936,8 +969,8 @@
     rows, width = x.shape
     ff = hid.shape[1]
     block = 2 * rows
-    gather = LineGather(cn, own, bn, gsem)
-    gather_dy = LineGather(cn, dy, dys, ysem)
+    gather = PairGather(cn, own, bn, gsem)
+    gather_dy = PairGather(cn, dy, dys, ysem)
     ring = RingGather(dpn, up, up_all, rsem)
     split = down_rest.shape[0]
     rest_ring = RingGather(dpn, down_rest, down_by.at[:, pl.ds(split, split)], dsem)
@@ -1126,7 +1159,7 @@
         own[r, :] = grad.astype(bf16)
 
     by_rows(rows, norm_back)
-    gather = LineGather(cn, own, dob_all, gsem)
+    gather = PairGather(cn, own, dob_all, gsem)
     gather.start()
     keep = pltpu.make_async_copy(own, dob_all.at[c], keep_sem)
     keep.start()
@@ -1422,7 +1455,7 @@
             pltpu.VMEM((2, dr, ff * cn), f32),
             pltpu.VMEM((ff_rows, width), f32),
             pltpu.VMEM((ff_rows // 2, width), bf16),
-            dma((5, n)),
+            dma((2, 5, n)),
             dma((2, cn)),
             dma((4, dpn // 2 + 1, cn)),
             ring_sem,
@@ -1485,8 +1518,8 @@
             pltpu.VMEM((width, ff), bf16),
             pltpu.VMEM((dpn, cn, dr, ff), bf16),
             pltpu.VMEM((dpn, ff_rows, width), bf16),
-            dma((5, n)),
-            dma((5, n)),
+            dma((2, 5, n)),
+            dma((2, 5, n)),
             ring_sem,
             ring_sem,
             dma((7,)),
@@ -1518,7 +1551,7 @@
             pltpu.VMEM((n, rows, width), bf16),
             pltpu.VMEM((n + 1, rows, width), bf16),
             dma((4, n + 1)),
-            dma((5, n)),
+            dma((2, 5, n)),
             dma((2,)),
             dma,
         ]

time: 451 us -> 452 us (level)
  no operation moved by 1% of the time
where the time goes in v10:
time: 452 us; the launch traced here: 449 us
  Pallas kernels  441 us (98%)
    pallas_call x5, Pallas kernels, call(): pl.pallas_call(kernel, out_shape=outs, in_specs=specs_in, out_specs=specs...  435 us

profile of v10, /device:TPU:9, one launch (start us, length us, event | category | flops | bytes accessed | tf_op | source)
XLA Modules:
  0.0 449.1 jit_solution(567698778218535756)
XLA Ops:
  0.6 1.2 select_maximum_fusion.gain_rows
  1.9 64.0 %shard_map.220 = (bf16[8,128,2176]{2,1,0:T(8,128)(2,1)}, bf16[4,8,64,896]{3,2,1,0:T(8,128)(2,1)}, bf16[8,64,1024]{2,1,0:T(8,128)(2,1)}, bf16[8,64,1024]{2,1,0:T(...) custom-call(bf16[128,2048]{1,0:T(8,128)(2,1)} %bitcast.23, ...), custom_call_target="tpu_custom_call" | custom-call | bytes 167772160 | tf_op jit(solution)/shard_map/pallas_call | solution.py:1385
  65.9 0.6 maximum_bitcast_fusion.inverse
  66.5 61.1 %shard_map.221 = (bf16[1024,2048]{1,0:T(8,128)(2,1)}, bf16[1024,768]{1,0:T(8,128)(2,1)}, bf16[1024,256]{1,0:T(8,128)(2,1)}, f32[1,256]{1,0:T(1,128)}, f32[8,2048...) custom-call(bf16[8,128,2176]{2,1,0:T(8,128)(2,1)} %get-tuple-element, ...), custom_call_target="tpu_custom_call" | custom-call | bytes 167772160 | tf_op jit(solution)/shard_map/pallas_call | solution.py:1385
  127.6 88.7 %shard_map.222 = (f32[128,2048]{1,0:T(8,128)}, bf16[8,128,2048]{2,1,0:T(8,128)(2,1)}, bf16[4,8,64,1024]{3,2,1,0:T(8,128)(2,1)}, bf16[1024,1024]{1,0:T(8,128)(2,1...) custom-call(bf16[1024,256]{1,0:T(8,128)(2,1)} %get-tuple-element.61.o, ...), custom_call_target="tpu_custom_call" | custom-call | bytes 167772160 | tf_op jit(solution)/shard_map/pallas_call | solution.py:1385
  216.3 115.1 %shard_map.223 = (f32[128,2048]{1,0:T(8,128)}, bf16[8,128,2048]{2,1,0:T(8,128)(2,1)}, f32[1,2048]{1,0:T(1,128)}, bf16[8,64,2048]{2,1,0:T(8,128)(2,1)}, bf16[128,2048]{1,0:T(8,128)(2,1)}) custom-call(bf16[1024,2048]{1,0:T(8,128)(2,1)} %bitcast.28, bf16[1024,2048]{1,0:T(8,128)(2,1)} %get-tuple-element.69.dgu_in, bf16[1024,1024]{1,0:T(8,128)(2,1)} %get-tuple-element.70.hid, ...), custom_call_target="tpu_custom_call" | custom-call | bytes 167772160 | tf_op jit(solution)/shard_map/pallas_call | solution.py:1385
  331.4 106.1 %shard_map.224 = (bf16[128,2048]{1,0:T(8,128)(2,1)}, f32[3,1,2048]{2,1,0:T(1,128)}, bf16[8,64,2048]{2,1,0:T(8,128)(2,1)}, bf16[256,2048]{1,0:T(8,128)(2,1)}, f32...) custom-call(bf16[8,64,2048]{2,1,0:T(8,128)(2,1)} %get-tuple-element.75.g_gu, ...), custom_call_target="tpu_custom_call" | custom-call | bytes 167772160 | tf_op jit(solution)/shard_map/pallas_call | solution.py:1385
  437.5 0.7 fusion
  438.2 0.6 dynamic-slice_bitcast_fusion
  438.8 0.0 copy-start
  438.8 0.0 copy-start.1
  438.8 5.8 %shard_map.225 = (f32[64,2048]{1,0:T(8,128)}, f32[64,2048]{1,0:T(8,128)}, f32[64,2048]{1,0:T(8,128)}, f32[64,2048]{1,0:T(8,128)}, f32[64,8192]{1,0:T(8,128)}, /*index=5*/f32[64,8192]{1,0:T(8,128)}, f32[256,2048]{1,0:T(8,128)}) custom-call(bf16[8,64,768]{2,1,0:T(8,128)(2,1)} %get-tuple-element.88.qkv_in, bf16[8,64,2048]{2,1,0:T(8,128)(2,1)} %get-tuple-element.89.gu_in, ...), custom_call_target="tpu_custom_call" | custom-call | tf_op jit(solution)/shard_map/pallas_call | solution.py:1604
  444.6 1.1 slice.11
  446.4 0.0 copy-done
  446.4 0.8 copy.27
  447.2 0.0 copy-done.1
  447.2 0.8 copy.28
  (1 shorter events, 0.0 us)
Async XLA Ops:
  438.8 7.6 %copy-start = (bf16[128,2048]{1,0:T(8,128)(2,1)S(1)}, bf16[128,2048]{1,0:T(8,128)(2,1)}, u32[]{:S(2)}) copy-start(bf16[128,2048]{1,0:T(8,128)(2,1)} %get-tuple-element.74) | copy-start | bytes 1572868
  438.8 8.4 %copy-start.1 = (bf16[128,2048]{1,0:T(8,128)(2,1)S(1)}, bf16[128,2048]{1,0:T(8,128)(2,1)}, u32[]{:S(2)}) copy-start(bf16[128,2048]{1,0:T(8,128)(2,1)} %get-tuple-element.87) | copy-start | bytes 1572868
